TPU v7x, 512 devices: a whole 4x4x16 slice. The times are simulated.
512 devices in a mesh: blk: 64 (over z, x_hi, core), sub: 8 (over y, x_lo).
Axes of the slice: x: 4 (x_hi: 2, x_lo: 2; x = x_hi * 2 + x_lo), y: 4, z: 16, core: 2. Of those that a mesh axis runs over, the one named last changes fastest.
Arguments:
- features: float32 [12, 256, 8192], P(None, 'sub', 'blk'), may hold values from -6 to 6
- inverse_diag: float32 [6, 6, 256, 8192], P(None, None, 'sub', 'blk'), may hold values from -0.12 to 1, as said below
- couplings: float32 [4, 256, 8192], P(None, 'sub', 'blk'), may hold values from 0.2 to 0.24
- mismatch: float32 [6, 256, 8192], P(None, 'sub', 'blk'), may hold values from -21 to 21
- production: float32 [6, 256, 8192], P(None, 'sub', 'blk'), may hold values from -6 to 6
- weight_in: float32 [128, 12], replicated, may hold values from -1.75 to 1.75
- bias_in: float32 [128], replicated, may hold values from -0.5 to 0.5
- weight_two: float32 [128, 128], replicated, may hold values from -0.5 to 0.5
- bias_two: float32 [128], replicated, may hold values from -0.5 to 0.5
- weight_three: float32 [128, 128], replicated, may hold values from -0.5 to 0.5
- bias_three: float32 [128], replicated, may hold values from -0.5 to 0.5
- weight_four: float32 [128, 128], replicated, may hold values from -0.5 to 0.5
- bias_four: float32 [128], replicated, may hold values from -0.5 to 0.5
- weight_out: float32 [128], replicated, may hold values from -0.5 to 0.5
Outputs:
- adjoint: float32 [6, 256, 8192], P(None, 'sub', 'blk')
- sensitivity: float32 [256, 8192], P('sub', 'blk')
- correction: float32 [256, 8192], P('sub', 'blk')
- grad_weight_in: float32 [128, 12], replicated
- grad_bias_in: float32 [128], replicated
- grad_weight_two: float32 [128, 128], replicated
- grad_bias_two: float32 [128], replicated
- grad_weight_three: float32 [128, 128], replicated
- grad_bias_three: float32 [128], replicated
- grad_weight_four: float32 [128, 128], replicated
- grad_bias_four: float32 [128], replicated
- grad_weight_out: float32 [128], replicated
Inputs may be any that keep to these rules, and one draw needn't show every extreme that they name: `inverse_diag`: a cell's 6 by 6 block with diagonal entries between 0.7 and 1.0 and off-diagonal entries of magnitude at most 0.12.
All inputs are finite; a program needn't handle non-finite values.
Results may differ from a plain program's by a relative error of at most 0.0003.
Values sent between devices are 32-bit elements; how exact they have to be, the bound alone decides.
No kernel may reach another device: no remote copies, remote signals or barrier semaphores. Data moves between devices by JAX's collectives and lax.ppermute only.
A program may use at most 64 MiB of HBM per device.

v0:
```python
import jax
import jax.numpy as jnp
from jax import lax
from jax.sharding import PartitionSpec as P

SWEEPS = 8


EPS = 1e-06
HIGH = lax.Precision.HIGHEST


def padded_2(value, sides, width, wrap):
    for axis, dim in sides:
        devices, length = (lax.axis_size(axis), value.shape[dim])
        up = [(i, (i + 1) % devices) for i in range(devices if wrap else devices - 1)]
        down = [(j, i) for i, j in up]
        last = lax.slice_in_dim(value, length - width, length, axis=dim)
        initial = lax.slice_in_dim(value, 0, width, axis=dim)
        before = lax.ppermute(last, axis, up)
        after = lax.ppermute(initial, axis, down)
        value = jnp.concatenate([before, value, after], axis=dim)
    return value


def sweep_padded(padded, inverse_diag, couplings, mismatch):
    upper_side = padded[:, :-2, 1:-1]
    lower_side = padded[:, 2:, 1:-1]
    pitch_low = padded[:, 1:-1, :-2]
    pitch_high = padded[:, 1:-1, 2:]
    rhs = mismatch + couplings[0] * upper_side + couplings[1] * lower_side
    rhs = rhs + couplings[2] * pitch_low + couplings[3] * pitch_high
    return jnp.sum(inverse_diag * rhs[None], axis=1)


def forward(inputs, weights):
    weight_in, bias_in, weight_two, bias_two, weight_three, bias_three, weight_four, bias_four = (
        weights
    )
    layer_one = jnp.tanh(
        jnp.einsum("ij,jc->ic", weight_in, inputs, precision=HIGH) + bias_in[:, None]
    )
    layer_two = jnp.tanh(
        jnp.einsum("ij,jc->ic", weight_two, layer_one, precision=HIGH) + bias_two[:, None]
    )
    layer_three = jnp.tanh(
        jnp.einsum("ij,jc->ic", weight_three, layer_two, precision=HIGH) + bias_three[:, None]
    )
    layer_four = jnp.tanh(
        jnp.einsum("ij,jc->ic", weight_four, layer_three, precision=HIGH) + bias_four[:, None]
    )
    return (layer_one, layer_two, layer_three, layer_four)


def top_terms(layer_four, layer_three, upstream, weight_out):
    grad_out = jnp.einsum("ic,c->i", layer_four, upstream, precision=HIGH)
    delta_four = weight_out[:, None] * upstream[None, :] * (1.0 - layer_four * layer_four)
    grad_four = jnp.einsum("ic,jc->ij", delta_four, layer_three, precision=HIGH)
    return (grad_out, grad_four, jnp.sum(delta_four, axis=1), delta_four)


def next_terms(delta_next, weight_next, layer_now, layer_prev):
    delta_now = jnp.einsum("ji,jc->ic", weight_next, delta_next, precision=HIGH) * (
        1.0 - layer_now * layer_now
    )
    grad_now = jnp.einsum("ic,jc->ij", delta_now, layer_prev, precision=HIGH)
    return (grad_now, jnp.sum(delta_now, axis=1), delta_now)


def local(
    features,
    inverse_diag,
    couplings,
    mismatch,
    production,
    weight_in,
    bias_in,
    weight_two,
    bias_two,
    weight_three,
    bias_three,
    weight_four,
    bias_four,
    weight_out,
):
    nvars, rows, cols = mismatch.shape
    adjoint = jnp.zeros((nvars, rows, cols), jnp.float32)
    for sweep_index in range(SWEEPS):
        widened = padded_2(adjoint, (("blk", 2),), 1, True)
        padded = padded_2(widened, (("sub", 1),), 1, False)
        adjoint = sweep_padded(padded, inverse_diag, couplings, mismatch)
    sensitivity = -jnp.sum(adjoint * production, axis=0)
    local_square = jnp.sum(sensitivity * sensitivity)
    inputs = features.reshape(features.shape[0], rows * cols)
    weights = (
        weight_in,
        bias_in,
        weight_two,
        bias_two,
        weight_three,
        bias_three,
        weight_four,
        bias_four,
    )
    layer_one, layer_two, layer_three, layer_four = forward(inputs, weights)
    correction = (1.0 + jnp.einsum("i,ic->c", weight_out, layer_four, precision=HIGH)).reshape(
        rows, cols
    )
    flat_sens = sensitivity.reshape(rows * cols)
    total_square = lax.psum(local_square, ("blk", "sub"))
    norm_value = jnp.sqrt(total_square + EPS)
    upstream = flat_sens / norm_value
    grad_out, grad_four, gb_four, delta_four = top_terms(
        layer_four, layer_three, upstream, weight_out
    )
    grad_out, grad_four, gb_four = lax.psum((grad_out, grad_four, gb_four), ("blk", "sub"))
    grad_three, gb_three, delta_three = next_terms(delta_four, weight_four, layer_three, layer_two)
    grad_three, gb_three = lax.psum((grad_three, gb_three), ("blk", "sub"))
    grad_two, gb_two, delta_two = next_terms(delta_three, weight_three, layer_two, layer_one)
    grad_two, gb_two = lax.psum((grad_two, gb_two), ("blk", "sub"))
    grad_one, gb_one, delta_one = next_terms(delta_two, weight_two, layer_one, inputs)
    grad_one, gb_one = lax.psum((grad_one, gb_one), ("blk", "sub"))
    results = (
        grad_one,
        gb_one,
        grad_two,
        gb_two,
        grad_three,
        gb_three,
        grad_four,
        gb_four,
        grad_out,
    )
    return (
        adjoint,
        sensitivity,
        correction,
        results[0],
        results[1],
        results[2],
        results[3],
        results[4],
        results[5],
        results[6],
        results[7],
        results[8],
    )


def solution(mesh):
    placed = (
        P(None, "sub", "blk"),
        P(None, None, "sub", "blk"),
        P(None, "sub", "blk"),
        P(None, "sub", "blk"),
        P(None, "sub", "blk"),
        P(),
        P(),
        P(),
        P(),
        P(),
        P(),
        P(),
        P(),
        P(),
    )
    return jax.shard_map(
        local,
        mesh=mesh,
        in_specs=placed,
        out_specs=(
            P(None, "sub", "blk"),
            P("sub", "blk"),
            P("sub", "blk"),
            P(),
            P(),
            P(),
            P(),
            P(),
            P(),
            P(),
            P(),
            P(),
        ),
        check_vma=False,
    )
```

profile of v0, /device:TPU:1, one launch (start us, length us, event | category | flops | bytes accessed | tf_op | source)
XLA Modules:
  0.0 789.4 jit_solution(17911993634000659095)
XLA Ops:
  7.3 8.9 %collective-permute-start.1 = (f32[6,32,1]{2,1,0:T(8,128)S(1)}, f32[6,32,1]{2,1,0:T(8,128)S(1)}, u32[]{:S(2)}, u32[]{:S(2)}) collective-permute-start(f32[6,32,1]{2,1,0:T(8,128)S(1)} %broadcast.37), channel_id=1, source_target_pairs={{8,0},{16,8},{24,16},{32,24},{40,32},{48,40},{56,48},{64,56},{72,6... | collective-permute-start | bytes 2312 | tf_op jit(solution)/shard_map/ppermute | solution.py:21
  18.1 6.8 collective-permute-done
  36.6 9.9 %collective-permute-start.5 = (f32[6,32,1]{2,1,0:T(8,128)S(1)}, f32[6,32,1]{2,1,0:T(8,128)S(1)}, u32[]{:S(2)}, u32[]{:S(2)}) collective-permute-start(f32[6,32,1]{2,1,0:T(8,128)S(1)} %get-tuple-element.52), channel_id=1, source_target_pairs={{8,0},{16,8},{24,16},{32,24},{40,32},{48,40},{56,48},{64,56},{72,6... | collective-permute-start | bytes 2312 | tf_op jit(solution)/shard_map/ppermute | solution.py:21
  47.5 4.5 collective-permute-start.6
  58.8 10.0 %collective-permute-start.9 = (f32[6,32,1]{2,1,0:T(8,128)S(1)}, f32[6,32,1]{2,1,0:T(8,128)S(1)}, u32[]{:S(2)}, u32[]{:S(2)}) collective-permute-start(f32[6,32,1]{2,1,0:T(8,128)S(1)} %get-tuple-element.50), channel_id=1, source_target_pairs={{8,0},{16,8},{24,16},{32,24},{40,32},{48,40},{56,48},{64,56},{72,6... | collective-permute-start | bytes 2312 | tf_op jit(solution)/shard_map/ppermute | solution.py:21
  73.7 3.3 collective-permute-done.11
  79.4 9.7 %collective-permute-start.13 = (f32[6,32,1]{2,1,0:T(8,128)S(1)}, f32[6,32,1]{2,1,0:T(8,128)S(1)}, u32[]{:S(2)}, u32[]{:S(2)}) collective-permute-start(f32[6,32,1]{2,1,0:T(8,128)S(1)} %get-tuple-element.48), channel_id=1, source_target_pairs={{8,0},{16,8},{24,16},{32,24},{40,32},{48,40},{56,48},{64,56},{72,6... | collective-permute-start | bytes 2312 | tf_op jit(solution)/shard_map/ppermute | solution.py:21
  90.1 4.5 collective-permute-start.14
  101.3 10.0 %collective-permute-start.17 = (f32[6,32,1]{2,1,0:T(8,128)S(1)}, f32[6,32,1]{2,1,0:T(8,128)S(1)}, u32[]{:S(2)}, u32[]{:S(2)}) collective-permute-start(f32[6,32,1]{2,1,0:T(8,128)S(1)} %get-tuple-element.46), channel_id=1, source_target_pairs={{8,0},{16,8},{24,16},{32,24},{40,32},{48,40},{56,48},{64,56},{72,6... | collective-permute-start | bytes 2312 | tf_op jit(solution)/shard_map/ppermute | solution.py:21
  116.3 3.2 collective-permute-done.19
  121.8 10.0 %collective-permute-start.21 = (f32[6,32,1]{2,1,0:T(8,128)S(1)}, f32[6,32,1]{2,1,0:T(8,128)S(1)}, u32[]{:S(2)}, u32[]{:S(2)}) collective-permute-start(f32[6,32,1]{2,1,0:T(8,128)S(1)} %get-tuple-element.44), channel_id=1, source_target_pairs={{8,0},{16,8},{24,16},{32,24},{40,32},{48,40},{56,48},{64,56},{72,6... | collective-permute-start | bytes 2312 | tf_op jit(solution)/shard_map/ppermute | solution.py:21
  132.8 4.2 collective-permute-start.22
  143.7 10.0 %collective-permute-start.25 = (f32[6,32,1]{2,1,0:T(8,128)S(1)}, f32[6,32,1]{2,1,0:T(8,128)S(1)}, u32[]{:S(2)}, u32[]{:S(2)}) collective-permute-start(f32[6,32,1]{2,1,0:T(8,128)S(1)} %get-tuple-element.42), channel_id=1, source_target_pairs={{8,0},{16,8},{24,16},{32,24},{40,32},{48,40},{56,48},{64,56},{72,6... | collective-permute-start | bytes 2312 | tf_op jit(solution)/shard_map/ppermute | solution.py:21
  164.2 10.0 %collective-permute-start.29 = (f32[6,32,1]{2,1,0:T(8,128)S(1)}, f32[6,32,1]{2,1,0:T(8,128)S(1)}, u32[]{:S(2)}, u32[]{:S(2)}) collective-permute-start(f32[6,32,1]{2,1,0:T(8,128)S(1)} %get-tuple-element.40), channel_id=1, source_target_pairs={{8,0},{16,8},{24,16},{32,24},{40,32},{48,40},{56,48},{64,56},{72,6... | collective-permute-start | bytes 2312 | tf_op jit(solution)/shard_map/ppermute | solution.py:21
  180.7 3.4 fusion.4
  185.5 3.2 fusion.3
  188.7 108.6 %psum.70 = f32[]{:T(128)} all-reduce(f32[]{:T(128)} %multiply_reduce_fusion.9), channel_id=1, replica_groups=mesh['blk'=64,'sub'=8] {'blk','sub'}, use_global_device_ids=true, to_apply=%region_10.0 | all-reduce | flops 1 | bytes 8 | tf_op jit(solution)/shard_map/psum | solution.py:110
  298.6 4.0 fusion.6
  307.4 3.6 fusion.91
  311.0 4.4 fusion.94
  318.6 4.2 fusion.93
  322.8 4.5 fusion.89
  331.4 99.6 %all-reduce.2 = (f32[128,12]{0,1:T(8,128)}, f32[128]{0:T(128)}, f32[128]{0:T(128)}, f32[128]{0:T(128)}, f32[128]{0:T(128)}, /*index=5*/f32[128]{0:T(128)}) all-reduce(f32[128,12]{0,1:T(8,128)S(1)} %fusion.92, f32[128]{0:T(128)S(1)} %get-tuple-element.57, ...), channel_id=1, replica_groups=mesh['blk'=64,'sub'=8] {'blk','sub'}, use_global_device_ids=true, to_apply=%region_11.0 | all-reduce | flops 2176 | bytes 17408 | tf_op jit(solution)/shard_map/psum | solution.py:122
  431.1 346.9 %all-reduce.6.cloned.1.call-done = (f32[128,128]{1,0:T(8,128)}, f32[128,128]{1,0:T(8,128)}, f32[128,128]{1,0:T(8,128)}) async-done(((f32[128,128]{1,0:T(8,128)}, f32[128,128]{1,0:T(8,128)}, f32[128,128]{1,0:T(8,128)}), (f32[128,128]{1,0:T(8,128)}, f32[128,128]{1,0:T(8,128)}, f32[128,128]{1,0:T(8,128)})) %all-reduce.6.cloned.1.call-update) | async-done | bytes 196624 | tf_op jit(solution)/shard_map/psum | solution.py:120
  (141 shorter events, 86.3 us)
Async XLA Ops:
  7.2 770.7 %all-reduce.6.cloned.1.call-start = ((), (), s32[]{:S(2)}) async-start(), calls=%async_computation | async-start | bytes 393216 | tf_op jit(solution)/shard_map/psum | solution.py:120
  7.3 10.9 %collective-permute-start.1 = (f32[6,32,1]{2,1,0:T(8,128)S(1)}, f32[6,32,1]{2,1,0:T(8,128)S(1)}, u32[]{:S(2)}, u32[]{:S(2)}) collective-permute-start(f32[6,32,1]{2,1,0:T(8,128)S(1)} %broadcast.37), channel_id=1, source_target_pairs={{8,0},{16,8},{24,16},{32,24},{40,32},{48,40},{56,48},{64,56},{72,6... | collective-permute-start | bytes 2312 | tf_op jit(solution)/shard_map/ppermute | solution.py:21
  16.2 8.7 %collective-permute-start = (f32[6,32,1]{2,1,0:T(8,128)S(1)}, f32[6,32,1]{2,1,0:T(8,128)S(1)}, u32[]{:S(2)}, u32[]{:S(2)}) collective-permute-start(f32[6,32,1]{2,1,0:T(8,128)S(1)} %broadcast.37), channel_id=1, source_target_pairs={{0,8},{8,16},{16,24},{24,32},{32,40},{40,48},{48,56},{56,64},{64,7... | collective-permute-start | bytes 2312 | tf_op jit(solution)/shard_map/ppermute | solution.py:20
  27.3 5.1 collective-permute-start.3
  34.7 11.8 %collective-permute-start.4 = (f32[6,32,1]{2,1,0:T(8,128)S(1)}, f32[6,32,1]{2,1,0:T(8,128)S(1)}, u32[]{:S(2)}, u32[]{:S(2)}) collective-permute-start(f32[6,32,1]{2,1,0:T(8,128)S(1)} %get-tuple-element.51), channel_id=1, source_target_pairs={{0,8},{8,16},{16,24},{24,32},{32,40},{40,48},{48,56},{56,64},{64,7... | collective-permute-start | bytes 2312 | tf_op jit(solution)/shard_map/ppermute | solution.py:20
  36.6 10.8 %collective-permute-start.5 = (f32[6,32,1]{2,1,0:T(8,128)S(1)}, f32[6,32,1]{2,1,0:T(8,128)S(1)}, u32[]{:S(2)}, u32[]{:S(2)}) collective-permute-start(f32[6,32,1]{2,1,0:T(8,128)S(1)} %get-tuple-element.52), channel_id=1, source_target_pairs={{8,0},{16,8},{24,16},{32,24},{40,32},{48,40},{56,48},{64,56},{72,6... | collective-permute-start | bytes 2312 | tf_op jit(solution)/shard_map/ppermute | solution.py:21
  47.5 5.8 collective-permute-start.6
  56.8 11.9 %collective-permute-start.8 = (f32[6,32,1]{2,1,0:T(8,128)S(1)}, f32[6,32,1]{2,1,0:T(8,128)S(1)}, u32[]{:S(2)}, u32[]{:S(2)}) collective-permute-start(f32[6,32,1]{2,1,0:T(8,128)S(1)} %get-tuple-element.49), channel_id=1, source_target_pairs={{0,8},{8,16},{16,24},{24,32},{32,40},{40,48},{48,56},{56,64},{64,7... | collective-permute-start | bytes 2312 | tf_op jit(solution)/shard_map/ppermute | solution.py:20
  58.8 10.9 %collective-permute-start.9 = (f32[6,32,1]{2,1,0:T(8,128)S(1)}, f32[6,32,1]{2,1,0:T(8,128)S(1)}, u32[]{:S(2)}, u32[]{:S(2)}) collective-permute-start(f32[6,32,1]{2,1,0:T(8,128)S(1)} %get-tuple-element.50), channel_id=1, source_target_pairs={{8,0},{16,8},{24,16},{32,24},{40,32},{48,40},{56,48},{64,56},{72,6... | collective-permute-start | bytes 2312 | tf_op jit(solution)/shard_map/ppermute | solution.py:21
  72.4 4.7 collective-permute-start.11
  77.4 11.6 %collective-permute-start.12 = (f32[6,32,1]{2,1,0:T(8,128)S(1)}, f32[6,32,1]{2,1,0:T(8,128)S(1)}, u32[]{:S(2)}, u32[]{:S(2)}) collective-permute-start(f32[6,32,1]{2,1,0:T(8,128)S(1)} %get-tuple-element.47), channel_id=1, source_target_pairs={{0,8},{8,16},{16,24},{24,32},{32,40},{40,48},{48,56},{56,64},{64,7... | collective-permute-start | bytes 2312 | tf_op jit(solution)/shard_map/ppermute | solution.py:20
  79.4 10.6 %collective-permute-start.13 = (f32[6,32,1]{2,1,0:T(8,128)S(1)}, f32[6,32,1]{2,1,0:T(8,128)S(1)}, u32[]{:S(2)}, u32[]{:S(2)}) collective-permute-start(f32[6,32,1]{2,1,0:T(8,128)S(1)} %get-tuple-element.48), channel_id=1, source_target_pairs={{8,0},{16,8},{24,16},{32,24},{40,32},{48,40},{56,48},{64,56},{72,6... | collective-permute-start | bytes 2312 | tf_op jit(solution)/shard_map/ppermute | solution.py:21
  90.1 5.8 collective-permute-start.14
  99.4 11.9 %collective-permute-start.16 = (f32[6,32,1]{2,1,0:T(8,128)S(1)}, f32[6,32,1]{2,1,0:T(8,128)S(1)}, u32[]{:S(2)}, u32[]{:S(2)}) collective-permute-start(f32[6,32,1]{2,1,0:T(8,128)S(1)} %get-tuple-element.45), channel_id=1, source_target_pairs={{0,8},{8,16},{16,24},{24,32},{32,40},{40,48},{48,56},{56,64},{64,7... | collective-permute-start | bytes 2312 | tf_op jit(solution)/shard_map/ppermute | solution.py:20
  101.3 10.9 %collective-permute-start.17 = (f32[6,32,1]{2,1,0:T(8,128)S(1)}, f32[6,32,1]{2,1,0:T(8,128)S(1)}, u32[]{:S(2)}, u32[]{:S(2)}) collective-permute-start(f32[6,32,1]{2,1,0:T(8,128)S(1)} %get-tuple-element.46), channel_id=1, source_target_pairs={{8,0},{16,8},{24,16},{32,24},{40,32},{48,40},{56,48},{64,56},{72,6... | collective-permute-start | bytes 2312 | tf_op jit(solution)/shard_map/ppermute | solution.py:21
  119.8 11.9 %collective-permute-start.20 = (f32[6,32,1]{2,1,0:T(8,128)S(1)}, f32[6,32,1]{2,1,0:T(8,128)S(1)}, u32[]{:S(2)}, u32[]{:S(2)}) collective-permute-start(f32[6,32,1]{2,1,0:T(8,128)S(1)} %get-tuple-element.43), channel_id=1, source_target_pairs={{0,8},{8,16},{16,24},{24,32},{32,40},{40,48},{48,56},{56,64},{64,7... | collective-permute-start | bytes 2312 | tf_op jit(solution)/shard_map/ppermute | solution.py:20
  121.8 10.9 %collective-permute-start.21 = (f32[6,32,1]{2,1,0:T(8,128)S(1)}, f32[6,32,1]{2,1,0:T(8,128)S(1)}, u32[]{:S(2)}, u32[]{:S(2)}) collective-permute-start(f32[6,32,1]{2,1,0:T(8,128)S(1)} %get-tuple-element.44), channel_id=1, source_target_pairs={{8,0},{16,8},{24,16},{32,24},{40,32},{48,40},{56,48},{64,56},{72,6... | collective-permute-start | bytes 2312 | tf_op jit(solution)/shard_map/ppermute | solution.py:21
  132.8 5.5 collective-permute-start.22
  141.8 11.9 %collective-permute-start.24 = (f32[6,32,1]{2,1,0:T(8,128)S(1)}, f32[6,32,1]{2,1,0:T(8,128)S(1)}, u32[]{:S(2)}, u32[]{:S(2)}) collective-permute-start(f32[6,32,1]{2,1,0:T(8,128)S(1)} %get-tuple-element.41), channel_id=1, source_target_pairs={{0,8},{8,16},{16,24},{24,32},{32,40},{40,48},{48,56},{56,64},{64,7... | collective-permute-start | bytes 2312 | tf_op jit(solution)/shard_map/ppermute | solution.py:20
  143.7 10.9 %collective-permute-start.25 = (f32[6,32,1]{2,1,0:T(8,128)S(1)}, f32[6,32,1]{2,1,0:T(8,128)S(1)}, u32[]{:S(2)}, u32[]{:S(2)}) collective-permute-start(f32[6,32,1]{2,1,0:T(8,128)S(1)} %get-tuple-element.42), channel_id=1, source_target_pairs={{8,0},{16,8},{24,16},{32,24},{40,32},{48,40},{56,48},{64,56},{72,6... | collective-permute-start | bytes 2312 | tf_op jit(solution)/shard_map/ppermute | solution.py:21
  162.3 13.8 %collective-permute-start.28 = (f32[6,32,1]{2,1,0:T(8,128)S(1)}, f32[6,32,1]{2,1,0:T(8,128)S(1)}, u32[]{:S(2)}, u32[]{:S(2)}) collective-permute-start(f32[6,32,1]{2,1,0:T(8,128)S(1)} %get-tuple-element.39), channel_id=1, source_target_pairs={{0,8},{8,16},{16,24},{24,32},{32,40},{40,48},{48,56},{56,64},{64,7... | collective-permute-start | bytes 2312 | tf_op jit(solution)/shard_map/ppermute | solution.py:20
  164.2 11.9 %collective-permute-start.29 = (f32[6,32,1]{2,1,0:T(8,128)S(1)}, f32[6,32,1]{2,1,0:T(8,128)S(1)}, u32[]{:S(2)}, u32[]{:S(2)}) collective-permute-start(f32[6,32,1]{2,1,0:T(8,128)S(1)} %get-tuple-element.40), channel_id=1, source_target_pairs={{8,0},{16,8},{24,16},{32,24},{40,32},{48,40},{56,48},{64,56},{72,6... | collective-permute-start | bytes 2312 | tf_op jit(solution)/shard_map/ppermute | solution.py:21
  176.2 8.0 %collective-permute-start.30 = (f32[6,1,130]{2,1,0:T(1,128)S(1)}, f32[6,1,130]{2,1,0:T(1,128)S(1)}, u32[]{:S(2)}, u32[]{:S(2)}) collective-permute-start(f32[6,1,130]{2,1,0:T(1,128)S(1)} %get-tuple-element.23), channel_id=1, source_target_pairs={{0,1},{1,2},{2,3},{3,4},{4,5},{5,6},{6,7},{8,9},{9,10},{10,11},{11... | collective-permute-start | bytes 9368 | tf_op jit(solution)/shard_map/ppermute | solution.py:20
  178.8 5.4 collective-permute-start.31
  (29 other events, 852.5 us)
Sparse Core Ops, SparseCore 0:
  329.8 448.0 all-reduce.5
where the time goes:
time: 796 us; the launch traced here: 789 us
  waiting for transfers between devices  381 us (48%)
  blocking collectives  208 us (26%)
  starting transfers between devices  131 us (16%)
  matrix products  38.9 us (5%)
  between operations  15.8 us (2%)
    psum x1, waiting for transfers between devices, local(): grad_two, gb_two = lax.psum((grad_two, gb_two), ('blk', 'sub'))  347 us
    psum x1, blocking collectives, local(): total_square = lax.psum(local_square, ('blk', 'sub'))  109 us
    psum x1, blocking collectives, local(): grad_one, gb_one = lax.psum((grad_one, gb_one), ('blk', 'sub'))  99.6 us
    ppermute x16, starting transfers between devices, padded_2(): after = lax.ppermute(initial, axis, down)  89.2 us
    ppermute x16, starting transfers between devices, padded_2(): before = lax.ppermute(last, axis, up)  41.6 us
    ppermute x16, waiting for transfers between devices, padded_2(): after = lax.ppermute(initial, axis, down)  27 us
  transfers between devices with their start and end apart: 33, of which 15 were waited for; matrix products, arithmetic and copies ran while one was open for 1% of the time, Pallas kernels for 0%

commit v1 on v0

v1 whole, which is shorter than its diff:
```python
import jax
import jax.numpy as jnp
from jax import lax
from jax.experimental import pallas as pl
from jax.experimental.pallas import tpu as pltpu
from jax.sharding import Mesh, PartitionSpec as P

SWEEPS = 8
EPS = 1e-06
BLK = ("z", "xh", "c")
SUB = ("y", "xl")
NEAR = ("xh", "c", "y", "xl")
FAR = ("z",)
F32 = jnp.float32
BF16 = jnp.bfloat16
GROUP = 4
MIB = 1 << 20


def split(value):
    high = value.astype(BF16)
    return high, (value - high.astype(F32)).astype(BF16)


def pair(value):
    return jnp.concatenate(split(value), axis=1)


def joined(both):
    return both[:, :128].astype(F32) + both[:, 128:].astype(F32)


def times(both, weights):
    out = jnp.dot(both, weights, preferred_element_type=F32)
    return out[:, :128] + out[:, 128:]


def stacked(weight):
    both = pair(weight)
    return jnp.concatenate([both, both], axis=0)


def forward_kernel(x_ref, win_ref, w2_ref, w3_ref, w4_ref, vec_ref,
                   xc_ref, l1_ref, l2_ref, l3_ref, l4_ref, s1, s2, s3, s4):
    @pl.when(pl.program_id(0) == 0)
    def _():
        high, low = split(win_ref[...])
        s1[...] = jnp.concatenate([high, high, low], axis=0)
        for raw, kept in ((w2_ref, s2), (w3_ref, s3), (w4_ref, s4)):
            kept[...] = stacked(raw[...].T)

    columns = []
    for r in range(GROUP):
        x = x_ref[r]
        high = x.astype(BF16).astype(F32)
        column = jnp.concatenate([high, x - high, high], axis=0).T.astype(BF16)
        xc_ref[r] = column
        columns.append(column)
    inputs = jnp.concatenate(columns, axis=0)
    layer = jnp.tanh(jnp.dot(inputs, s1[...], preferred_element_type=F32) + vec_ref[0:1])
    for k, (out, weights) in enumerate(((l1_ref, s2), (l2_ref, s3), (l3_ref, s4))):
        both = pair(layer)
        out[...] = both.reshape(GROUP, 128, 256)
        layer = jnp.tanh(times(both, weights[...]) + vec_ref[k + 1 : k + 2])
    l4_ref[...] = layer.reshape(GROUP, 128, 128)


def forward_call(x, win, w2, w3, w4, vec, rows):
    whole = lambda shape: pl.BlockSpec(shape, lambda i: (0, 0))
    block = lambda a, b: pl.BlockSpec((GROUP, a, b), lambda i: (i, 0, 0))
    return pl.pallas_call(
        forward_kernel,
        grid=(rows // GROUP,),
        in_specs=[block(16, 128), whole((16, 128))] + [whole((128, 128))] * 3 + [whole((8, 128))],
        out_specs=[block(128, 48)] + [block(128, 256)] * 3 + [block(128, 128)],
        out_shape=[jax.ShapeDtypeStruct((rows, 128, 48), BF16)]
        + [jax.ShapeDtypeStruct((rows, 128, 256), BF16)] * 3
        + [jax.ShapeDtypeStruct((rows, 128, 128), F32)],
        scratch_shapes=[pltpu.VMEM((48, 128), BF16)] + [pltpu.VMEM((256, 256), BF16)] * 3,
        compiler_params=pltpu.CompilerParams(vmem_limit_bytes=24 * MIB),
        cost_estimate=pl.CostEstimate(flops=8 * 10**9, bytes_accessed=9 * 10**6, transcendentals=2 * 10**6),
        name="forward",
    )(x, win, w2, w3, w4, vec)


def backward_kernel(l1_ref, l2_ref, l3_ref, l4_ref, w2_ref, w3_ref, w4_ref, vec_ref,
                    corr_ref, l4t_ref, d3t_ref, d2t_ref, d1t_ref, s2, s3, s4, wt):
    @pl.when(pl.program_id(0) == 0)
    def _():
        for raw, kept in ((w2_ref, s2), (w3_ref, s3), (w4_ref, s4)):
            kept[...] = stacked(raw[...])
        wt[...] = jnp.broadcast_to(vec_ref[4:5], (128, 128)).T

    layer = l4_ref[...].reshape(GROUP * 128, 128)
    for r in range(GROUP):
        turned = l4_ref[r].T
        l4t_ref[r] = turned
        corr_ref[r] = 1.0 + jnp.sum(turned * wt[...], axis=0, keepdims=True)
    delta = vec_ref[4:5] * (1.0 - layer * layer)
    for below, weights, out in ((l3_ref, s4, d3t_ref), (l2_ref, s3, d2t_ref), (l1_ref, s2, d1t_ref)):
        layer = joined(below[...].reshape(GROUP * 128, 256))
        delta = times(pair(delta), weights[...]) * (1.0 - layer * layer)
        for r in range(GROUP):
            out[r] = delta[r * 128 : (r + 1) * 128].T


def backward_call(l1, l2, l3, l4, w2, w3, w4, vec, rows):
    whole = lambda shape: pl.BlockSpec(shape, lambda i: (0, 0))
    block = lambda a, b: pl.BlockSpec((GROUP, a, b), lambda i: (i, 0, 0))
    return pl.pallas_call(
        backward_kernel,
        grid=(rows // GROUP,),
        in_specs=[block(128, 256)] * 3 + [block(128, 128)] + [whole((128, 128))] * 3 + [whole((8, 128))],
        out_specs=[block(1, 128)] + [block(128, 128)] * 4,
        out_shape=[jax.ShapeDtypeStruct((rows, 1, 128), F32)]
        + [jax.ShapeDtypeStruct((rows, 128, 128), F32)] * 4,
        scratch_shapes=[pltpu.VMEM((256, 256), BF16)] * 3 + [pltpu.VMEM((128, 128), F32)],
        compiler_params=pltpu.CompilerParams(vmem_limit_bytes=24 * MIB),
        cost_estimate=pl.CostEstimate(flops=8 * 10**9, bytes_accessed=17 * 10**6, transcendentals=0),
        name="backward",
    )(l1, l2, l3, l4, w2, w3, w4, vec)


def pack_kernel(up_ref, inv_ref, cpl_ref, mis_ref, down_ref, right_ref, left_ref):
    rows = mis_ref.shape[1]
    tiles = rows // 8 + 2
    lane = lax.broadcasted_iota(jnp.int32, (8, 128), 1)

    def tile(a, t):
        if t == 0:
            return up_ref[a]
        if t == tiles - 1:
            return down_ref[a]
        at = pl.ds(8 * (t - 1), 8)
        if a < 36:
            return inv_ref[a, at]
        return cpl_ref[a - 36, at] if a < 40 else mis_ref[a - 40, at]

    for t in range(tiles):
        for j in range(3):
            right = jnp.zeros((8, 128), F32)
            left = jnp.zeros((8, 128), F32)
            for k in range(min(16, 46 - 16 * j)):
                value = tile(16 * j + k, t)
                here = (lane >= 8 * k) & (lane < 8 * k + 8)
                right = jnp.where(here, pltpu.roll(value, (8 * k + 8) % 128, 1), right)
                left = jnp.where(here, pltpu.roll(value, 8 * k, 1) if k else value, left)
            right_ref[j, pl.ds(8 * t, 8)] = right
            left_ref[j, pl.ds(8 * t, 8)] = left


def pack_call(up, inv, cpl, mis, down):
    rows = mis.shape[1]
    return pl.pallas_call(
        pack_kernel,
        out_shape=[jax.ShapeDtypeStruct((3, rows + 16, 128), F32)] * 2,
        name="pack",
    )(up, inv, cpl, mis, down)


def final_kernel(up_ref, inv_ref, cpl_ref, mis_ref, down_ref, prod_ref, froml_ref, fromr_ref,
                 xc_hbm, l1_hbm, l2_hbm, l3_hbm, l4t_hbm, d3t_hbm, d2t_hbm, d1t_hbm, vec_ref,
                 adj_ref, sens_ref, sums_ref,
                 ext, main, side, wt, acc4, acc3, acc2, acc1, flat,
                 xc, l1, l2, l3, l4t, d3t, d2t, d1t, sem):
    moves = [
        pltpu.make_async_copy(source, target, sem.at[i])
        for i, (source, target) in enumerate(
            ((l4t_hbm, l4t), (l3_hbm, l3), (d3t_hbm, d3t), (l2_hbm, l2),
             (d2t_hbm, d2t), (l1_hbm, l1), (d1t_hbm, d1t), (xc_hbm, xc)))
    ]
    for move in moves:
        move.start()

    rows = mis_ref.shape[1]
    tiles = rows // 8 + 2
    lane = lax.broadcasted_iota(jnp.int32, (8, 128), 1)
    first, last = lane == 0, lane == 127

    def tile(a, t):
        if t == 0:
            return up_ref[a]
        if t == tiles - 1:
            return down_ref[a]
        at = pl.ds(8 * (t - 1), 8)
        if a < 36:
            return inv_ref[a, at]
        return cpl_ref[a - 36, at] if a < 40 else mis_ref[a - 40, at]

    for a in range(46):
        j, k = a // 16, a % 16
        for t in range(tiles):
            at = pl.ds(8 * t, 8)
            high = fromr_ref[j, at]
            low = froml_ref[j, at]
            high = pltpu.roll(high, (128 - 8 * k) % 128, 1) if k else high
            low = pltpu.roll(low, 120 - 8 * k, 1) if k != 15 else low
            ext[a, at] = jnp.where(lane < 8, high, jnp.where(lane >= 120, low, 0.0))

    edge = jnp.zeros((8, 128), F32)
    for field in (main, side):
        for s in range(2):
            for i in range(6):
                field[s, i, 0:8] = edge
                field[s, i, pl.ds(8 * tiles + 8, 8)] = edge

    def solve(field, s, t, coefficient, rhs):
        for i in range(6):
            total = coefficient(6 * i) * rhs[0]
            for j in range(1, 6):
                total = total + coefficient(6 * i + j) * rhs[j]
            field[s, i, pl.ds(8 * t + 8, 8)] = total

    for t in range(tiles):
        at = pl.ds(8 * t, 8)
        solve(main, 0, t, lambda a: tile(a, t), [tile(40 + i, t) for i in range(6)])
        solve(side, 0, t, lambda a: ext[a, at], [ext[40 + i, at] for i in range(6)])

    def sweep(n, carry):
        s = lax.rem(n, 2)
        for t in range(tiles):
            at = pl.ds(8 * t, 8)
            near, beside = [], []
            for i in range(6):
                m = main[s, i, pl.ds(8 * t + 8, 8)]
                e = side[s, i, pl.ds(8 * t + 8, 8)]
                m_low, m_high = pltpu.roll(m, 1, 1), pltpu.roll(m, 127, 1)
                e_low, e_high = pltpu.roll(e, 1, 1), pltpu.roll(e, 127, 1)
                rhs = tile(40 + i, t) + tile(36, t) * main[s, i, pl.ds(8 * t + 7, 8)]
                rhs = rhs + tile(37, t) * main[s, i, pl.ds(8 * t + 9, 8)]
                rhs = rhs + tile(38, t) * jnp.where(first, e_low, m_low)
                near.append(rhs + tile(39, t) * jnp.where(last, e_high, m_high))
                rhs = ext[40 + i, at] + ext[36, at] * side[s, i, pl.ds(8 * t + 7, 8)]
                rhs = rhs + ext[37, at] * side[s, i, pl.ds(8 * t + 9, 8)]
                rhs = rhs + ext[38, at] * jnp.where(first, m_low, e_low)
                beside.append(rhs + ext[39, at] * jnp.where(last, m_high, e_high))
            solve(main, 1 - s, t, lambda a: tile(a, t), near)
            solve(side, 1 - s, t, lambda a: ext[a, at], beside)
        return carry

    lax.fori_loop(0, SWEEPS - 1, sweep, 0)
    done = (SWEEPS - 1) % 2

    square = jnp.zeros((8, 128), F32)
    for t in range(rows // 8):
        at = pl.ds(8 * t, 8)
        total = jnp.zeros((8, 128), F32)
        for i in range(6):
            value = main[done, i, pl.ds(8 * t + 16, 8)]
            adj_ref[i, at] = value
            total = total + value * prod_ref[i, at]
        sens_ref[at] = -total
        square = square + total * total

    wt[...] = jnp.broadcast_to(vec_ref[4:5], (128, 128)).T
    for acc in (acc4, acc3, acc2, acc1):
        acc[...] = jnp.zeros_like(acc)
    flat[...] = jnp.zeros_like(flat)

    def term(scaled, layer, acc, slot, g):
        total = flat[slot]
        pieces = []
        for value in scaled:
            total = total + value
            high, low = split(value)
            pieces.append(jnp.concatenate([high, low], axis=0))
        flat[slot] = total
        left = jnp.concatenate(pieces, axis=1)
        right = layer[pl.ds(2 * g, 2)].reshape(256, layer.shape[2])
        acc[...] += jnp.dot(left, right, preferred_element_type=F32)

    def both(g):
        return [sens_ref[pl.ds(2 * g + r, 1), :] for r in range(2)]

    for move in moves[:2]:
        move.wait()

    def top(g, carry):
        weights = both(g)
        out = flat[4]
        scaled = []
        for r in range(2):
            value = l4t[2 * g + r]
            out = out + value * weights[r]
            scaled.append(wt[...] * (1.0 - value * value) * weights[r])
        flat[4] = out
        term(scaled, l3, acc4, 3, g)
        return carry

    lax.fori_loop(0, rows // 2, top, 0)

    for n, (delta, layer, acc, slot) in enumerate(((d3t, l2, acc3, 2), (d2t, l1, acc2, 1), (d1t, xc, acc1, 0))):
        for move in moves[2 + 2 * n : 4 + 2 * n]:
            move.wait()

        def lower(g, carry):
            weights = both(g)
            term([delta[2 * g + r] * weights[r] for r in range(2)], layer, acc, slot, g)
            return carry

        lax.fori_loop(0, rows // 2, lower, 0)

    for n, acc in enumerate((acc4, acc3, acc2)):
        sums_ref[pl.ds(128 * n, 128)] = (acc[0:128, 0:128] + acc[128:256, 0:128]) + (
            acc[0:128, 128:256] + acc[128:256, 128:256])
    lanes = lax.broadcasted_iota(jnp.int32, (128, 128), 1)
    block = jnp.zeros((128, 128), F32)
    for slot in range(5):
        block = jnp.where(lanes == 16 + slot, jnp.sum(flat[slot], axis=1, keepdims=True), block)
    block = jnp.where(lanes == 21, jnp.sum(square), block)
    own = acc1[0:128] + acc1[128:256]
    own = jnp.concatenate([own, jnp.zeros((128, 80), F32)], axis=1)
    own = own + pltpu.roll(own, 112, 1)
    sums_ref[pl.ds(384, 128)] = jnp.where(lanes < 12, own, block)


def final_call(up, inv, cpl, mis, down, prod, froml, fromr, xc, l1, l2, l3, l4t, d3t, d2t, d1t, vec):
    rows = mis.shape[1]
    vmem = pl.BlockSpec(memory_space=pltpu.VMEM)
    hbm = pl.BlockSpec(memory_space=pl.ANY)
    big = [l1, l2, l3, l4t, d3t, d2t, d1t]
    return pl.pallas_call(
        final_kernel,
        in_specs=[vmem] * 8 + [hbm] * 8 + [vmem],
        out_specs=[vmem] * 3,
        out_shape=[
            jax.ShapeDtypeStruct((6, rows, 128), F32),
            jax.ShapeDtypeStruct((rows, 128), F32),
            jax.ShapeDtypeStruct((512, 128), F32),
        ],
        scratch_shapes=[
            pltpu.VMEM((46, rows + 16, 128), F32),
            pltpu.VMEM((2, 6, rows + 32, 128), F32),
            pltpu.VMEM((2, 6, rows + 32, 128), F32),
            pltpu.VMEM((128, 128), F32),
            pltpu.VMEM((256, 256), F32),
            pltpu.VMEM((256, 256), F32),
            pltpu.VMEM((256, 256), F32),
            pltpu.VMEM((256, 48), F32),
            pltpu.VMEM((5, 128, 128), F32),
            pltpu.VMEM(xc.shape, BF16),
        ]
        + [pltpu.VMEM(value.shape, value.dtype) for value in big]
        + [pltpu.SemaphoreType.DMA((8,))],
        compiler_params=pltpu.CompilerParams(vmem_limit_bytes=40 * MIB),
        name="final",
    )(up, inv, cpl, mis, down, prod, froml, fromr, xc, *big, vec)


def unpack_kernel(sums_ref, w4_ref, w3_ref, w2_ref, win_ref, b1_ref, b2_ref, b3_ref, b4_ref, out_ref):
    block = sums_ref[pl.ds(384, 128)]
    scale = 1.0 / jnp.sqrt(jnp.broadcast_to(block[0:1, 21:22], (1, 128)) + EPS)
    for n, ref in enumerate((w4_ref, w3_ref, w2_ref)):
        ref[...] = sums_ref[pl.ds(128 * n, 128)] * scale
    block = block * scale
    win_ref[...] = block[:, 0:12]
    turned = block.T
    for n, ref in enumerate((b1_ref, b2_ref, b3_ref, b4_ref, out_ref)):
        ref[...] = turned[16 + n : 17 + n]


def unpack_call(sums):
    shapes = [(128, 128)] * 3 + [(128, 12)] + [(1, 128)] * 5
    return pl.pallas_call(
        unpack_kernel,
        out_shape=[jax.ShapeDtypeStruct(shape, F32) for shape in shapes],
        name="unpack",
    )(sums)


def shifted(last, initial, axes, wrap):
    size = lax.axis_size(axes)
    up = [(i, (i + 1) % size) for i in range(size if wrap else size - 1)]
    down = [(j, i) for i, j in up]
    return lax.ppermute(last, axes, up), lax.ppermute(initial, axes, down)


def summed(value):
    near, far = lax.axis_size(NEAR), lax.axis_size(FAR)
    rows = value.shape[0] // near
    part = lax.all_to_all(value.reshape(near, rows, 128), NEAR, 0, 0)
    part = jnp.sum(part, axis=0)
    part = lax.all_to_all(jnp.broadcast_to(part[None], (far, rows, 128)), FAR, 0, 0)
    part = jnp.sum(part, axis=0)
    whole = lax.all_to_all(jnp.broadcast_to(part[None], (near, rows, 128)), NEAR, 0, 0)
    return whole.reshape(near * rows, 128)


def local(features, inverse_diag, couplings, mismatch, production, weight_in, bias_in, weight_two,
          bias_two, weight_three, bias_three, weight_four, bias_four, weight_out):
    nvars, rows, cols = mismatch.shape
    inverse = inverse_diag.reshape(nvars * nvars, rows, cols)
    fields = (inverse, couplings, mismatch)
    last = jnp.concatenate([field[:, rows - 8 :] for field in fields], axis=0)
    initial = jnp.concatenate([field[:, :8] for field in fields], axis=0)
    above, below = shifted(last, initial, SUB, False)

    x = jnp.pad(jnp.transpose(features, (1, 0, 2)), ((0, 0), (0, 4), (0, 0)))
    win = jnp.pad(weight_in.T, ((0, 4), (0, 0)))
    vec = jnp.stack([bias_in, bias_two, bias_three, bias_four] + [weight_out] * 4)
    xc, l1, l2, l3, l4 = forward_call(x, win, weight_two, weight_three, weight_four, vec, rows)

    right, left = pack_call(above, inverse, couplings, mismatch, below)
    from_low, from_high = shifted(right, left, BLK, True)
    correction, l4t, d3t, d2t, d1t = backward_call(
        l1, l2, l3, l4, weight_two, weight_three, weight_four, vec, rows)

    adjoint, sensitivity, sums = final_call(
        above, inverse, couplings, mismatch, below, production, from_low, from_high,
        xc, l1, l2, l3, l4t, d3t, d2t, d1t, vec)
    g4, g3, g2, gin, b1, b2, b3, b4, gout = unpack_call(summed(sums))
    flat = lambda value: value.reshape(128)
    return (adjoint, sensitivity, correction.reshape(rows, cols), gin, flat(b1), g2, flat(b2),
            g3, flat(b3), g4, flat(b4), flat(gout))


def solution(mesh):
    sizes = (16, 2, 2, 4, 2) if mesh.devices.size == 512 else (mesh.shape["blk"], 1, 1, mesh.shape["sub"], 1)
    fine = Mesh(mesh.devices.reshape(sizes), BLK + SUB)
    three = P(None, SUB, BLK)
    two = P(SUB, BLK)
    return jax.shard_map(
        local,
        mesh=fine,
        in_specs=(three, P(None, None, SUB, BLK), three, three, three) + (P(),) * 9,
        out_specs=(three, two, two) + (P(),) * 9,
        check_vma=False,
    )
```

time: 796 us -> 134 us (0.17)
  waiting for transfers between devices: 381 us -> 0.01 us
  blocking collectives: 208 us -> 59.9 us
  starting transfers between devices: 131 us -> 13.3 us
  matrix products: 38.9 us -> 0 us
  Pallas kernels: 0 us -> 32.3 us
  local copies, waits for them, and re-layouts: 7.86 us -> 24.9 us
  between operations: 15.8 us -> 0.95 us
    psum x1 -> x0, waiting for transfers between devices: 347 us -> none  [local(): grad_two, gb_two = lax.psum((grad_two, gb_two), ('blk', 'sub'))]
    psum x2 -> x0, blocking collectives: 208 us -> none  [the longest x1 109 us: local(): total_square = lax.psum(local_square, ('blk', 'sub'))]
    ppermute x32 -> x4, starting transfers between devices: 131 us -> 13.3 us  [shifted(): return (lax.ppermute(last, axes, up), lax.ppermute(initial, axes, down))]
    all_to_all x0 -> x3, blocking collectives: none -> 59.9 us  [the longest x1 22.8 us: summed(): part = lax.all_to_all(value.reshape(near, rows, 128), NEAR, 0, 0)]
    dot_general x13 -> x0, matrix products: 38.9 us -> none  [the longest x3 10.3 us: next_terms(): grad_now = jnp.einsum('ic,jc->ij', delta_now, layer_prev, precision=HIGH)]
    ppermute x32 -> x4, waiting for transfers between devices: 33.8 us -> 0.01 us  [shifted(): return (lax.ppermute(last, axes, up), lax.ppermute(initial, axes, down))]
    pallas_call x0 -> x5, Pallas kernels: none -> 32.3 us  [the longest x1 16.4 us: final_call(): pl.pallas_call(final_kernel, in_specs=[vmem] * 8 + [hbm] * 8 + [vmem], ou...]
    unnamed x45 -> x64, local copies, waits for them, and re-layouts: 6.47 us -> 21.6 us
  transfers between devices with their start and end apart: 33 -> 4, of which waited for: 15 -> 0; matrix products, arithmetic and copies ran while one was open for 1% -> 2% of each run, Pallas kernels for 0% -> 9%
where the time goes in v1:
time: 134 us; the launch traced here: 133 us
  blocking collectives  59.9 us (45%)
  Pallas kernels  32.3 us (24%)
  local copies, waits for them, and re-layouts  24.9 us (19%)
  starting transfers between devices  13.3 us (10%)
  other arithmetic  1.47 us (1%)
    all_to_all x1, blocking collectives, summed(): part = lax.all_to_all(value.reshape(near, rows, 128), NEAR, 0, 0)  22.8 us
    all_to_all x1, blocking collectives, summed(): lax.all_to_all(jnp.broadcast_to(part[None], (far, rows, 128)), FAR, 0, 0)  21.7 us
    unnamed x64, local copies, waits for them, and re-layouts  21.6 us
    pallas_call x1, Pallas kernels, final_call(): pl.pallas_call(final_kernel, in_specs=[vmem] * 8 + [hbm] * 8 + [vmem], ou...  16.4 us
    all_to_all x1, blocking collectives, summed(): lax.all_to_all(jnp.broadcast_to(part[None], (near, rows, 128)), NEAR, 0, 0)  15.4 us
    ppermute x4, starting transfers between devices, shifted(): return (lax.ppermute(last, axes, up), lax.ppermute(initial, axes, down))  13.3 us
    pallas_call x1, Pallas kernels, forward_call(): pl.pallas_call(forward_kernel, grid=(rows // GROUP,), in_specs=[block(16,...  5.97 us
    pallas_call x1, Pallas kernels, backward_call(): pl.pallas_call(backward_kernel, grid=(rows // GROUP,), in_specs=[block(12...  5.7 us
  transfers between devices with their start and end apart: 4, of which 0 were waited for; matrix products, arithmetic and copies ran while one was open for 2% of the time, Pallas kernels for 9%

profile of v1, /device:TPU:1, one launch (start us, length us, event | category | flops | bytes accessed | tf_op | source)
XLA Modules:
  0.0 132.8 jit_solution(2145795621169963214)
XLA Ops:
  0.7 1.0 fusion
  3.9 3.9 %collective-permute-start = (f32[46,8,128]{2,1,0:T(8,128)}, f32[46,8,128]{2,1,0:T(8,128)S(1)}, u32[]{:S(2)}, u32[]{:S(2)}) collective-permute-start(f32[46,8,128]{2,1,0:T(8,128)} %pad_maximum_fusion), channel_id=1, source_target_pairs={{0,1},{1,2},{2,3},{3,4},{4,5},{5,6},{6,7},{8,9},{9,10},{10,11},{11... | collective-permute-start | bytes 565256 | tf_op jit(solution)/shard_map/ppermute | solution.py:375
  8.6 1.3 collective-permute-start.1
  9.9 1.0 copy.31
  11.8 0.9 copy-done.15
  15.2 6.0 %forward.1 = (bf16[32,128,48]{2,1,0:T(8,128)(2,1)S(1)}, bf16[32,128,256]{2,1,0:T(8,128)(2,1)S(1)}, bf16[32,128,256]{2,1,0:T(8,128)(2,1)S(1)}, bf16[32,128,256]{2,1,0:T(8,128)(2,1)S(1)}, f32[32,128,128]{2,1,0:T(8,128)S(1)}) custom-call(f32[32,16,128]{2,1,0:T(8,128)S(1)} %copy-done.15, f32[16,128]{1,0:T(8,128)S(1)} %pad.9.win_ref, f32[128,128]{1,0:T(8,128)S(1)} %copy-done.17, ...), custom_call_target="tpu_custom_call" | custom-call | flops 8000000000 | bytes 9000000 | tf_op jit(solution)/shard_map/forward/pallas_call | solution.py:71
  21.2 1.3 %copy-done.1 = bf16[32,128,256]{2,1,0:T(8,128)(2,1)} copy-done((bf16[32,128,256]{2,1,0:T(8,128)(2,1)}, bf16[32,128,256]{2,1,0:T(8,128)(2,1)S(1)}, u32[]{:S(2)}) %copy-start.1) | copy-done | bytes 2097176
  22.6 1.3 %copy-done.4 = bf16[32,128,256]{2,1,0:T(8,128)(2,1)} copy-done((bf16[32,128,256]{2,1,0:T(8,128)(2,1)}, bf16[32,128,256]{2,1,0:T(8,128)(2,1)S(1)}, u32[]{:S(2)}) %copy-start.4) | copy-done | bytes 2097176
  23.9 1.4 %copy-done.23 = f32[32,128,128]{2,1,0:T(8,128)} copy-done((f32[32,128,128]{2,1,0:T(8,128)}, f32[32,128,128]{2,1,0:T(8,128)S(1)}, u32[]{:S(2)}) %copy-start.23) | copy-done | bytes 2097176
  26.6 2.5 %pack.1 = (f32[3,48,128]{2,1,0:T(8,128)}, f32[3,48,128]{2,1,0:T(8,128)}) custom-call(f32[46,8,128]{2,1,0:T(8,128)} %copy-done.9, f32[36,32,128]{2,1,0:T(8,128)} %bitcast.19, f32[4,32,128]{2,1,0:T(8,128)} %cpl_ref.3, f32[6,32,128]{2,1,0:T(8,128)} %mis_ref.3, f32[46,8,128]{2,1,0:T(8,128)} %copy-done.11), custom_call_target="tpu_custom_call" | custom-call | tf_op jit(solution)/shard_map/pack/pallas_call | solution.py:154
  29.1 5.2 %collective-permute-start.2 = (f32[3,48,128]{2,1,0:T(8,128)}, f32[3,48,128]{2,1,0:T(8,128)S(1)}, u32[]{:S(2)}, u32[]{:S(2)}) collective-permute-start(f32[3,48,128]{2,1,0:T(8,128)} %get-tuple-element.36), channel_id=1, source_target_pairs={{0,8},{8,16},{16,24},{24,32},{32,40},{40,48},{48,56},{56,64},{64,7... | collective-permute-start | bytes 221192 | tf_op jit(solution)/shard_map/ppermute | solution.py:375
  34.3 2.9 %collective-permute-start.3 = (f32[3,48,128]{2,1,0:T(8,128)}, f32[3,48,128]{2,1,0:T(8,128)S(1)}, u32[]{:S(2)}, u32[]{:S(2)}) collective-permute-start(f32[3,48,128]{2,1,0:T(8,128)} %get-tuple-element.37), channel_id=1, source_target_pairs={{8,0},{16,8},{24,16},{32,24},{40,32},{48,40},{56,48},{64,56},{72,6... | collective-permute-start | bytes 221192 | tf_op jit(solution)/shard_map/ppermute | solution.py:375
  37.2 1.6 %copy-done.2 = bf16[32,128,256]{2,1,0:T(8,128)(2,1)S(1)} copy-done((bf16[32,128,256]{2,1,0:T(8,128)(2,1)S(1)}, bf16[32,128,256]{2,1,0:T(8,128)(2,1)}, u32[]{:S(2)}) %copy-start.2) | copy-done | bytes 2097176
  38.8 1.6 %copy-done.5 = bf16[32,128,256]{2,1,0:T(8,128)(2,1)S(1)} copy-done((bf16[32,128,256]{2,1,0:T(8,128)(2,1)S(1)}, bf16[32,128,256]{2,1,0:T(8,128)(2,1)}, u32[]{:S(2)}) %copy-start.5) | copy-done | bytes 2097176
  42.9 1.6 %copy-done.24 = f32[32,128,128]{2,1,0:T(8,128)S(1)} copy-done((f32[32,128,128]{2,1,0:T(8,128)S(1)}, f32[32,128,128]{2,1,0:T(8,128)}, u32[]{:S(2)}) %copy-start.24) | copy-done | bytes 2097176
  44.5 5.7 %backward.1 = (f32[32,1,128]{2,1,0:T(1,128)}, f32[32,128,128]{2,1,0:T(8,128)S(1)}, f32[32,128,128]{2,1,0:T(8,128)S(1)}, f32[32,128,128]{2,1,0:T(8,128)S(1)}, f32[32,128,128]{2,1,0:T(8,128)S(1)}) custom-call(bf16[32,128,256]{2,1,0:T(8,128)(2,1)S(1)} %get-tuple-element.39.l1_ref.l1_hbm, bf16[32,128,256]{2,1,0:T(8,128)(2,1)S(1)} %copy-done.2, ...), custom_call_target="tpu_custom_call" | custom-call | flops 8000000000 | bytes 17000000 | tf_op jit(solution)/shard_map/backward/pallas_call | solution.py:110
  50.2 1.4 %copy-done.7 = f32[32,128,128]{2,1,0:T(8,128)} copy-done((f32[32,128,128]{2,1,0:T(8,128)}, f32[32,128,128]{2,1,0:T(8,128)S(1)}, u32[]{:S(2)}) %copy-start.7) | copy-done | bytes 2097176
  51.6 1.4 %copy-done.8 = f32[32,128,128]{2,1,0:T(8,128)} copy-done((f32[32,128,128]{2,1,0:T(8,128)}, f32[32,128,128]{2,1,0:T(8,128)S(1)}, u32[]{:S(2)}) %copy-start.8) | copy-done | bytes 2097176
  53.1 16.4 %final.1 = (f32[6,32,128]{2,1,0:T(8,128)}, f32[32,128]{1,0:T(8,128)}, f32[512,128]{1,0:T(8,128)S(1)}) custom-call(f32[46,8,128]{2,1,0:T(8,128)S(1)} %copy-done.10, f32[36,32,128]{2,1,0:T(8,128)S(1)} %bitcast.20, f32[4,32,128]{2,1,0:T(8,128)S(1)} %copy-done.14, f32[6,32,128]{2,1,0:T(8,128)S(1)} %copy-done.13, f32[46,8,128]{2,1,0:T(8,128)S(1)} %copy-done.12, ...), custom_call_target="tpu_custom_call" | custom-call | tf_op jit(solution)/shard_map/final/pallas_call | solution.py:322
  69.5 22.8 %all_to_all.15 = f32[32,16,128]{2,1,0:T(8,128)S(1)} all-to-all(f32[32,16,128]{2,1,0:T(8,128)S(1)} %bitcast.21), channel_id=1, replica_groups=mesh['z'=16,'xh'=2,'c'=2,'y'=4,'xl'=2] {'xh','c','y','xl'}, dimensions={0} | all-to-all | bytes 524288 | tf_op jit(solution)/shard_map/all_to_all | solution.py:381
  92.4 21.7 %all_to_all.16 = f32[16,16,128]{2,1,0:T(8,128)S(1)} all-to-all(f32[16,16,128]{2,1,0:T(8,128)S(1)} %broadcast_in_dim.4), channel_id=1, replica_groups=mesh['z'=16,'xh'=2,'c'=2,'y'=4,'xl'=2] {'z'}, dimensions={0} | all-to-all | bytes 262144 | tf_op jit(solution)/shard_map/all_to_all | solution.py:383
  114.1 15.4 %all_to_all.17 = f32[32,16,128]{2,1,0:T(8,128)} all-to-all(f32[32,16,128]{2,1,0:T(8,128)S(1)} %broadcast_in_dim.5), channel_id=1, replica_groups=mesh['z'=16,'xh'=2,'c'=2,'y'=4,'xl'=2] {'xh','c','y','xl'}, dimensions={0} | all-to-all | bytes 524288 | tf_op jit(solution)/shard_map/all_to_all | solution.py:385
  129.5 1.7 %unpack.1 = (f32[128,128]{1,0:T(8,128)}, f32[128,128]{1,0:T(8,128)}, f32[128,128]{1,0:T(8,128)}, f32[128,12]{1,0:T(8,128)}, f32[1,128]{1,0:T(1,128)}, /*index=5*...) custom-call(f32[512,128]{1,0:T(8,128)} %bitcast.23), custom_call_target="tpu_custom_call" | custom-call | tf_op jit(solution)/shard_map/unpack/pallas_call | solution.py:364
  131.3 1.5 %copy.29 = f32[128,12]{0,1:T(8,128)} copy(f32[128,12]{1,0:T(8,128)} %get-tuple-element.75) | data formatting | bytes 12288
  (68 shorter events, 10.2 us)
Async XLA Ops:
  0.6 11.0 %copy-start.26 = (f32[128,12]{0,1:T(8,128)S(1)}, f32[128,12]{0,1:T(8,128)}, u32[]{:S(2)}) copy-start(f32[128,12]{0,1:T(8,128)} %param.19) | copy-start | bytes 18436
  0.7 11.0 %copy-start.27 = (f32[128]{0:T(128)S(1)}, f32[128]{0:T(128)}, u32[]{:S(2)}) copy-start(f32[128]{0:T(128)} %param.20) | copy-start | bytes 1540
  0.7 11.0 %copy-start.28 = (f32[128]{0:T(128)S(1)}, f32[128]{0:T(128)}, u32[]{:S(2)}) copy-start(f32[128]{0:T(128)} %param.22) | copy-start | bytes 1540
  0.7 11.0 %copy-start.29 = (f32[128]{0:T(128)S(1)}, f32[128]{0:T(128)}, u32[]{:S(2)}) copy-start(f32[128]{0:T(128)} %param.24) | copy-start | bytes 1540
  0.7 11.0 %copy-start.30 = (f32[128]{0:T(128)S(1)}, f32[128]{0:T(128)}, u32[]{:S(2)}) copy-start(f32[128]{0:T(128)} %param.26) | copy-start | bytes 1540
  0.7 11.0 %copy-start.25 = (f32[128]{0:T(128)S(1)}, f32[128]{0:T(128)}, u32[]{:S(2)}) copy-start(f32[128]{0:T(128)} %param.27) | copy-start | bytes 1540
  3.9 21.3 %collective-permute-start = (f32[46,8,128]{2,1,0:T(8,128)}, f32[46,8,128]{2,1,0:T(8,128)S(1)}, u32[]{:S(2)}, u32[]{:S(2)}) collective-permute-start(f32[46,8,128]{2,1,0:T(8,128)} %pad_maximum_fusion), channel_id=1, source_target_pairs={{0,1},{1,2},{2,3},{3,4},{4,5},{5,6},{6,7},{8,9},{9,10},{10,11},{11... | collective-permute-start | bytes 565256 | tf_op jit(solution)/shard_map/ppermute | solution.py:375
  8.6 16.7 %collective-permute-start.1 = (f32[46,8,128]{2,1,0:T(8,128)}, f32[46,8,128]{2,1,0:T(8,128)S(1)}, u32[]{:S(2)}, u32[]{:S(2)}) collective-permute-start(f32[46,8,128]{2,1,0:T(8,128)} %pad_maximum_fusion.1), channel_id=1, source_target_pairs={{1,0},{2,1},{3,2},{4,3},{5,4},{6,5},{7,6},{9,8},{10,9},{11,10},{12... | collective-permute-start | bytes 565256 | tf_op jit(solution)/shard_map/ppermute | solution.py:375
  23.9 1.4 %copy-start.23 = (f32[32,128,128]{2,1,0:T(8,128)}, f32[32,128,128]{2,1,0:T(8,128)S(1)}, u32[]{:S(2)}) copy-start(f32[32,128,128]{2,1,0:T(8,128)S(1)} %get-tuple-element.42.l4_ref) | copy-start | bytes 6291460
  29.1 23.9 %collective-permute-start.2 = (f32[3,48,128]{2,1,0:T(8,128)}, f32[3,48,128]{2,1,0:T(8,128)S(1)}, u32[]{:S(2)}, u32[]{:S(2)}) collective-permute-start(f32[3,48,128]{2,1,0:T(8,128)} %get-tuple-element.36), channel_id=1, source_target_pairs={{0,8},{8,16},{16,24},{24,32},{32,40},{40,48},{48,56},{56,64},{64,7... | collective-permute-start | bytes 221192 | tf_op jit(solution)/shard_map/ppermute | solution.py:375
  34.3 18.7 %collective-permute-start.3 = (f32[3,48,128]{2,1,0:T(8,128)}, f32[3,48,128]{2,1,0:T(8,128)S(1)}, u32[]{:S(2)}, u32[]{:S(2)}) collective-permute-start(f32[3,48,128]{2,1,0:T(8,128)} %get-tuple-element.37), channel_id=1, source_target_pairs={{8,0},{16,8},{24,16},{32,24},{40,32},{48,40},{56,48},{64,56},{72,6... | collective-permute-start | bytes 221192 | tf_op jit(solution)/shard_map/ppermute | solution.py:375
  37.2 1.6 %copy-start.2 = (bf16[32,128,256]{2,1,0:T(8,128)(2,1)S(1)}, bf16[32,128,256]{2,1,0:T(8,128)(2,1)}, u32[]{:S(2)}) copy-start(bf16[32,128,256]{2,1,0:T(8,128)(2,1)} %copy-done.1) | copy-start | bytes 6291460
  38.8 1.6 %copy-start.5 = (bf16[32,128,256]{2,1,0:T(8,128)(2,1)S(1)}, bf16[32,128,256]{2,1,0:T(8,128)(2,1)}, u32[]{:S(2)}) copy-start(bf16[32,128,256]{2,1,0:T(8,128)(2,1)} %copy-done.4) | copy-start | bytes 6291460
  42.9 1.6 %copy-start.24 = (f32[32,128,128]{2,1,0:T(8,128)S(1)}, f32[32,128,128]{2,1,0:T(8,128)}, u32[]{:S(2)}) copy-start(f32[32,128,128]{2,1,0:T(8,128)} %copy-done.23) | copy-start | bytes 6291460
  44.5 8.5 %copy-start = (f32[6,6,32,128]{3,2,1,0:T(8,128)S(1)}, f32[6,6,32,128]{3,2,1,0:T(8,128)}, u32[]{:S(2)}) copy-start(f32[6,6,32,128]{3,2,1,0:T(8,128)} %param.15) | copy-start | bytes 1769476
  44.5 8.6 %copy-start.3 = (bf16[32,128,256]{2,1,0:T(8,128)(2,1)S(1)}, bf16[32,128,256]{2,1,0:T(8,128)(2,1)}, u32[]{:S(2)}) copy-start(bf16[32,128,256]{2,1,0:T(8,128)(2,1)} %copy-done.1) | copy-start | bytes 6291460
  44.5 8.6 %copy-start.6 = (bf16[32,128,256]{2,1,0:T(8,128)(2,1)S(1)}, bf16[32,128,256]{2,1,0:T(8,128)(2,1)}, u32[]{:S(2)}) copy-start(bf16[32,128,256]{2,1,0:T(8,128)(2,1)} %copy-done.4) | copy-start | bytes 6291460
  44.5 8.6 %copy-start.10 = (f32[46,8,128]{2,1,0:T(8,128)S(1)}, f32[46,8,128]{2,1,0:T(8,128)}, u32[]{:S(2)}) copy-start(f32[46,8,128]{2,1,0:T(8,128)} %copy-done.9) | copy-start | bytes 565252
  44.5 8.6 %copy-start.12 = (f32[46,8,128]{2,1,0:T(8,128)S(1)}, f32[46,8,128]{2,1,0:T(8,128)}, u32[]{:S(2)}) copy-start(f32[46,8,128]{2,1,0:T(8,128)} %copy-done.11) | copy-start | bytes 565252
  44.5 8.6 %copy-start.13 = (f32[6,32,128]{2,1,0:T(8,128)S(1)}, f32[6,32,128]{2,1,0:T(8,128)}, u32[]{:S(2)}) copy-start(f32[6,32,128]{2,1,0:T(8,128)} %mis_ref.3) | copy-start | bytes 294916
  44.5 8.6 %copy-start.14 = (f32[4,32,128]{2,1,0:T(8,128)S(1)}, f32[4,32,128]{2,1,0:T(8,128)}, u32[]{:S(2)}) copy-start(f32[4,32,128]{2,1,0:T(8,128)} %cpl_ref.3) | copy-start | bytes 196612
  44.5 8.6 %copy-start.16 = (f32[6,32,128]{2,1,0:T(8,128)S(1)}, f32[6,32,128]{2,1,0:T(8,128)}, u32[]{:S(2)}) copy-start(f32[6,32,128]{2,1,0:T(8,128)} %prod_ref.1) | copy-start | bytes 294916
  50.2 1.4 %copy-start.7 = (f32[32,128,128]{2,1,0:T(8,128)}, f32[32,128,128]{2,1,0:T(8,128)S(1)}, u32[]{:S(2)}) copy-start(f32[32,128,128]{2,1,0:T(8,128)S(1)} %get-tuple-element.45.d2t_hbm) | copy-start | bytes 6291460
  51.6 1.4 %copy-start.8 = (f32[32,128,128]{2,1,0:T(8,128)}, f32[32,128,128]{2,1,0:T(8,128)S(1)}, u32[]{:S(2)}) copy-start(f32[32,128,128]{2,1,0:T(8,128)S(1)} %get-tuple-element.46.d1t_hbm) | copy-start | bytes 6291460
  (11 other events, 10.0 us)

commit v2 on v1

v2 whole, which is shorter than its diff:
```python
import functools
import jax
import jax.numpy as jnp
from jax import lax
from jax.experimental import pallas as pl
from jax.experimental.pallas import tpu as pltpu
from jax.sharding import Mesh, PartitionSpec as P

SWEEPS = 8
EPS = 1e-06
BLK = ("z", "xh", "c")
SUB = ("y", "xl")
NEAR = ("xh", "c", "y", "xl")
FAR = ("z",)
F32 = jnp.float32
BF16 = jnp.bfloat16
GROUP = 4
WIDE = 4
PARTS = 4
MIB = 1 << 20
LIMIT = 8 * MIB


def split(value):
    high = value.astype(BF16)
    return high, (value - high.astype(F32)).astype(BF16)


def pair(value):
    return jnp.concatenate(split(value), axis=1)


def joined(both):
    return both[:, :128].astype(F32) + both[:, 128:].astype(F32)


def times(both, weights):
    out = jnp.dot(both, weights, preferred_element_type=F32)
    return out[:, :128] + out[:, 128:]


def stacked(weight):
    both = pair(weight)
    return jnp.concatenate([both, both], axis=0)


VMEM = pl.BlockSpec(memory_space=pltpu.VMEM)
ANY = pl.BlockSpec(memory_space=pl.ANY)
HBM = pl.BlockSpec(memory_space=pltpu.MemorySpace.HBM)


def network_rows(x_ref, base, count, prepared, vectors, outs):
    s1, f2, f3, f4, b2, b3, b4, wt = prepared
    bias1, bias2, bias3, bias4, wout = (vectors.at[pl.ds(n, 1)] for n in range(5))
    corr_ref, xc_ref, l1_ref, l2_ref, l3_ref, l4t_ref, d3t_ref, d2t_ref, d1t_ref = outs
    pad = jnp.zeros((4, 128), F32)

    def step(g, carry):
        at = GROUP * g
        columns = []
        for r in range(GROUP):
            x = jnp.concatenate([x_ref[:, base + at + r, :], pad], axis=0)
            high = x.astype(BF16).astype(F32)
            column = jnp.concatenate([high, x - high, high], axis=0).T.astype(BF16)
            xc_ref[at + r] = column
            columns.append(column)
        inputs = jnp.concatenate(columns, axis=0)
        layer = jnp.tanh(jnp.dot(inputs, s1[...], preferred_element_type=F32) + bias1[...])
        layers = []
        for out, weights, bias in ((l1_ref, f2, bias2), (l2_ref, f3, bias3), (l3_ref, f4, bias4)):
            layers.append(layer)
            both = pair(layer)
            out[pl.ds(at, GROUP)] = both.reshape(GROUP, 128, 256)
            layer = jnp.tanh(times(both, weights[...]) + bias[...])
        for r in range(GROUP):
            turned = layer[128 * r : 128 * r + 128].T
            l4t_ref[at + r] = turned
            corr_ref[at + r] = 1.0 + jnp.sum(turned * wt[...], axis=0, keepdims=True)
        delta = wout[...] * (1.0 - layer * layer)
        for weights, out in ((b4, d3t_ref), (b3, d2t_ref), (b2, d1t_ref)):
            layer = layers.pop()
            delta = times(pair(delta), weights[...]) * (1.0 - layer * layer)
            for r in range(GROUP):
                out[at + r] = delta[128 * r : 128 * r + 128].T
        return carry

    lax.fori_loop(0, count // GROUP, step, 0)


def network_shapes(count):
    return [
        jax.ShapeDtypeStruct((count, 1, 128), F32),
        jax.ShapeDtypeStruct((count, 128, 48), BF16),
    ] + [jax.ShapeDtypeStruct((count, 128, 256), BF16)] * 3 + [jax.ShapeDtypeStruct((count, 128, 128), F32)] * 4


PREPARED = [jax.ShapeDtypeStruct((48, 128), BF16)] + [jax.ShapeDtypeStruct((256, 256), BF16)] * 6 + [
    jax.ShapeDtypeStruct((128, 128), F32)]


def cost(count):
    return pl.CostEstimate(flops=count * 3 * 10**8, bytes_accessed=count * 1000, transcendentals=0)


def strips(fields, out, row, sem):
    moves, at = [], 0
    for i, field in enumerate(fields):
        n = field.shape[0]
        moves.append(pltpu.make_async_copy(field.at[:, pl.ds(row, 8)], out.at[pl.ds(at, n)], sem.at[i]))
        at += n
    for move in moves:
        move.start()
    return moves


def last_kernel(inv_hbm, cpl_hbm, mis_hbm, out_hbm, sem):
    rows = mis_hbm.shape[1]
    for move in strips((inv_hbm, cpl_hbm, mis_hbm), out_hbm, rows - 8, sem):
        move.wait()


def last_call(inv, cpl, mis):
    return pl.pallas_call(
        last_kernel,
        in_specs=[HBM] * 3,
        out_specs=ANY,
        out_shape=jax.ShapeDtypeStruct((46, 8, 128), F32),
        scratch_shapes=[pltpu.SemaphoreType.DMA((3,))],
        compiler_params=pltpu.CompilerParams(vmem_limit_bytes=MIB),
        name="last_rows",
    )(inv, cpl, mis)


def opening_kernel(base, count, last_hbm, inv_hbm, cpl_hbm, mis_hbm, x_hbm, win_hbm, w2_hbm, w3_hbm, w4_hbm, *rest):
    vectors, rest = rest[:5], rest[5:]
    strip, x_ref, vec, prepared, outs = rest[0], rest[1], rest[2], rest[3:11], rest[11:20]
    win_ref, w2_ref, w3_ref, w4_ref, sem, strip_sem = rest[20:]
    moves = [
        pltpu.make_async_copy(source, target, sem.at[i])
        for i, (source, target) in enumerate(
            [(w2_hbm, w2_ref), (w3_hbm, w3_ref), (w4_hbm, w4_ref), (win_hbm, win_ref), (x_hbm, x_ref)]
            + [(vector, vec.at[pl.ds(n, 1)]) for n, vector in enumerate(vectors)])
    ]
    for move in moves:
        move.start()
    held = strips((inv_hbm, cpl_hbm, mis_hbm), strip, 0, strip_sem)
    s1, f2, f3, f4, b2, b3, b4, wt = prepared
    for move in moves:
        move.wait()
    win = jnp.concatenate([win_ref[...], jnp.zeros((4, 128), F32)], axis=0)
    high = win.astype(BF16).astype(F32)
    s1[...] = jnp.concatenate([high, high, win - high], axis=0).astype(BF16)
    for raw, ahead, back in ((w2_ref, f2, b2), (w3_ref, f3, b3), (w4_ref, f4, b4)):
        ahead[...] = stacked(raw[...].T)
        back[...] = stacked(raw[...])
    wt[...] = jnp.broadcast_to(vec[4:5], (128, 128)).T
    network_rows(x_ref, base, count, prepared, vec, outs)
    for move in held:
        move.wait()


def opening_call(base, count, last, inv, cpl, mis, x, win, w2, w3, w4, vectors):
    return pl.pallas_call(
        functools.partial(opening_kernel, base, count),
        in_specs=[ANY] + [HBM] * 13,
        out_specs=[ANY] + [VMEM] * 19,
        out_shape=[jax.ShapeDtypeStruct((46, 8, 128), F32), jax.ShapeDtypeStruct(x.shape, F32),
                   jax.ShapeDtypeStruct((8, 128), F32)] + PREPARED + network_shapes(count),
        scratch_shapes=[pltpu.VMEM((12, 128), F32)] + [pltpu.VMEM((128, 128), F32)] * 3
        + [pltpu.SemaphoreType.DMA((10,)), pltpu.SemaphoreType.DMA((3,))],
        compiler_params=pltpu.CompilerParams(vmem_limit_bytes=LIMIT),
        cost_estimate=cost(count),
        name="network_first",
    )(last, inv, cpl, mis, x, win, w2, w3, w4, *vectors)


def middle_kernel(base, count, token, x_ref, *rest):
    network_rows(x_ref, base, count, rest[:8], rest[8], rest[9:])


def middle_call(base, count, token, x, prepared, vectors):
    return pl.pallas_call(
        functools.partial(middle_kernel, base, count),
        in_specs=[ANY] + [VMEM] * 10,
        out_specs=[VMEM] * 9,
        out_shape=network_shapes(count),
        compiler_params=pltpu.CompilerParams(vmem_limit_bytes=LIMIT),
        cost_estimate=cost(count),
        name="network",
    )(token, x, *prepared, vectors)


def packed(up_ref, inv_ref, cpl_ref, mis_ref, down_ref, out_ref, offset):
    rows = mis_ref.shape[1]
    tiles = rows // 8 + 2
    lane = lax.broadcasted_iota(jnp.int32, (8, 128), 1)
    for t in range(tiles):
        for j in range(3):
            out = jnp.zeros((8, 128), F32)
            for k in range(min(16, 46 - 16 * j)):
                value = tile_of(up_ref, inv_ref, cpl_ref, mis_ref, down_ref, 16 * j + k, t)
                by = (8 * k - offset) % 128
                here = (lane >= 8 * k) & (lane < 8 * k + 8)
                out = jnp.where(here, pltpu.roll(value, by, 1) if by else value, out)
            out_ref[j, pl.ds(8 * t, 8)] = out


def tile_of(up_ref, inv_ref, cpl_ref, mis_ref, down_ref, a, t):
    if t == 0:
        return up_ref[a]
    if t == mis_ref.shape[1] // 8 + 1:
        return down_ref[a]
    at = pl.ds(8 * (t - 1), 8)
    if a < 36:
        return inv_ref[a, at]
    return cpl_ref[a - 36, at] if a < 40 else mis_ref[a - 40, at]


def right_kernel(up_ref, inv_ref, cpl_ref, mis_ref, down_ref, out_ref):
    packed(up_ref, inv_ref, cpl_ref, mis_ref, down_ref, out_ref, 120)


def right_call(up, inv, cpl, mis, down):
    rows = mis.shape[1]
    return pl.pallas_call(
        right_kernel,
        in_specs=[VMEM] * 5,
        out_specs=VMEM,
        out_shape=jax.ShapeDtypeStruct((3, rows + 16, 128), F32),
        compiler_params=pltpu.CompilerParams(vmem_limit_bytes=LIMIT),
        name="right_columns",
    )(up, inv, cpl, mis, down)


def third_kernel(base, count, up_ref, inv_ref, cpl_ref, mis_ref, down_ref, x_ref, *rest):
    network_rows(x_ref, base, count, rest[:8], rest[8], rest[10:])
    packed(up_ref, inv_ref, cpl_ref, mis_ref, down_ref, rest[9], 0)


def third_call(base, count, up, inv, cpl, mis, down, x, prepared, vectors):
    rows = mis.shape[1]
    return pl.pallas_call(
        functools.partial(third_kernel, base, count),
        in_specs=[VMEM] * 15,
        out_specs=[VMEM] * 10,
        out_shape=[jax.ShapeDtypeStruct((3, rows + 16, 128), F32)] + network_shapes(count),
        compiler_params=pltpu.CompilerParams(vmem_limit_bytes=LIMIT),
        cost_estimate=cost(count),
        name="network_left",
    )(up, inv, cpl, mis, down, x, *prepared, vectors)


def final_kernel(up_ref, inv_ref, cpl_ref, mis_ref, down_ref, prod_ref, froml_ref, fromr_ref, wt, *rest):
    parts = [rest[8 * p : 8 * p + 8] for p in range(PARTS)]
    adj_ref, sens_ref, sums_ref, ext, main, side, acc4, acc3, acc2, acc1, flat = rest[8 * PARTS :]
    rows = mis_ref.shape[1]
    tiles = rows // 8 + 2
    lane = lax.broadcasted_iota(jnp.int32, (8, 128), 1)
    first, last = lane == 0, lane == 127

    def tile(a, t):
        return tile_of(up_ref, inv_ref, cpl_ref, mis_ref, down_ref, a, t)

    for a in range(46):
        j, k = a // 16, a % 16
        for t in range(tiles):
            at = pl.ds(8 * t, 8)
            high = fromr_ref[j, at]
            low = froml_ref[j, at]
            high = pltpu.roll(high, (128 - 8 * k) % 128, 1) if k else high
            low = pltpu.roll(low, 120 - 8 * k, 1) if k != 15 else low
            ext[a, at] = jnp.where(lane < 8, high, jnp.where(lane >= 120, low, 0.0))

    edge = jnp.zeros((8, 128), F32)
    for field in (main, side):
        for s in range(2):
            for i in range(6):
                field[s, i, 0:8] = edge
                field[s, i, pl.ds(8 * tiles + 8, 8)] = edge

    def solve(field, s, t, coefficient, rhs):
        for i in range(6):
            total = coefficient(6 * i) * rhs[0]
            for j in range(1, 6):
                total = total + coefficient(6 * i + j) * rhs[j]
            field[s, i, pl.ds(8 * t + 8, 8)] = total

    for t in range(tiles):
        at = pl.ds(8 * t, 8)
        solve(main, 0, t, lambda a: tile(a, t), [tile(40 + i, t) for i in range(6)])
        solve(side, 0, t, lambda a: ext[a, at], [ext[40 + i, at] for i in range(6)])

    def sweep(n, carry):
        s = lax.rem(n, 2)
        for t in range(tiles):
            at = pl.ds(8 * t, 8)
            near, beside = [], []
            for i in range(6):
                m = main[s, i, pl.ds(8 * t + 8, 8)]
                e = side[s, i, pl.ds(8 * t + 8, 8)]
                m_low, m_high = pltpu.roll(m, 1, 1), pltpu.roll(m, 127, 1)
                e_low, e_high = pltpu.roll(e, 1, 1), pltpu.roll(e, 127, 1)
                rhs = tile(40 + i, t) + tile(36, t) * main[s, i, pl.ds(8 * t + 7, 8)]
                rhs = rhs + tile(37, t) * main[s, i, pl.ds(8 * t + 9, 8)]
                rhs = rhs + tile(38, t) * jnp.where(first, e_low, m_low)
                near.append(rhs + tile(39, t) * jnp.where(last, e_high, m_high))
                rhs = ext[40 + i, at] + ext[36, at] * side[s, i, pl.ds(8 * t + 7, 8)]
                rhs = rhs + ext[37, at] * side[s, i, pl.ds(8 * t + 9, 8)]
                rhs = rhs + ext[38, at] * jnp.where(first, m_low, e_low)
                beside.append(rhs + ext[39, at] * jnp.where(last, m_high, e_high))
            solve(main, 1 - s, t, lambda a: tile(a, t), near)
            solve(side, 1 - s, t, lambda a: ext[a, at], beside)
        return carry

    lax.fori_loop(0, SWEEPS - 1, sweep, 0)
    done = (SWEEPS - 1) % 2

    square = jnp.zeros((8, 128), F32)
    for t in range(rows // 8):
        at = pl.ds(8 * t, 8)
        total = jnp.zeros((8, 128), F32)
        for i in range(6):
            value = main[done, i, pl.ds(8 * t + 16, 8)]
            adj_ref[i, at] = value
            total = total + value * prod_ref[i, at]
        sens_ref[at] = -total
        square = square + total * total

    for acc in (acc4, acc3, acc2, acc1):
        acc[...] = jnp.zeros_like(acc)
    flat[...] = jnp.zeros_like(flat)

    def term(scaled, right, acc, slot):
        total = flat[slot]
        pieces = []
        for value in scaled:
            total = total + value
            high, low = split(value)
            pieces.append(jnp.concatenate([high, low], axis=0))
        flat[slot] = total
        left = jnp.concatenate(pieces, axis=1)
        acc[...] += jnp.dot(left, right.reshape(128 * len(pieces), right.shape[2]), preferred_element_type=F32)

    base = 0
    for part in parts:
        xc, l1, l2, l3, l4t, d3t, d2t, d1t = part

        def gather(g, carry, base=base, part=part):
            xc, l1, l2, l3, l4t, d3t, d2t, d1t = part
            at = WIDE * g
            some = pl.ds(at, WIDE)
            weights = [sens_ref[pl.ds(base + at + r, 1), :] for r in range(WIDE)]
            out = flat[4]
            scaled = []
            for r in range(WIDE):
                value = l4t[at + r]
                out = out + value * weights[r]
                scaled.append(wt[...] * (1.0 - value * value) * weights[r])
            flat[4] = out
            term(scaled, l3[some], acc4, 3)
            for delta, layer, acc, slot in ((d3t, l2, acc3, 2), (d2t, l1, acc2, 1), (d1t, xc, acc1, 0)):
                term([delta[at + r] * weights[r] for r in range(WIDE)], layer[some], acc, slot)
            return carry

        lax.fori_loop(0, l1.shape[0] // WIDE, gather, 0)
        base += l1.shape[0]

    for n, acc in enumerate((acc4, acc3, acc2)):
        sums_ref[pl.ds(128 * n, 128)] = (acc[0:128, 0:128] + acc[128:256, 0:128]) + (
            acc[0:128, 128:256] + acc[128:256, 128:256])
    lanes = lax.broadcasted_iota(jnp.int32, (128, 128), 1)
    block = jnp.zeros((128, 128), F32)
    for slot in range(5):
        block = jnp.where(lanes == 16 + slot, jnp.sum(flat[slot], axis=1, keepdims=True), block)
    block = jnp.where(lanes == 21, jnp.sum(square), block)
    own = acc1[0:128] + acc1[128:256]
    own = jnp.concatenate([own, jnp.zeros((128, 80), F32)], axis=1)
    own = own + pltpu.roll(own, 112, 1)
    sums_ref[pl.ds(384, 128)] = jnp.where(lanes < 12, own, block)


def final_call(up, inv, cpl, mis, down, prod, froml, fromr, wt, parts):
    rows = mis.shape[1]
    flat = [value for part in parts for value in part]
    return pl.pallas_call(
        final_kernel,
        in_specs=[VMEM] * (9 + len(flat)),
        out_specs=[VMEM] * 3,
        out_shape=[
            jax.ShapeDtypeStruct((6, rows, 128), F32),
            jax.ShapeDtypeStruct((rows, 128), F32),
            jax.ShapeDtypeStruct((512, 128), F32),
        ],
        scratch_shapes=[
            pltpu.VMEM((46, rows + 16, 128), F32),
            pltpu.VMEM((2, 6, rows + 32, 128), F32),
            pltpu.VMEM((2, 6, rows + 32, 128), F32),
            pltpu.VMEM((256, 256), F32),
            pltpu.VMEM((256, 256), F32),
            pltpu.VMEM((256, 256), F32),
            pltpu.VMEM((256, 48), F32),
            pltpu.VMEM((5, 128, 128), F32),
        ],
        compiler_params=pltpu.CompilerParams(vmem_limit_bytes=LIMIT),
        name="final",
    )(up, inv, cpl, mis, down, prod, froml, fromr, wt, *flat)


def unpack_kernel(sums_ref, w4_ref, w3_ref, w2_ref, win_ref, b1_ref, b2_ref, b3_ref, b4_ref, out_ref):
    block = sums_ref[pl.ds(384, 128)]
    scale = 1.0 / jnp.sqrt(jnp.broadcast_to(block[0:1, 21:22], (1, 128)) + EPS)
    for n, ref in enumerate((w4_ref, w3_ref, w2_ref)):
        ref[...] = sums_ref[pl.ds(128 * n, 128)] * scale
    block = block * scale
    turned = block.T
    win_ref[...] = turned[0:12]
    for n, ref in enumerate((b1_ref, b2_ref, b3_ref, b4_ref, out_ref)):
        ref[...] = turned[16 + n : 17 + n]


def unpack_call(sums):
    shapes = [(128, 128)] * 3 + [(12, 128)] + [(1, 128)] * 5
    return pl.pallas_call(
        unpack_kernel,
        in_specs=[VMEM],
        out_shape=[jax.ShapeDtypeStruct(shape, F32) for shape in shapes],
        name="unpack",
    )(sums)


def sent(value, axes, wrap, by):
    size = lax.axis_size(axes)
    pairs = [(i, (i + by) % size) for i in range(size) if wrap or 0 <= i + by < size]
    return lax.ppermute(value, axes, pairs)


def summed(value):
    near, far = lax.axis_size(NEAR), lax.axis_size(FAR)
    rows = value.shape[0] // near
    part = lax.all_to_all(value.reshape(near, rows, 128), NEAR, 0, 0)
    part = jnp.sum(part, axis=0)
    part = lax.all_to_all(jnp.broadcast_to(part[None], (far, rows, 128)), FAR, 0, 0)
    part = jnp.sum(part, axis=0)
    whole = lax.all_to_all(jnp.broadcast_to(part[None], (near, rows, 128)), NEAR, 0, 0)
    return whole.reshape(near * rows, 128)


def local(features, inverse_diag, couplings, mismatch, production, weight_in, bias_in, weight_two,
          bias_two, weight_three, bias_three, weight_four, bias_four, weight_out):
    nvars, rows, cols = mismatch.shape
    inverse = inverse_diag.reshape(nvars * nvars, rows, cols)
    win = weight_in.T
    vectors = [v.reshape(1, 128) for v in (bias_in, bias_two, bias_three, bias_four, weight_out)]
    count = rows // PARTS

    last = last_call(inverse, couplings, mismatch)
    above = sent(last, SUB, False, 1)
    initial, features, vectors, *rest = opening_call(
        0, count, last, inverse, couplings, mismatch, features, win, weight_two, weight_three, weight_four, vectors)
    prepared, first = rest[:8], rest[8:]
    below = sent(initial, SUB, False, -1)
    second = middle_call(count, count, above, features, prepared, vectors)

    right = right_call(above, inverse, couplings, mismatch, below)
    from_low = sent(right, BLK, True, 1)
    left, *third = third_call(2 * count, count, above, inverse, couplings, mismatch, below, features,
                              prepared, vectors)
    from_high = sent(left, BLK, True, -1)
    fourth = middle_call(3 * count, count, from_low, features, prepared, vectors)

    parts = (first, second, third, fourth)
    correction = jnp.concatenate([part[0] for part in parts], axis=0)
    adjoint, sensitivity, sums = final_call(
        above, inverse, couplings, mismatch, below, production, from_low, from_high, prepared[7],
        [part[1:] for part in parts])
    g4, g3, g2, gin, b1, b2, b3, b4, gout = unpack_call(summed(sums))
    flat = lambda value: value.reshape(128)
    return (adjoint, sensitivity, correction.reshape(rows, cols), gin.T, flat(b1), g2, flat(b2),
            g3, flat(b3), g4, flat(b4), flat(gout))


def solution(mesh):
    sizes = (16, 2, 2, 4, 2) if mesh.devices.size == 512 else (mesh.shape["blk"], 1, 1, mesh.shape["sub"], 1)
    fine = Mesh(mesh.devices.reshape(sizes), BLK + SUB)
    three = P(None, SUB, BLK)
    two = P(SUB, BLK)
    return jax.shard_map(
        local,
        mesh=fine,
        in_specs=(three, P(None, None, SUB, BLK), three, three, three) + (P(),) * 9,
        out_specs=(three, two, two) + (P(),) * 9,
        check_vma=False,
    )
```

time: 134 us -> 109 us (0.81)
  local copies, waits for them, and re-layouts: 24.9 us -> 8.12 us
  blocking collectives: 59.9 us -> 44.1 us
  waiting for transfers between devices: 0.01 us -> 13.5 us
  Pallas kernels: 32.3 us -> 20 us
  starting transfers between devices: 13.3 us -> 21.4 us
    all_to_all x1 -> x0, blocking collectives: 15.4 us -> none  [summed(): lax.all_to_all(jnp.broadcast_to(part[None], (near, rows, 128)), NEAR, 0, 0)]
    unnamed x64 -> x36, local copies, waits for them, and re-layouts: 21.6 us -> 7.38 us
    pallas_call x5 -> x8, Pallas kernels: 32.3 us -> 20 us  [the longest x1 7.35 us: final_call(): pl.pallas_call(final_kernel, in_specs=[VMEM] * (9 + len(flat)), out_specs...]
    all_to_all x0 -> x1, waiting for transfers between devices: none -> 8.2 us  [summed(): lax.all_to_all(jnp.broadcast_to(part[None], (near, rows, 128)), NEAR, 0, 0)]
    all_to_all x0 -> x1, starting transfers between devices: none -> 6.8 us  [summed(): lax.all_to_all(jnp.broadcast_to(part[None], (near, rows, 128)), NEAR, 0, 0)]
    ppermute x4, waiting for transfers between devices: 0.01 us -> 5.33 us  [sent(): return lax.ppermute(value, axes, pairs)]
    slice x3 -> x0, local copies, waits for them, and re-layouts: 2.54 us -> none  [local(): initial = jnp.concatenate([field[:, :8] for field in fields], axis=0)]
    all_to_all x1, blocking collectives: 22.8 us -> 21.5 us  [summed(): part = lax.all_to_all(value.reshape(near, rows, 128), NEAR, 0, 0)]
  transfers between devices with their start and end apart: 4 -> 5, of which waited for: 0 -> 3; matrix products, arithmetic and copies ran while one was open for 2% -> 1% of each run, Pallas kernels for 9% -> 10%
where the time goes in v2:
time: 109 us
  blocking collectives  44.1 us (40%)
  starting transfers between devices  21.4 us (20%)
  Pallas kernels  20 us (18%)
  waiting for transfers between devices  13.5 us (12%)
  local copies, waits for them, and re-layouts  8.12 us (7%)
    all_to_all x1, blocking collectives, summed(): lax.all_to_all(jnp.broadcast_to(part[None], (far, rows, 128)), FAR, 0, 0)  22.6 us
    all_to_all x1, blocking collectives, summed(): part = lax.all_to_all(value.reshape(near, rows, 128), NEAR, 0, 0)  21.5 us
    ppermute x4, starting transfers between devices, sent(): return lax.ppermute(value, axes, pairs)  14.6 us
    all_to_all x1, waiting for transfers between devices, summed(): lax.all_to_all(jnp.broadcast_to(part[None], (near, rows, 128)), NEAR, 0, 0)  8.2 us
    unnamed x36, local copies, waits for them, and re-layouts  7.38 us
    pallas_call x1, Pallas kernels, final_call(): pl.pallas_call(final_kernel, in_specs=[VMEM] * (9 + len(flat)), out_specs...  7.35 us
    all_to_all x1, starting transfers between devices, summed(): lax.all_to_all(jnp.broadcast_to(part[None], (near, rows, 128)), NEAR, 0, 0)  6.8 us
    ppermute x4, waiting for transfers between devices, sent(): return lax.ppermute(value, axes, pairs)  5.33 us
  transfers between devices with their start and end apart: 5, of which 3 were waited for; matrix products, arithmetic and copies ran while one was open for 1% of the time, Pallas kernels for 10%

profile of v2, /device:TPU:1, one launch (start us, length us, event | category | flops | bytes accessed | tf_op | source)
XLA Modules:
  0.0 108.6 jit_solution(12728408062550037079)
XLA Ops:
  0.7 1.1 copy-done
  1.7 0.9 copy-done.2
  2.6 0.8 copy-done.4
  3.5 4.1 %collective-permute-start = (f32[46,8,128]{2,1,0:T(8,128)S(1)}, f32[46,8,128]{2,1,0:T(8,128)S(1)}, u32[]{:S(2)}, u32[]{:S(2)}) collective-permute-start(f32[46,8,128]{2,1,0:T(8,128)S(1)} %last_rows.1.last_hbm), channel_id=1, source_target_pairs={{0,1},{1,2},{2,3},{3,4},{4,5},{5,6},{6,7},{8,9},{9,10},{10,11},{11... | collective-permute-start | bytes 565256 | tf_op jit(solution)/shard_map/ppermute | solution.py:434
  8.3 0.8 copy-done.8
  9.2 0.8 copy-done.9
  10.0 0.8 copy-done.10
  10.9 0.7 copy-done.11
  11.6 3.1 %network_first.1 = (f32[46,8,128]{2,1,0:T(8,128)S(1)}, f32[12,32,128]{2,1,0:T(8,128)S(1)}, f32[8,128]{1,0:T(8,128)S(1)}, bf16[48,128]{1,0:T(8,128)(2,1)S(1)}, bf...) custom-call(f32[46,8,128]{2,1,0:T(8,128)S(1)} %last_rows.1.last_hbm,, ...), custom_call_target="tpu_custom_call" | custom-call | flops 2400000000 | bytes 8000 | tf_op jit(solution)/shard_map/network_first/pallas_call | solution.py:163
  14.7 1.3 %collective-permute-start.1 = (f32[46,8,128]{2,1,0:T(8,128)S(1)}, f32[46,8,128]{2,1,0:T(8,128)S(1)}, u32[]{:S(2)}, u32[]{:S(2)}) collective-permute-start(f32[46,8,128]{2,1,0:T(8,128)S(1)} %get-tuple-element.72), channel_id=1, source_target_pairs={{1,0},{2,1},{3,2},{4,3},{5,4},{6,5},{7,6},{9,8},{10,9},{11,10},{12... | collective-permute-start | bytes 565256 | tf_op jit(solution)/shard_map/ppermute | solution.py:434
  16.0 5.0 %collective-permute-done.1.down_ref = f32[46,8,128]{2,1,0:T(8,128)S(1)} collective-permute-done((f32[46,8,128]{2,1,0:T(8,128)S(1)}, f32[46,8,128]{2,1,0:T(8,128)S(1)}, u32[]{:S(2)}, u32[]{:S(2)}) %collective-permute-start.1) | collective-permute-done | bytes 188448 | tf_op jit(solution)/shard_map/ppermute | solution.py:434
  21.4 7.1 %collective-permute-start.2 = (f32[3,48,128]{2,1,0:T(8,128)S(1)}, f32[3,48,128]{2,1,0:T(8,128)S(1)}, u32[]{:S(2)}, u32[]{:S(2)}) collective-permute-start(f32[3,48,128]{2,1,0:T(8,128)S(1)} %right_columns.1), channel_id=1, source_target_pairs={{0,8},{8,16},{16,24},{24,32},{32,40},{40,48},{48,56},{56,64},{64,7... | collective-permute-start | bytes 221192 | tf_op jit(solution)/shard_map/ppermute | solution.py:434
  28.4 2.7 %network_left.1 = (f32[3,48,128]{2,1,0:T(8,128)S(1)}, f32[8,1,128]{2,1,0:T(1,128)S(1)}, bf16[8,128,48]{2,1,0:T(8,128)(2,1)S(1)}, bf16[8,128,256]{2,1,0:T(8,128)(...) custom-call(f32[46,8,128]{2,1,0:T(8,128)S(1)} %collective-permute-do, ...), custom_call_target="tpu_custom_call" | custom-call | flops 2400000000 | bytes 8000 | tf_op jit(solution)/shard_map/network_left/pallas_call | solution.py:242
  31.1 2.1 %collective-permute-start.3 = (f32[3,48,128]{2,1,0:T(8,128)S(1)}, f32[3,48,128]{2,1,0:T(8,128)S(1)}, u32[]{:S(2)}, u32[]{:S(2)}) collective-permute-start(f32[3,48,128]{2,1,0:T(8,128)S(1)} %get-tuple-element.83), channel_id=1, source_target_pairs={{0,504},{8,0},{16,8},{24,16},{32,24},{40,32},{48,40},{56,48},{64,5... | collective-permute-start | bytes 221192 | tf_op jit(solution)/shard_map/ppermute | solution.py:434
  33.3 2.3 %network.2 = (f32[8,1,128]{2,1,0:T(1,128)S(1)}, bf16[8,128,48]{2,1,0:T(8,128)(2,1)S(1)}, bf16[8,128,256]{2,1,0:T(8,128)(2,1)S(1)}, bf16[8,128,256]{2,1,0:T(8,128...) custom-call(f32[46,8,128]{2,1,0:T(8,128)S(1)} %collective-permute-do, ...), custom_call_target="tpu_custom_call" | custom-call | flops 2400000000 | bytes 8000 | tf_op jit(solution)/shard_map/network/pallas_call | solution.py:182
  35.6 2.3 %network.3 = (f32[8,1,128]{2,1,0:T(1,128)S(1)}, bf16[8,128,48]{2,1,0:T(8,128)(2,1)S(1)}, bf16[8,128,256]{2,1,0:T(8,128)(2,1)S(1)}, bf16[8,128,256]{2,1,0:T(8,128...) custom-call(f32[3,48,128]{2,1,0:T(8,128)S(1)} %collective-permute-do, ...), custom_call_target="tpu_custom_call" | custom-call | flops 2400000000 | bytes 8000 | tf_op jit(solution)/shard_map/network/pallas_call | solution.py:182
  38.3 7.3 %final.1 = (f32[6,32,128]{2,1,0:T(8,128)}, f32[32,128]{1,0:T(8,128)}, f32[512,128]{1,0:T(8,128)S(1)}) custom-call(f32[46,8,128]{2,1,0:T(8,128)S(1)} %collective-permute-done.up_ref.token, f32[36,32,128]{2,1,0:T(8,128)S(1)} %bitcast.20, f32[4,32,128]{2,1,0:T(8,128)S(1)} %copy-done.5, f32[6,32,128]{2,1,0:T(8,128)S(1)} %copy-done.3, ...), custom_call_target="tpu_custom_call" | custom-call | tf_op jit(solution)/shard_map/final/pallas_call | solution.py:385
  45.6 21.5 %all_to_all.15 = f32[32,16,128]{2,1,0:T(8,128)S(1)} all-to-all(f32[32,16,128]{2,1,0:T(8,128)S(1)} %bitcast.21), channel_id=1, replica_groups=mesh['z'=16,'xh'=2,'c'=2,'y'=4,'xl'=2] {'xh','c','y','xl'}, dimensions={0} | all-to-all | bytes 524288 | tf_op jit(solution)/shard_map/all_to_all | solution.py:440
  67.1 22.6 %all_to_all.16 = f32[16,16,128]{2,1,0:T(8,128)S(1)} all-to-all(f32[16,16,128]{2,1,0:T(8,128)S(1)} %broadcast_in_dim.4), channel_id=1, replica_groups=mesh['z'=16,'xh'=2,'c'=2,'y'=4,'xl'=2] {'z'}, dimensions={0} | all-to-all | bytes 262144 | tf_op jit(solution)/shard_map/all_to_all | solution.py:442
  89.8 0.7 broadcast_in_dim.5
  90.5 6.8 %all-to-all-start.2 = ((f32[32,16,128]{2,1,0:T(8,128)}), f32[32,16,128]{2,1,0:T(8,128)S(1)}, u32[]{:S(2)}, u32[]{:S(2)}) async-start(f32[32,16,128]{2,1,0:T(8,128)} %broadcast_in_dim.5), calls=%async_computation.2 | async-start | bytes 524288 | tf_op jit(solution)/shard_map/all_to_all | solution.py:444
  97.9 8.2 %all-to-all-done.2 = f32[32,16,128]{2,1,0:T(8,128)S(1)} async-done(((f32[32,16,128]{2,1,0:T(8,128)}), f32[32,16,128]{2,1,0:T(8,128)S(1)}, u32[]{:S(2)}, u32[]{:S(2)}) %all-to-all-start.2) | async-done | bytes 262176 | tf_op jit(solution)/shard_map/all_to_all | solution.py:444
  106.1 0.7 copy-done.17
  106.9 1.7 %unpack.1 = (f32[128,128]{1,0:T(8,128)}, f32[128,128]{1,0:T(8,128)}, f32[128,128]{1,0:T(8,128)}, f32[12,128]{1,0:T(8,128)}, f32[1,128]{1,0:T(1,128)}, /*index=5*...) custom-call(f32[512,128]{1,0:T(8,128)} %bitcast.28), custom_call_target="tpu_custom_call" | custom-call | tf_op jit(solution)/shard_map/unpack/pallas_call | solution.py:423
  (37 shorter events, 2.1 us)
Async XLA Ops:
  0.6 1.1 copy-start
  1.7 0.9 copy-start.2
  2.6 0.8 copy-start.4
  3.4 4.2 %copy-start.1 = (f32[6,6,32,128]{3,2,1,0:T(8,128)S(1)}, f32[6,6,32,128]{3,2,1,0:T(8,128)}, u32[]{:S(2)}) copy-start(f32[6,6,32,128]{3,2,1,0:T(8,128)} %param.15) | copy-start | bytes 1769476
  3.4 4.2 %copy-start.3 = (f32[6,32,128]{2,1,0:T(8,128)S(1)}, f32[6,32,128]{2,1,0:T(8,128)}, u32[]{:S(2)}) copy-start(f32[6,32,128]{2,1,0:T(8,128)} %mis_ref.5) | copy-start | bytes 294916
  3.4 4.3 %copy-start.5 = (f32[4,32,128]{2,1,0:T(8,128)S(1)}, f32[4,32,128]{2,1,0:T(8,128)}, u32[]{:S(2)}) copy-start(f32[4,32,128]{2,1,0:T(8,128)} %cpl_ref.5) | copy-start | bytes 196612
  3.5 4.3 %copy-start.7 = (f32[12,32,128]{2,1,0:T(8,128)S(1)}, f32[12,32,128]{2,1,0:T(8,128)}, u32[]{:S(2)}) copy-start(f32[12,32,128]{2,1,0:T(8,128)} %x_hbm.1) | copy-start | bytes 589828
  3.5 12.5 %collective-permute-start = (f32[46,8,128]{2,1,0:T(8,128)S(1)}, f32[46,8,128]{2,1,0:T(8,128)S(1)}, u32[]{:S(2)}, u32[]{:S(2)}) collective-permute-start(f32[46,8,128]{2,1,0:T(8,128)S(1)} %last_rows.1.last_hbm), channel_id=1, source_target_pairs={{0,1},{1,2},{2,3},{3,4},{4,5},{5,6},{6,7},{8,9},{9,10},{10,11},{11... | collective-permute-start | bytes 565256 | tf_op jit(solution)/shard_map/ppermute | solution.py:434
  7.6 0.7 copy-start.15
  7.6 0.7 copy-start.16
  7.6 0.7 copy-start.12
  7.7 0.7 copy-start.13
  7.7 0.7 copy-start.14
  8.3 0.8 copy-start.8
  9.2 0.8 copy-start.9
  10.0 0.8 copy-start.10
  10.9 0.7 copy-start.11
  14.7 6.3 %collective-permute-start.1 = (f32[46,8,128]{2,1,0:T(8,128)S(1)}, f32[46,8,128]{2,1,0:T(8,128)S(1)}, u32[]{:S(2)}, u32[]{:S(2)}) collective-permute-start(f32[46,8,128]{2,1,0:T(8,128)S(1)} %get-tuple-element.72), channel_id=1, source_target_pairs={{1,0},{2,1},{3,2},{4,3},{5,4},{6,5},{7,6},{9,8},{10,9},{11,10},{12... | collective-permute-start | bytes 565256 | tf_op jit(solution)/shard_map/ppermute | solution.py:434
  21.4 14.2 %collective-permute-start.2 = (f32[3,48,128]{2,1,0:T(8,128)S(1)}, f32[3,48,128]{2,1,0:T(8,128)S(1)}, u32[]{:S(2)}, u32[]{:S(2)}) collective-permute-start(f32[3,48,128]{2,1,0:T(8,128)S(1)} %right_columns.1), channel_id=1, source_target_pairs={{0,8},{8,16},{16,24},{24,32},{32,40},{40,48},{48,56},{56,64},{64,7... | collective-permute-start | bytes 221192 | tf_op jit(solution)/shard_map/ppermute | solution.py:434
  31.1 7.2 %collective-permute-start.3 = (f32[3,48,128]{2,1,0:T(8,128)S(1)}, f32[3,48,128]{2,1,0:T(8,128)S(1)}, u32[]{:S(2)}, u32[]{:S(2)}) collective-permute-start(f32[3,48,128]{2,1,0:T(8,128)S(1)} %get-tuple-element.83), channel_id=1, source_target_pairs={{0,504},{8,0},{16,8},{24,16},{32,24},{40,32},{48,40},{56,48},{64,5... | collective-permute-start | bytes 221192 | tf_op jit(solution)/shard_map/ppermute | solution.py:434
  35.6 2.7 %copy-start.6 = (f32[6,32,128]{2,1,0:T(8,128)S(1)}, f32[6,32,128]{2,1,0:T(8,128)}, u32[]{:S(2)}) copy-start(f32[6,32,128]{2,1,0:T(8,128)} %prod_ref.1) | copy-start | bytes 294916
  90.5 15.6 %all-to-all-start.2 = ((f32[32,16,128]{2,1,0:T(8,128)}), f32[32,16,128]{2,1,0:T(8,128)S(1)}, u32[]{:S(2)}, u32[]{:S(2)}) async-start(f32[32,16,128]{2,1,0:T(8,128)} %broadcast_in_dim.5), calls=%async_computation.2 | async-start | bytes 524288 | tf_op jit(solution)/shard_map/all_to_all | solution.py:444
  106.1 0.7 copy-start.17

commit v3 on v2

--- a/solution.py
+++ b/solution.py
@@ -113,28 +113,34 @@
     return moves
 
 
-def last_kernel(inv_hbm, cpl_hbm, mis_hbm, out_hbm, sem):
+def pinned(*values):
+    return [pltpu.with_memory_space_constraint(value, pltpu.MemorySpace.HBM) for value in values]
+
+
+def edge_kernel(inv_hbm, cpl_hbm, mis_hbm, last, initial, sem):
     rows = mis_hbm.shape[1]
-    for move in strips((inv_hbm, cpl_hbm, mis_hbm), out_hbm, rows - 8, sem):
+    fields = (inv_hbm, cpl_hbm, mis_hbm)
+    moves = strips(fields, last, rows - 8, sem.at[0]) + strips(fields, initial, 0, sem.at[1])
+    for move in moves:
         move.wait()
 
 
-def last_call(inv, cpl, mis):
-    return pl.pallas_call(
-        last_kernel,
+def edge_call(inv, cpl, mis):
+    return pl.pallas_call(
+        edge_kernel,
         in_specs=[HBM] * 3,
-        out_specs=ANY,
-        out_shape=jax.ShapeDtypeStruct((46, 8, 128), F32),
-        scratch_shapes=[pltpu.SemaphoreType.DMA((3,))],
+        out_specs=[ANY] * 2,
+        out_shape=[jax.ShapeDtypeStruct((46, 8, 128), F32)] * 2,
+        scratch_shapes=[pltpu.SemaphoreType.DMA((2, 3))],
         compiler_params=pltpu.CompilerParams(vmem_limit_bytes=MIB),
-        name="last_rows",
-    )(inv, cpl, mis)
-
-
-def opening_kernel(base, count, last_hbm, inv_hbm, cpl_hbm, mis_hbm, x_hbm, win_hbm, w2_hbm, w3_hbm, w4_hbm, *rest):
+        name="edge_rows",
+    )(*pinned(inv, cpl, mis))
+
+
+def opening_kernel(base, count, last_hbm, first_hbm, x_hbm, win_hbm, w2_hbm, w3_hbm, w4_hbm, *rest):
     vectors, rest = rest[:5], rest[5:]
-    strip, x_ref, vec, prepared, outs = rest[0], rest[1], rest[2], rest[3:11], rest[11:20]
-    win_ref, w2_ref, w3_ref, w4_ref, sem, strip_sem = rest[20:]
+    x_ref, vec, prepared, outs = rest[0], rest[1], rest[2:10], rest[10:19]
+    win_ref, w2_ref, w3_ref, w4_ref, sem = rest[19:]
     moves = [
         pltpu.make_async_copy(source, target, sem.at[i])
         for i, (source, target) in enumerate(
@@ -143,7 +149,6 @@
     ]
     for move in moves:
         move.start()
-    held = strips((inv_hbm, cpl_hbm, mis_hbm), strip, 0, strip_sem)
     s1, f2, f3, f4, b2, b3, b4, wt = prepared
     for move in moves:
         move.wait()
@@ -155,23 +160,21 @@
         back[...] = stacked(raw[...])
     wt[...] = jnp.broadcast_to(vec[4:5], (128, 128)).T
     network_rows(x_ref, base, count, prepared, vec, outs)
-    for move in held:
-        move.wait()
-
-
-def opening_call(base, count, last, inv, cpl, mis, x, win, w2, w3, w4, vectors):
+
+
+def opening_call(base, count, last, initial, x, win, w2, w3, w4, vectors):
     return pl.pallas_call(
         functools.partial(opening_kernel, base, count),
-        in_specs=[ANY] + [HBM] * 13,
-        out_specs=[ANY] + [VMEM] * 19,
-        out_shape=[jax.ShapeDtypeStruct((46, 8, 128), F32), jax.ShapeDtypeStruct(x.shape, F32),
+        in_specs=[ANY] * 2 + [HBM] * 10,
+        out_specs=[VMEM] * 19,
+        out_shape=[jax.ShapeDtypeStruct(x.shape, F32),
                    jax.ShapeDtypeStruct((8, 128), F32)] + PREPARED + network_shapes(count),
         scratch_shapes=[pltpu.VMEM((12, 128), F32)] + [pltpu.VMEM((128, 128), F32)] * 3
-        + [pltpu.SemaphoreType.DMA((10,)), pltpu.SemaphoreType.DMA((3,))],
+        + [pltpu.SemaphoreType.DMA((10,))],
         compiler_params=pltpu.CompilerParams(vmem_limit_bytes=LIMIT),
         cost_estimate=cost(count),
         name="network_first",
-    )(last, inv, cpl, mis, x, win, w2, w3, w4, *vectors)
+    )(last, initial, *pinned(x, win, w2, w3, w4, *vectors))
 
 
 def middle_kernel(base, count, token, x_ref, *rest):
@@ -216,20 +219,20 @@
     return cpl_ref[a - 36, at] if a < 40 else mis_ref[a - 40, at]
 
 
-def right_kernel(up_ref, inv_ref, cpl_ref, mis_ref, down_ref, out_ref):
+def right_kernel(up_ref, inv_ref, cpl_ref, mis_ref, down_ref, token, out_ref):
     packed(up_ref, inv_ref, cpl_ref, mis_ref, down_ref, out_ref, 120)
 
 
-def right_call(up, inv, cpl, mis, down):
+def right_call(up, inv, cpl, mis, down, token):
     rows = mis.shape[1]
     return pl.pallas_call(
         right_kernel,
-        in_specs=[VMEM] * 5,
+        in_specs=[VMEM] * 5 + [ANY],
         out_specs=VMEM,
         out_shape=jax.ShapeDtypeStruct((3, rows + 16, 128), F32),
         compiler_params=pltpu.CompilerParams(vmem_limit_bytes=LIMIT),
         name="right_columns",
-    )(up, inv, cpl, mis, down)
+    )(up, inv, cpl, mis, down, token)
 
 
 def third_kernel(base, count, up_ref, inv_ref, cpl_ref, mis_ref, down_ref, x_ref, *rest):
@@ -251,8 +254,8 @@
 
 
 def final_kernel(up_ref, inv_ref, cpl_ref, mis_ref, down_ref, prod_ref, froml_ref, fromr_ref, wt, *rest):
-    parts = [rest[8 * p : 8 * p + 8] for p in range(PARTS)]
-    adj_ref, sens_ref, sums_ref, ext, main, side, acc4, acc3, acc2, acc1, flat = rest[8 * PARTS :]
+    parts = [rest[9 * p : 9 * p + 9] for p in range(PARTS)]
+    adj_ref, sens_ref, corr_ref, sums_ref, ext, main, side, acc4, acc3, acc2, acc1, flat = rest[9 * PARTS :]
     rows = mis_ref.shape[1]
     tiles = rows // 8 + 2
     lane = lax.broadcasted_iota(jnp.int32, (8, 128), 1)
@@ -343,10 +346,12 @@
 
     base = 0
     for part in parts:
-        xc, l1, l2, l3, l4t, d3t, d2t, d1t = part
+        corr, l1 = part[0], part[2]
+        for r in range(corr.shape[0]):
+            corr_ref[base + r : base + r + 1] = corr[r]
 
         def gather(g, carry, base=base, part=part):
-            xc, l1, l2, l3, l4t, d3t, d2t, d1t = part
+            _, xc, l1, l2, l3, l4t, d3t, d2t, d1t = part
             at = WIDE * g
             some = pl.ds(at, WIDE)
             weights = [sens_ref[pl.ds(base + at + r, 1), :] for r in range(WIDE)]
@@ -385,9 +390,10 @@
     return pl.pallas_call(
         final_kernel,
         in_specs=[VMEM] * (9 + len(flat)),
-        out_specs=[VMEM] * 3,
+        out_specs=[VMEM] * 4,
         out_shape=[
             jax.ShapeDtypeStruct((6, rows, 128), F32),
+            jax.ShapeDtypeStruct((rows, 128), F32),
             jax.ShapeDtypeStruct((rows, 128), F32),
             jax.ShapeDtypeStruct((512, 128), F32),
         ],
@@ -424,6 +430,7 @@
         unpack_kernel,
         in_specs=[VMEM],
         out_shape=[jax.ShapeDtypeStruct(shape, F32) for shape in shapes],
+        compiler_params=pltpu.CompilerParams(vmem_limit_bytes=2 * MIB),
         name="unpack",
     )(sums)
 
@@ -453,15 +460,15 @@
     vectors = [v.reshape(1, 128) for v in (bias_in, bias_two, bias_three, bias_four, weight_out)]
     count = rows // PARTS
 
-    last = last_call(inverse, couplings, mismatch)
+    last, initial = edge_call(inverse, couplings, mismatch)
     above = sent(last, SUB, False, 1)
-    initial, features, vectors, *rest = opening_call(
-        0, count, last, inverse, couplings, mismatch, features, win, weight_two, weight_three, weight_four, vectors)
+    below = sent(initial, SUB, False, -1)
+    features, vectors, *rest = opening_call(
+        0, count, last, initial, features, win, weight_two, weight_three, weight_four, vectors)
     prepared, first = rest[:8], rest[8:]
-    below = sent(initial, SUB, False, -1)
-    second = middle_call(count, count, above, features, prepared, vectors)
-
-    right = right_call(above, inverse, couplings, mismatch, below)
+    second = middle_call(count, count, first[0], features, prepared, vectors)
+
+    right = right_call(above, inverse, couplings, mismatch, below, second[0])
     from_low = sent(right, BLK, True, 1)
     left, *third = third_call(2 * count, count, above, inverse, couplings, mismatch, below, features,
                               prepared, vectors)
@@ -469,13 +476,12 @@
     fourth = middle_call(3 * count, count, from_low, features, prepared, vectors)
 
     parts = (first, second, third, fourth)
-    correction = jnp.concatenate([part[0] for part in parts], axis=0)
-    adjoint, sensitivity, sums = final_call(
+    adjoint, sensitivity, correction, sums = final_call(
         above, inverse, couplings, mismatch, below, production, from_low, from_high, prepared[7],
-        [part[1:] for part in parts])
+        parts)
     g4, g3, g2, gin, b1, b2, b3, b4, gout = unpack_call(summed(sums))
     flat = lambda value: value.reshape(128)
-    return (adjoint, sensitivity, correction.reshape(rows, cols), gin.T, flat(b1), g2, flat(b2),
+    return (adjoint, sensitivity, correction, gin.T, flat(b1), g2, flat(b2),
             g3, flat(b3), g4, flat(b4), flat(gout))
 
 

time: 109 us -> 98.2 us (0.901)
  blocking collectives: 44.1 us -> 57.5 us
  waiting for transfers between devices: 13.5 us -> 3.91 us
  local copies, waits for them, and re-layouts: 8.12 us -> 0.05 us
  starting transfers between devices: 21.4 us -> 14.4 us
  Pallas kernels: 20 us -> 21.1 us
    all_to_all x0 -> x1, blocking collectives: none -> 15.1 us  [summed(): lax.all_to_all(jnp.broadcast_to(part[None], (near, rows, 128)), NEAR, 0, 0)]
    all_to_all x1 -> x0, waiting for transfers between devices: 8.2 us -> none  [summed(): lax.all_to_all(jnp.broadcast_to(part[None], (near, rows, 128)), NEAR, 0, 0)]
    unnamed x36 -> x8, local copies, waits for them, and re-layouts: 7.38 us -> 0.03 us
    all_to_all x1 -> x0, starting transfers between devices: 6.8 us -> none  [summed(): lax.all_to_all(jnp.broadcast_to(part[None], (near, rows, 128)), NEAR, 0, 0)]
    all_to_all x1, blocking collectives: 21.5 us -> 18.2 us  [summed(): part = lax.all_to_all(value.reshape(near, rows, 128), NEAR, 0, 0)]
    all_to_all x1, blocking collectives: 22.6 us -> 24.2 us  [summed(): lax.all_to_all(jnp.broadcast_to(part[None], (far, rows, 128)), FAR, 0, 0)]
    ppermute x4, waiting for transfers between devices: 5.33 us -> 3.91 us  [sent(): return lax.ppermute(value, axes, pairs)]
  transfers between devices with their start and end apart: 5 -> 4, of which waited for: 3 -> 2; matrix products, arithmetic and copies ran while one was open for 1% -> 0% of each run, Pallas kernels for 10% -> 11%
where the time goes in v3:
time: 98.2 us; the launch traced here: 97.9 us
  blocking collectives  57.5 us (59%)
  Pallas kernels  21.1 us (21%)
  starting transfers between devices  14.4 us (15%)
  waiting for transfers between devices  3.91 us (4%)
    all_to_all x1, blocking collectives, summed(): lax.all_to_all(jnp.broadcast_to(part[None], (far, rows, 128)), FAR, 0, 0)  24.2 us
    all_to_all x1, blocking collectives, summed(): part = lax.all_to_all(value.reshape(near, rows, 128), NEAR, 0, 0)  18.2 us
    all_to_all x1, blocking collectives, summed(): lax.all_to_all(jnp.broadcast_to(part[None], (near, rows, 128)), NEAR, 0, 0)  15.1 us
    ppermute x4, starting transfers between devices, sent(): return lax.ppermute(value, axes, pairs)  14.4 us
    pallas_call x1, Pallas kernels, final_call(): pl.pallas_call(final_kernel, in_specs=[VMEM] * (9 + len(flat)), out_specs...  7.91 us
    pallas_call x2, Pallas kernels, middle_call(): pl.pallas_call(functools.partial(middle_kernel, base, count), in_specs=[A...  4.68 us
    ppermute x4, waiting for transfers between devices, sent(): return lax.ppermute(value, axes, pairs)  3.91 us
    pallas_call x1, Pallas kernels, opening_call(): pl.pallas_call(functools.partial(opening_kernel, base, count), in_specs=[...  3.68 us
  transfers between devices with their start and end apart: 4, of which 2 were waited for; matrix products, arithmetic and copies ran while one was open for 0% of the time, Pallas kernels for 11%

profile of v3, /device:TPU:1, one launch (start us, length us, event | category | flops | bytes accessed | tf_op | source)
XLA Modules:
  0.0 97.9 jit_solution(10837649077357702644)
XLA Ops:
  0.6 1.1 %edge_rows.1 = (f32[46,8,128]{2,1,0:T(8,128)S(1)}, f32[46,8,128]{2,1,0:T(8,128)S(1)}) custom-call(f32[36,32,128]{2,1,0:T(8,128)} %bitcast.15, f32[4,32,128]{2,1,0:T(8,128)} %cpl_ref.5, f32[6,32,128]{2,1,0:T(8,128)} %mis_ref.5), custom_call_target="tpu_custom_call" | custom-call | tf_op jit(solution)/shard_map/edge_rows/pallas_call | solution.py:129
  1.7 4.0 %collective-permute-start = (f32[46,8,128]{2,1,0:T(8,128)S(1)}, f32[46,8,128]{2,1,0:T(8,128)S(1)}, u32[]{:S(2)}, u32[]{:S(2)}) collective-permute-start(f32[46,8,128]{2,1,0:T(8,128)S(1)} %get-tuple-element.74.last_hbm), channel_id=1, source_target_pairs={{0,1},{1,2},{2,3},{3,4},{4,5},{5,6},{6,7},{8,9},{9,10},{10,11},{11... | collective-permute-start | bytes 565256 | tf_op jit(solution)/shard_map/ppermute | solution.py:441
  5.7 1.3 %collective-permute-start.1 = (f32[46,8,128]{2,1,0:T(8,128)S(1)}, f32[46,8,128]{2,1,0:T(8,128)S(1)}, u32[]{:S(2)}, u32[]{:S(2)}) collective-permute-start(f32[46,8,128]{2,1,0:T(8,128)S(1)} %get-tuple-element.75.first_hbm), channel_id=1, source_target_pairs={{1,0},{2,1},{3,2},{4,3},{5,4},{6,5},{7,6},{9,8},{10,9},{11,10},{12... | collective-permute-start | bytes 565256 | tf_op jit(solution)/shard_map/ppermute | solution.py:441
  7.0 3.7 %network_first.1 = (f32[12,32,128]{2,1,0:T(8,128)S(1)}, f32[8,128]{1,0:T(8,128)S(1)}, bf16[48,128]{1,0:T(8,128)(2,1)S(1)}, bf16[256,256]{1,0:T(8,128)(2,1)S(1)},...) custom-call(f32[46,8,128]{2,1,0:T(8,128)S(1)} %get-tuple-element.74., ...), custom_call_target="tpu_custom_call" | custom-call | flops 2400000000 | bytes 8000 | tf_op jit(solution)/shard_map/network_first/pallas_call | solution.py:166
  10.7 0.0 copy-start
  10.7 0.0 copy-start.1
  10.7 0.0 copy-start.2
  10.7 2.3 %network.2 = (f32[8,1,128]{2,1,0:T(1,128)S(1)}, bf16[8,128,48]{2,1,0:T(8,128)(2,1)S(1)}, bf16[8,128,256]{2,1,0:T(8,128)(2,1)S(1)}, bf16[8,128,256]{2,1,0:T(8,128...) custom-call(f32[8,1,128]{2,1,0:T(1,128)S(1)} %get-tuple-element.76.t, ...), custom_call_target="tpu_custom_call" | custom-call | flops 2400000000 | bytes 8000 | tf_op jit(solution)/shard_map/network/pallas_call | solution.py:185
  13.1 0.0 collective-permute-done.up_ref
  13.1 0.9 collective-permute-done.1.down_ref
  13.9 0.0 copy-done.1
  13.9 0.3 right_columns.1
  14.3 7.2 %collective-permute-start.2 = (f32[3,48,128]{2,1,0:T(8,128)S(1)}, f32[3,48,128]{2,1,0:T(8,128)S(1)}, u32[]{:S(2)}, u32[]{:S(2)}) collective-permute-start(f32[3,48,128]{2,1,0:T(8,128)S(1)} %right_columns.1), channel_id=1, source_target_pairs={{0,8},{8,16},{16,24},{24,32},{32,40},{40,48},{48,56},{56,64},{64,7... | collective-permute-start | bytes 221192 | tf_op jit(solution)/shard_map/ppermute | solution.py:441
  21.5 2.7 %network_left.1 = (f32[3,48,128]{2,1,0:T(8,128)S(1)}, f32[8,1,128]{2,1,0:T(1,128)S(1)}, bf16[8,128,48]{2,1,0:T(8,128)(2,1)S(1)}, bf16[8,128,256]{2,1,0:T(8,128)(...) custom-call(f32[46,8,128]{2,1,0:T(8,128)S(1)} %collective-permute-do, ...), custom_call_target="tpu_custom_call" | custom-call | flops 2400000000 | bytes 8000 | tf_op jit(solution)/shard_map/network_left/pallas_call | solution.py:245
  24.2 1.9 %collective-permute-start.3 = (f32[3,48,128]{2,1,0:T(8,128)S(1)}, f32[3,48,128]{2,1,0:T(8,128)S(1)}, u32[]{:S(2)}, u32[]{:S(2)}) collective-permute-start(f32[3,48,128]{2,1,0:T(8,128)S(1)} %get-tuple-element.88), channel_id=1, source_target_pairs={{0,504},{8,0},{16,8},{24,16},{32,24},{40,32},{48,40},{56,48},{64,5... | collective-permute-start | bytes 221192 | tf_op jit(solution)/shard_map/ppermute | solution.py:441
  26.2 0.0 collective-permute-done.2.token.froml_ref
  26.2 0.0 copy-start.3
  26.2 2.3 %network.3 = (f32[8,1,128]{2,1,0:T(1,128)S(1)}, bf16[8,128,48]{2,1,0:T(8,128)(2,1)S(1)}, bf16[8,128,256]{2,1,0:T(8,128)(2,1)S(1)}, bf16[8,128,256]{2,1,0:T(8,128...) custom-call(f32[3,48,128]{2,1,0:T(8,128)S(1)} %collective-permute-do, ...), custom_call_target="tpu_custom_call" | custom-call | flops 2400000000 | bytes 8000 | tf_op jit(solution)/shard_map/network/pallas_call | solution.py:185
  28.5 3.0 %collective-permute-done.3.fromr_ref = f32[3,48,128]{2,1,0:T(8,128)S(1)} collective-permute-done((f32[3,48,128]{2,1,0:T(8,128)S(1)}, f32[3,48,128]{2,1,0:T(8,128)S(1)}, u32[]{:S(2)}, u32[]{:S(2)}) %collective-permute-start.3) | collective-permute-done | bytes 73760 | tf_op jit(solution)/shard_map/ppermute | solution.py:441
  31.6 7.9 %final.1 = (f32[6,32,128]{2,1,0:T(8,128)}, f32[32,128]{1,0:T(8,128)}, f32[32,128]{1,0:T(8,128)}, f32[512,128]{1,0:T(8,128)S(1)}) custom-call(f32[46,8,128]{2,1,0:T(8,128)S(1)} %collective-permute-done.up_ref, f32[36,32,128]{2,1,0:T(8,128)S(1)} %bitcast.18, f32[4,32,128]{2,1,0:T(8,128)S(1)} %copy-done.2, f32[6,32,128]{2,1,0:T(8,128)S(1)} %copy-done.1, ...), custom_call_target="tpu_custom_call" | custom-call | tf_op jit(solution)/shard_map/final/pallas_call | solution.py:390
  39.5 18.2 %all_to_all.15 = f32[32,16,128]{2,1,0:T(8,128)S(1)} all-to-all(f32[32,16,128]{2,1,0:T(8,128)S(1)} %bitcast.20), channel_id=1, replica_groups=mesh['z'=16,'xh'=2,'c'=2,'y'=4,'xl'=2] {'xh','c','y','xl'}, dimensions={0} | all-to-all | bytes 524288 | tf_op jit(solution)/shard_map/all_to_all | solution.py:447
  57.7 24.2 %all_to_all.16 = f32[16,16,128]{2,1,0:T(8,128)S(1)} all-to-all(f32[16,16,128]{2,1,0:T(8,128)S(1)} %broadcast_in_dim.4), channel_id=1, replica_groups=mesh['z'=16,'xh'=2,'c'=2,'y'=4,'xl'=2] {'z'}, dimensions={0} | all-to-all | bytes 262144 | tf_op jit(solution)/shard_map/all_to_all | solution.py:449
  82.0 15.1 %all_to_all.17 = f32[32,16,128]{2,1,0:T(8,128)S(1)} all-to-all(f32[32,16,128]{2,1,0:T(8,128)S(1)} %broadcast_in_dim.5), channel_id=1, replica_groups=mesh['z'=16,'xh'=2,'c'=2,'y'=4,'xl'=2] {'xh','c','y','xl'}, dimensions={0} | all-to-all | bytes 524288 | tf_op jit(solution)/shard_map/all_to_all | solution.py:451
  97.1 0.8 unpack.1
  (7 shorter events, 0.1 us)
Async XLA Ops:
  1.7 11.3 %collective-permute-start = (f32[46,8,128]{2,1,0:T(8,128)S(1)}, f32[46,8,128]{2,1,0:T(8,128)S(1)}, u32[]{:S(2)}, u32[]{:S(2)}) collective-permute-start(f32[46,8,128]{2,1,0:T(8,128)S(1)} %get-tuple-element.74.last_hbm), channel_id=1, source_target_pairs={{0,1},{1,2},{2,3},{3,4},{4,5},{5,6},{6,7},{8,9},{9,10},{10,11},{11... | collective-permute-start | bytes 565256 | tf_op jit(solution)/shard_map/ppermute | solution.py:441
  5.7 8.2 %collective-permute-start.1 = (f32[46,8,128]{2,1,0:T(8,128)S(1)}, f32[46,8,128]{2,1,0:T(8,128)S(1)}, u32[]{:S(2)}, u32[]{:S(2)}) collective-permute-start(f32[46,8,128]{2,1,0:T(8,128)S(1)} %get-tuple-element.75.first_hbm), channel_id=1, source_target_pairs={{1,0},{2,1},{3,2},{4,3},{5,4},{6,5},{7,6},{9,8},{10,9},{11,10},{12... | collective-permute-start | bytes 565256 | tf_op jit(solution)/shard_map/ppermute | solution.py:441
  10.7 3.3 %copy-start = (f32[6,6,32,128]{3,2,1,0:T(8,128)S(1)}, f32[6,6,32,128]{3,2,1,0:T(8,128)}, u32[]{:S(2)}) copy-start(f32[6,6,32,128]{3,2,1,0:T(8,128)} %param.15) | copy-start | bytes 1769476
  10.7 3.2 %copy-start.1 = (f32[6,32,128]{2,1,0:T(8,128)S(1)}, f32[6,32,128]{2,1,0:T(8,128)}, u32[]{:S(2)}) copy-start(f32[6,32,128]{2,1,0:T(8,128)} %mis_ref.5) | copy-start | bytes 294916
  10.7 3.2 %copy-start.2 = (f32[4,32,128]{2,1,0:T(8,128)S(1)}, f32[4,32,128]{2,1,0:T(8,128)}, u32[]{:S(2)}) copy-start(f32[4,32,128]{2,1,0:T(8,128)} %cpl_ref.5) | copy-start | bytes 196612
  14.3 11.9 %collective-permute-start.2 = (f32[3,48,128]{2,1,0:T(8,128)S(1)}, f32[3,48,128]{2,1,0:T(8,128)S(1)}, u32[]{:S(2)}, u32[]{:S(2)}) collective-permute-start(f32[3,48,128]{2,1,0:T(8,128)S(1)} %right_columns.1), channel_id=1, source_target_pairs={{0,8},{8,16},{16,24},{24,32},{32,40},{40,48},{48,56},{56,64},{64,7... | collective-permute-start | bytes 221192 | tf_op jit(solution)/shard_map/ppermute | solution.py:441
  24.2 7.3 %collective-permute-start.3 = (f32[3,48,128]{2,1,0:T(8,128)S(1)}, f32[3,48,128]{2,1,0:T(8,128)S(1)}, u32[]{:S(2)}, u32[]{:S(2)}) collective-permute-start(f32[3,48,128]{2,1,0:T(8,128)S(1)} %get-tuple-element.88), channel_id=1, source_target_pairs={{0,504},{8,0},{16,8},{24,16},{32,24},{40,32},{48,40},{56,48},{64,5... | collective-permute-start | bytes 221192 | tf_op jit(solution)/shard_map/ppermute | solution.py:441
  26.2 5.4 %copy-start.3 = (f32[6,32,128]{2,1,0:T(8,128)S(1)}, f32[6,32,128]{2,1,0:T(8,128)}, u32[]{:S(2)}) copy-start(f32[6,32,128]{2,1,0:T(8,128)} %prod_ref.1) | copy-start | bytes 294916

commit v4 on v3

--- a/solution.py
+++ b/solution.py
@@ -14,9 +14,9 @@
 FAR = ("z",)
 F32 = jnp.float32
 BF16 = jnp.bfloat16
-GROUP = 4
-WIDE = 4
-PARTS = 4
+GROUP = 8
+WIDE = 8
+PARTS = 3
 MIB = 1 << 20
 LIMIT = 8 * MIB
 
@@ -255,7 +255,8 @@
 
 def final_kernel(up_ref, inv_ref, cpl_ref, mis_ref, down_ref, prod_ref, froml_ref, fromr_ref, wt, *rest):
     parts = [rest[9 * p : 9 * p + 9] for p in range(PARTS)]
-    adj_ref, sens_ref, corr_ref, sums_ref, ext, main, side, acc4, acc3, acc2, acc1, flat = rest[9 * PARTS :]
+    adj_ref, sens_ref, corr_ref, sums_ref, ext, *rest = rest[9 * PARTS :]
+    main, side, (acc4, acc3, acc2, acc1, flat) = rest[0:2], rest[2:4], rest[4:]
     rows = mis_ref.shape[1]
     tiles = rows // 8 + 2
     lane = lax.broadcasted_iota(jnp.int32, (8, 128), 1)
@@ -275,55 +276,59 @@
             ext[a, at] = jnp.where(lane < 8, high, jnp.where(lane >= 120, low, 0.0))
 
     edge = jnp.zeros((8, 128), F32)
-    for field in (main, side):
-        for s in range(2):
-            for i in range(6):
-                field[s, i, 0:8] = edge
-                field[s, i, pl.ds(8 * tiles + 8, 8)] = edge
-
-    def solve(field, s, t, coefficient, rhs):
+    for field in main + side:
+        for i in range(6):
+            field[i, 0:8] = edge
+            field[i, pl.ds(8 * tiles + 8, 8)] = edge
+
+    def solve(field, t, coefficient, rhs):
         for i in range(6):
             total = coefficient(6 * i) * rhs[0]
             for j in range(1, 6):
                 total = total + coefficient(6 * i + j) * rhs[j]
-            field[s, i, pl.ds(8 * t + 8, 8)] = total
+            field[i, pl.ds(8 * t + 8, 8)] = total
 
     for t in range(tiles):
         at = pl.ds(8 * t, 8)
-        solve(main, 0, t, lambda a: tile(a, t), [tile(40 + i, t) for i in range(6)])
-        solve(side, 0, t, lambda a: ext[a, at], [ext[40 + i, at] for i in range(6)])
-
-    def sweep(n, carry):
-        s = lax.rem(n, 2)
+        solve(main[0], t, lambda a: tile(a, t), [tile(40 + i, t) for i in range(6)])
+        solve(side[0], t, lambda a: ext[a, at], [ext[40 + i, at] for i in range(6)])
+
+    def sweep(main, side, main_next, side_next):
         for t in range(tiles):
             at = pl.ds(8 * t, 8)
             near, beside = [], []
             for i in range(6):
-                m = main[s, i, pl.ds(8 * t + 8, 8)]
-                e = side[s, i, pl.ds(8 * t + 8, 8)]
+                m = main[i, pl.ds(8 * t + 8, 8)]
+                e = side[i, pl.ds(8 * t + 8, 8)]
                 m_low, m_high = pltpu.roll(m, 1, 1), pltpu.roll(m, 127, 1)
                 e_low, e_high = pltpu.roll(e, 1, 1), pltpu.roll(e, 127, 1)
-                rhs = tile(40 + i, t) + tile(36, t) * main[s, i, pl.ds(8 * t + 7, 8)]
-                rhs = rhs + tile(37, t) * main[s, i, pl.ds(8 * t + 9, 8)]
+                rhs = tile(40 + i, t) + tile(36, t) * main[i, pl.ds(8 * t + 7, 8)]
+                rhs = rhs + tile(37, t) * main[i, pl.ds(8 * t + 9, 8)]
                 rhs = rhs + tile(38, t) * jnp.where(first, e_low, m_low)
                 near.append(rhs + tile(39, t) * jnp.where(last, e_high, m_high))
-                rhs = ext[40 + i, at] + ext[36, at] * side[s, i, pl.ds(8 * t + 7, 8)]
-                rhs = rhs + ext[37, at] * side[s, i, pl.ds(8 * t + 9, 8)]
+                rhs = ext[40 + i, at] + ext[36, at] * side[i, pl.ds(8 * t + 7, 8)]
+                rhs = rhs + ext[37, at] * side[i, pl.ds(8 * t + 9, 8)]
                 rhs = rhs + ext[38, at] * jnp.where(first, m_low, e_low)
                 beside.append(rhs + ext[39, at] * jnp.where(last, m_high, e_high))
-            solve(main, 1 - s, t, lambda a: tile(a, t), near)
-            solve(side, 1 - s, t, lambda a: ext[a, at], beside)
+            solve(main_next, t, lambda a: tile(a, t), near)
+            solve(side_next, t, lambda a: ext[a, at], beside)
+
+    def two(n, carry):
+        sweep(main[0], side[0], main[1], side[1])
+        sweep(main[1], side[1], main[0], side[0])
         return carry
 
-    lax.fori_loop(0, SWEEPS - 1, sweep, 0)
-    done = (SWEEPS - 1) % 2
+    lax.fori_loop(0, (SWEEPS - 1) // 2, two, 0)
+    if (SWEEPS - 1) % 2:
+        sweep(main[0], side[0], main[1], side[1])
+    done = main[(SWEEPS - 1) % 2]
 
     square = jnp.zeros((8, 128), F32)
     for t in range(rows // 8):
         at = pl.ds(8 * t, 8)
         total = jnp.zeros((8, 128), F32)
         for i in range(6):
-            value = main[done, i, pl.ds(8 * t + 16, 8)]
+            value = done[i, pl.ds(8 * t + 16, 8)]
             adj_ref[i, at] = value
             total = total + value * prod_ref[i, at]
         sens_ref[at] = -total
@@ -399,8 +404,10 @@
         ],
         scratch_shapes=[
             pltpu.VMEM((46, rows + 16, 128), F32),
-            pltpu.VMEM((2, 6, rows + 32, 128), F32),
-            pltpu.VMEM((2, 6, rows + 32, 128), F32),
+            pltpu.VMEM((6, rows + 32, 128), F32),
+            pltpu.VMEM((6, rows + 32, 128), F32),
+            pltpu.VMEM((6, rows + 32, 128), F32),
+            pltpu.VMEM((6, rows + 32, 128), F32),
             pltpu.VMEM((256, 256), F32),
             pltpu.VMEM((256, 256), F32),
             pltpu.VMEM((256, 256), F32),
@@ -458,24 +465,23 @@
     inverse = inverse_diag.reshape(nvars * nvars, rows, cols)
     win = weight_in.T
     vectors = [v.reshape(1, 128) for v in (bias_in, bias_two, bias_three, bias_four, weight_out)]
-    count = rows // PARTS
+    count = rows // 4
 
     last, initial = edge_call(inverse, couplings, mismatch)
     above = sent(last, SUB, False, 1)
     below = sent(initial, SUB, False, -1)
     features, vectors, *rest = opening_call(
-        0, count, last, initial, features, win, weight_two, weight_three, weight_four, vectors)
+        0, 2 * count, last, initial, features, win, weight_two, weight_three, weight_four, vectors)
     prepared, first = rest[:8], rest[8:]
-    second = middle_call(count, count, first[0], features, prepared, vectors)
-
-    right = right_call(above, inverse, couplings, mismatch, below, second[0])
+
+    right = right_call(above, inverse, couplings, mismatch, below, first[0])
     from_low = sent(right, BLK, True, 1)
-    left, *third = third_call(2 * count, count, above, inverse, couplings, mismatch, below, features,
+    left, *second = third_call(2 * count, count, above, inverse, couplings, mismatch, below, features,
                               prepared, vectors)
     from_high = sent(left, BLK, True, -1)
-    fourth = middle_call(3 * count, count, from_low, features, prepared, vectors)
-
-    parts = (first, second, third, fourth)
+    third = middle_call(3 * count, count, from_low, features, prepared, vectors)
+
+    parts = (first, second, third)
     adjoint, sensitivity, correction, sums = final_call(
         above, inverse, couplings, mismatch, below, production, from_low, from_high, prepared[7],
         parts)

time: 98.2 us -> 95.8 us (0.976)
  Pallas kernels: 21.1 us -> 15.9 us
  waiting for transfers between devices: 3.91 us -> 7.46 us
    ppermute x4, waiting for transfers between devices: 3.91 us -> 7.46 us  [sent(): return lax.ppermute(value, axes, pairs)]
    pallas_call x2 -> x1, Pallas kernels: 4.68 us -> 1.39 us  [middle_call(): pl.pallas_call(functools.partial(middle_kernel, base, count), in_specs=[A...]
    all_to_all x1, blocking collectives: 18.2 us -> 17 us  [summed(): part = lax.all_to_all(value.reshape(near, rows, 128), NEAR, 0, 0)]
    pallas_call x1, Pallas kernels: 2.68 us -> 1.46 us  [third_call(): pl.pallas_call(functools.partial(third_kernel, base, count), in_specs=[VM...]
    pallas_call x1, Pallas kernels: 7.91 us -> 6.75 us  [final_call(): pl.pallas_call(final_kernel, in_specs=[VMEM] * (9 + len(flat)), out_specs...]
  transfers between devices with their start and end apart: 4 -> 4, of which waited for: 2 -> 2; matrix products, arithmetic and copies ran while one was open for 0% -> 0% of each run, Pallas kernels for 11% -> 7%
where the time goes in v4:
time: 95.8 us; the launch traced here: 95.5 us
  blocking collectives  56.8 us (59%)
  Pallas kernels  15.9 us (17%)
  starting transfers between devices  14.4 us (15%)
  waiting for transfers between devices  7.46 us (8%)
    all_to_all x1, blocking collectives, summed(): lax.all_to_all(jnp.broadcast_to(part[None], (far, rows, 128)), FAR, 0, 0)  24.7 us
    all_to_all x1, blocking collectives, summed(): part = lax.all_to_all(value.reshape(near, rows, 128), NEAR, 0, 0)  17 us
    all_to_all x1, blocking collectives, summed(): lax.all_to_all(jnp.broadcast_to(part[None], (near, rows, 128)), NEAR, 0, 0)  15.1 us
    ppermute x4, starting transfers between devices, sent(): return lax.ppermute(value, axes, pairs)  14.4 us
    ppermute x4, waiting for transfers between devices, sent(): return lax.ppermute(value, axes, pairs)  7.46 us
    pallas_call x1, Pallas kernels, final_call(): pl.pallas_call(final_kernel, in_specs=[VMEM] * (9 + len(flat)), out_specs...  6.75 us
    pallas_call x1, Pallas kernels, opening_call(): pl.pallas_call(functools.partial(opening_kernel, base, count), in_specs=[...  4.16 us
  transfers between devices with their start and end apart: 4, of which 2 were waited for; matrix products, arithmetic and copies ran while one was open for 0% of the time, Pallas kernels for 7%

profile of v4, /device:TPU:1, one launch (start us, length us, event | category | flops | bytes accessed | tf_op | source)
XLA Modules:
  0.0 95.5 jit_solution(15673816002207690973)
XLA Ops:
  0.6 1.1 %edge_rows.1 = (f32[46,8,128]{2,1,0:T(8,128)S(1)}, f32[46,8,128]{2,1,0:T(8,128)S(1)}) custom-call(f32[36,32,128]{2,1,0:T(8,128)} %bitcast.15, f32[4,32,128]{2,1,0:T(8,128)} %cpl_ref.5, f32[6,32,128]{2,1,0:T(8,128)} %mis_ref.5), custom_call_target="tpu_custom_call" | custom-call | tf_op jit(solution)/shard_map/edge_rows/pallas_call | solution.py:129
  1.7 4.0 %collective-permute-start = (f32[46,8,128]{2,1,0:T(8,128)S(1)}, f32[46,8,128]{2,1,0:T(8,128)S(1)}, u32[]{:S(2)}, u32[]{:S(2)}) collective-permute-start(f32[46,8,128]{2,1,0:T(8,128)S(1)} %get-tuple-element.65.last_hbm), channel_id=1, source_target_pairs={{0,1},{1,2},{2,3},{3,4},{4,5},{5,6},{6,7},{8,9},{9,10},{10,11},{11... | collective-permute-start | bytes 565256 | tf_op jit(solution)/shard_map/ppermute | solution.py:448
  5.7 1.3 %collective-permute-start.1 = (f32[46,8,128]{2,1,0:T(8,128)S(1)}, f32[46,8,128]{2,1,0:T(8,128)S(1)}, u32[]{:S(2)}, u32[]{:S(2)}) collective-permute-start(f32[46,8,128]{2,1,0:T(8,128)S(1)} %get-tuple-element.66.first_hbm), channel_id=1, source_target_pairs={{1,0},{2,1},{3,2},{4,3},{5,4},{6,5},{7,6},{9,8},{10,9},{11,10},{12... | collective-permute-start | bytes 565256 | tf_op jit(solution)/shard_map/ppermute | solution.py:448
  7.0 0.0 copy-start
  7.0 0.0 copy-start.1
  7.0 0.0 copy-start.2
  7.0 4.2 %network_first.1 = (f32[12,32,128]{2,1,0:T(8,128)S(1)}, f32[8,128]{1,0:T(8,128)S(1)}, bf16[48,128]{1,0:T(8,128)(2,1)S(1)}, bf16[256,256]{1,0:T(8,128)(2,1)S(1)},...) custom-call(f32[46,8,128]{2,1,0:T(8,128)S(1)} %get-tuple-element.65., ...), custom_call_target="tpu_custom_call" | custom-call | flops 4800000000 | bytes 16000 | tf_op jit(solution)/shard_map/network_first/pallas_call | solution.py:166
  11.2 0.0 collective-permute-done.up_ref
  11.2 2.7 %collective-permute-done.1.down_ref = f32[46,8,128]{2,1,0:T(8,128)S(1)} collective-permute-done((f32[46,8,128]{2,1,0:T(8,128)S(1)}, f32[46,8,128]{2,1,0:T(8,128)S(1)}, u32[]{:S(2)}, u32[]{:S(2)}) %collective-permute-start.1) | collective-permute-done | bytes 188448 | tf_op jit(solution)/shard_map/ppermute | solution.py:448
  13.9 0.0 copy-done.1
  13.9 0.3 right_columns.1
  14.3 7.2 %collective-permute-start.2 = (f32[3,48,128]{2,1,0:T(8,128)S(1)}, f32[3,48,128]{2,1,0:T(8,128)S(1)}, u32[]{:S(2)}, u32[]{:S(2)}) collective-permute-start(f32[3,48,128]{2,1,0:T(8,128)S(1)} %right_columns.1), channel_id=1, source_target_pairs={{0,8},{8,16},{16,24},{24,32},{32,40},{40,48},{48,56},{56,64},{64,7... | collective-permute-start | bytes 221192 | tf_op jit(solution)/shard_map/ppermute | solution.py:448
  21.6 1.5 %network_left.1 = (f32[3,48,128]{2,1,0:T(8,128)S(1)}, f32[8,1,128]{2,1,0:T(1,128)S(1)}, bf16[8,128,48]{2,1,0:T(8,128)(2,1)S(1)}, bf16[8,128,256]{2,1,0:T(8,128)(...) custom-call(f32[46,8,128]{2,1,0:T(8,128)S(1)} %collective-permute-do, ...), custom_call_target="tpu_custom_call" | custom-call | flops 2400000000 | bytes 8000 | tf_op jit(solution)/shard_map/network_left/pallas_call | solution.py:245
  23.0 1.9 %collective-permute-start.3 = (f32[3,48,128]{2,1,0:T(8,128)S(1)}, f32[3,48,128]{2,1,0:T(8,128)S(1)}, u32[]{:S(2)}, u32[]{:S(2)}) collective-permute-start(f32[3,48,128]{2,1,0:T(8,128)S(1)} %get-tuple-element.78), channel_id=1, source_target_pairs={{0,504},{8,0},{16,8},{24,16},{32,24},{40,32},{48,40},{56,48},{64,5... | collective-permute-start | bytes 221192 | tf_op jit(solution)/shard_map/ppermute | solution.py:448
  24.9 0.0 collective-permute-done.2.token.froml_ref
  24.9 0.0 copy-start.3
  25.0 1.4 %network.1 = (f32[8,1,128]{2,1,0:T(1,128)S(1)}, bf16[8,128,48]{2,1,0:T(8,128)(2,1)S(1)}, bf16[8,128,256]{2,1,0:T(8,128)(2,1)S(1)}, bf16[8,128,256]{2,1,0:T(8,128...) custom-call(f32[3,48,128]{2,1,0:T(8,128)S(1)} %collective-permute-do, ...), custom_call_target="tpu_custom_call" | custom-call | flops 2400000000 | bytes 8000 | tf_op jit(solution)/shard_map/network/pallas_call | solution.py:185
  26.3 4.7 %collective-permute-done.3.fromr_ref = f32[3,48,128]{2,1,0:T(8,128)S(1)} collective-permute-done((f32[3,48,128]{2,1,0:T(8,128)S(1)}, f32[3,48,128]{2,1,0:T(8,128)S(1)}, u32[]{:S(2)}, u32[]{:S(2)}) %collective-permute-start.3) | collective-permute-done | bytes 73760 | tf_op jit(solution)/shard_map/ppermute | solution.py:448
  31.1 0.0 copy-done.3
  31.1 6.7 %final.1 = (f32[6,32,128]{2,1,0:T(8,128)}, f32[32,128]{1,0:T(8,128)}, f32[32,128]{1,0:T(8,128)}, f32[512,128]{1,0:T(8,128)S(1)}) custom-call(f32[46,8,128]{2,1,0:T(8,128)S(1)} %collective-permute-done.up_ref, f32[36,32,128]{2,1,0:T(8,128)S(1)} %bitcast.18, f32[4,32,128]{2,1,0:T(8,128)S(1)} %copy-done.2, f32[6,32,128]{2,1,0:T(8,128)S(1)} %copy-done.1, ...), custom_call_target="tpu_custom_call" | custom-call | tf_op jit(solution)/shard_map/final/pallas_call | solution.py:395
  37.8 17.0 %all_to_all.15 = f32[32,16,128]{2,1,0:T(8,128)S(1)} all-to-all(f32[32,16,128]{2,1,0:T(8,128)S(1)} %bitcast.20), channel_id=1, replica_groups=mesh['z'=16,'xh'=2,'c'=2,'y'=4,'xl'=2] {'xh','c','y','xl'}, dimensions={0} | all-to-all | bytes 524288 | tf_op jit(solution)/shard_map/all_to_all | solution.py:454
  54.9 24.7 %all_to_all.16 = f32[16,16,128]{2,1,0:T(8,128)S(1)} all-to-all(f32[16,16,128]{2,1,0:T(8,128)S(1)} %broadcast_in_dim.4), channel_id=1, replica_groups=mesh['z'=16,'xh'=2,'c'=2,'y'=4,'xl'=2] {'z'}, dimensions={0} | all-to-all | bytes 262144 | tf_op jit(solution)/shard_map/all_to_all | solution.py:456
  79.6 15.1 %all_to_all.17 = f32[32,16,128]{2,1,0:T(8,128)S(1)} all-to-all(f32[32,16,128]{2,1,0:T(8,128)S(1)} %broadcast_in_dim.5), channel_id=1, replica_groups=mesh['z'=16,'xh'=2,'c'=2,'y'=4,'xl'=2] {'xh','c','y','xl'}, dimensions={0} | all-to-all | bytes 524288 | tf_op jit(solution)/shard_map/all_to_all | solution.py:458
  94.7 0.8 unpack.1
  (6 shorter events, 0.1 us)
Async XLA Ops:
  1.7 9.5 %collective-permute-start = (f32[46,8,128]{2,1,0:T(8,128)S(1)}, f32[46,8,128]{2,1,0:T(8,128)S(1)}, u32[]{:S(2)}, u32[]{:S(2)}) collective-permute-start(f32[46,8,128]{2,1,0:T(8,128)S(1)} %get-tuple-element.65.last_hbm), channel_id=1, source_target_pairs={{0,1},{1,2},{2,3},{3,4},{4,5},{5,6},{6,7},{8,9},{9,10},{10,11},{11... | collective-permute-start | bytes 565256 | tf_op jit(solution)/shard_map/ppermute | solution.py:448
  5.7 8.2 %collective-permute-start.1 = (f32[46,8,128]{2,1,0:T(8,128)S(1)}, f32[46,8,128]{2,1,0:T(8,128)S(1)}, u32[]{:S(2)}, u32[]{:S(2)}) collective-permute-start(f32[46,8,128]{2,1,0:T(8,128)S(1)} %get-tuple-element.66.first_hbm), channel_id=1, source_target_pairs={{1,0},{2,1},{3,2},{4,3},{5,4},{6,5},{7,6},{9,8},{10,9},{11,10},{12... | collective-permute-start | bytes 565256 | tf_op jit(solution)/shard_map/ppermute | solution.py:448
  7.0 6.9 %copy-start = (f32[6,6,32,128]{3,2,1,0:T(8,128)S(1)}, f32[6,6,32,128]{3,2,1,0:T(8,128)}, u32[]{:S(2)}) copy-start(f32[6,6,32,128]{3,2,1,0:T(8,128)} %param.15) | copy-start | bytes 1769476
  7.0 6.9 %copy-start.1 = (f32[6,32,128]{2,1,0:T(8,128)S(1)}, f32[6,32,128]{2,1,0:T(8,128)}, u32[]{:S(2)}) copy-start(f32[6,32,128]{2,1,0:T(8,128)} %mis_ref.5) | copy-start | bytes 294916
  7.0 6.9 %copy-start.2 = (f32[4,32,128]{2,1,0:T(8,128)S(1)}, f32[4,32,128]{2,1,0:T(8,128)}, u32[]{:S(2)}) copy-start(f32[4,32,128]{2,1,0:T(8,128)} %cpl_ref.5) | copy-start | bytes 196612
  14.3 10.6 %collective-permute-start.2 = (f32[3,48,128]{2,1,0:T(8,128)S(1)}, f32[3,48,128]{2,1,0:T(8,128)S(1)}, u32[]{:S(2)}, u32[]{:S(2)}) collective-permute-start(f32[3,48,128]{2,1,0:T(8,128)S(1)} %right_columns.1), channel_id=1, source_target_pairs={{0,8},{8,16},{16,24},{24,32},{32,40},{40,48},{48,56},{56,64},{64,7... | collective-permute-start | bytes 221192 | tf_op jit(solution)/shard_map/ppermute | solution.py:448
  23.0 8.1 %collective-permute-start.3 = (f32[3,48,128]{2,1,0:T(8,128)S(1)}, f32[3,48,128]{2,1,0:T(8,128)S(1)}, u32[]{:S(2)}, u32[]{:S(2)}) collective-permute-start(f32[3,48,128]{2,1,0:T(8,128)S(1)} %get-tuple-element.78), channel_id=1, source_target_pairs={{0,504},{8,0},{16,8},{24,16},{32,24},{40,32},{48,40},{56,48},{64,5... | collective-permute-start | bytes 221192 | tf_op jit(solution)/shard_map/ppermute | solution.py:448
  24.9 6.1 %copy-start.3 = (f32[6,32,128]{2,1,0:T(8,128)S(1)}, f32[6,32,128]{2,1,0:T(8,128)}, u32[]{:S(2)}) copy-start(f32[6,32,128]{2,1,0:T(8,128)} %prod_ref.1) | copy-start | bytes 294916

commit v5 on v4

--- a/solution.py
+++ b/solution.py
@@ -15,9 +15,9 @@
 F32 = jnp.float32
 BF16 = jnp.bfloat16
 GROUP = 8
-WIDE = 8
 PARTS = 3
 MIB = 1 << 20
+ROWS = 416
 LIMIT = 8 * MIB
 
 
@@ -193,6 +193,11 @@
     )(token, x, *prepared, vectors)
 
 
+def place(lane, k, offset):
+    moved = (lane + offset) & 127
+    return (moved >= 8 * k) & (moved < 8 * k + 8)
+
+
 def packed(up_ref, inv_ref, cpl_ref, mis_ref, down_ref, out_ref, offset):
     rows = mis_ref.shape[1]
     tiles = rows // 8 + 2
@@ -202,9 +207,8 @@
             out = jnp.zeros((8, 128), F32)
             for k in range(min(16, 46 - 16 * j)):
                 value = tile_of(up_ref, inv_ref, cpl_ref, mis_ref, down_ref, 16 * j + k, t)
-                by = (8 * k - offset) % 128
-                here = (lane >= 8 * k) & (lane < 8 * k + 8)
-                out = jnp.where(here, pltpu.roll(value, by, 1) if by else value, out)
+                here = place(lane, k, offset)
+                out = jnp.where(here, pltpu.roll(value, 8 * k, 1) if k else value, out)
             out_ref[j, pl.ds(8 * t, 8)] = out
 
 
@@ -219,25 +223,25 @@
     return cpl_ref[a - 36, at] if a < 40 else mis_ref[a - 40, at]
 
 
-def right_kernel(up_ref, inv_ref, cpl_ref, mis_ref, down_ref, token, out_ref):
-    packed(up_ref, inv_ref, cpl_ref, mis_ref, down_ref, out_ref, 120)
-
-
-def right_call(up, inv, cpl, mis, down, token):
+def far_kernel(up_ref, inv_ref, cpl_ref, mis_ref, down_ref, token, out_ref):
+    packed(up_ref, inv_ref, cpl_ref, mis_ref, down_ref, out_ref, 8 * lax.axis_index("c"))
+
+
+def far_call(up, inv, cpl, mis, down, token):
     rows = mis.shape[1]
     return pl.pallas_call(
-        right_kernel,
+        far_kernel,
         in_specs=[VMEM] * 5 + [ANY],
         out_specs=VMEM,
         out_shape=jax.ShapeDtypeStruct((3, rows + 16, 128), F32),
         compiler_params=pltpu.CompilerParams(vmem_limit_bytes=LIMIT),
-        name="right_columns",
+        name="far_columns",
     )(up, inv, cpl, mis, down, token)
 
 
 def third_kernel(base, count, up_ref, inv_ref, cpl_ref, mis_ref, down_ref, x_ref, *rest):
     network_rows(x_ref, base, count, rest[:8], rest[8], rest[10:])
-    packed(up_ref, inv_ref, cpl_ref, mis_ref, down_ref, rest[9], 0)
+    packed(up_ref, inv_ref, cpl_ref, mis_ref, down_ref, rest[9], 8 - 8 * lax.axis_index("c"))
 
 
 def third_call(base, count, up, inv, cpl, mis, down, x, prepared, vectors):
@@ -249,11 +253,11 @@
         out_shape=[jax.ShapeDtypeStruct((3, rows + 16, 128), F32)] + network_shapes(count),
         compiler_params=pltpu.CompilerParams(vmem_limit_bytes=LIMIT),
         cost_estimate=cost(count),
-        name="network_left",
+        name="network_near",
     )(up, inv, cpl, mis, down, x, *prepared, vectors)
 
 
-def final_kernel(up_ref, inv_ref, cpl_ref, mis_ref, down_ref, prod_ref, froml_ref, fromr_ref, wt, *rest):
+def final_kernel(up_ref, inv_ref, cpl_ref, mis_ref, down_ref, prod_ref, far_ref, near_ref, wt, *rest):
     parts = [rest[9 * p : 9 * p + 9] for p in range(PARTS)]
     adj_ref, sens_ref, corr_ref, sums_ref, ext, *rest = rest[9 * PARTS :]
     main, side, (acc4, acc3, acc2, acc1, flat) = rest[0:2], rest[2:4], rest[4:]
@@ -265,15 +269,14 @@
     def tile(a, t):
         return tile_of(up_ref, inv_ref, cpl_ref, mis_ref, down_ref, a, t)
 
+    offset = 8 * lax.axis_index("c")
     for a in range(46):
         j, k = a // 16, a % 16
         for t in range(tiles):
             at = pl.ds(8 * t, 8)
-            high = fromr_ref[j, at]
-            low = froml_ref[j, at]
-            high = pltpu.roll(high, (128 - 8 * k) % 128, 1) if k else high
-            low = pltpu.roll(low, 120 - 8 * k, 1) if k != 15 else low
-            ext[a, at] = jnp.where(lane < 8, high, jnp.where(lane >= 120, low, 0.0))
+            both = jnp.where(place(lane, k, offset), near_ref[j, at], far_ref[j, at])
+            both = pltpu.roll(both, 128 - 8 * k, 1) if k else both
+            ext[a, at] = jnp.where((lane < 8) | (lane >= 120), both, 0.0)
 
     edge = jnp.zeros((8, 128), F32)
     for field in main + side:
@@ -293,8 +296,8 @@
         solve(main[0], t, lambda a: tile(a, t), [tile(40 + i, t) for i in range(6)])
         solve(side[0], t, lambda a: ext[a, at], [ext[40 + i, at] for i in range(6)])
 
-    def sweep(main, side, main_next, side_next):
-        for t in range(tiles):
+    def sweep(main, side, main_next, side_next, final=False):
+        for t in range(1, tiles - 1) if final else range(tiles):
             at = pl.ds(8 * t, 8)
             near, beside = [], []
             for i in range(6):
@@ -311,17 +314,20 @@
                 rhs = rhs + ext[38, at] * jnp.where(first, m_low, e_low)
                 beside.append(rhs + ext[39, at] * jnp.where(last, m_high, e_high))
             solve(main_next, t, lambda a: tile(a, t), near)
-            solve(side_next, t, lambda a: ext[a, at], beside)
+            if not final:
+                solve(side_next, t, lambda a: ext[a, at], beside)
 
     def two(n, carry):
         sweep(main[0], side[0], main[1], side[1])
         sweep(main[1], side[1], main[0], side[0])
         return carry
 
-    lax.fori_loop(0, (SWEEPS - 1) // 2, two, 0)
-    if (SWEEPS - 1) % 2:
+    lax.fori_loop(0, (SWEEPS - 2) // 2, two, 0)
+    if SWEEPS % 2:
         sweep(main[0], side[0], main[1], side[1])
-    done = main[(SWEEPS - 1) % 2]
+    at = SWEEPS % 2
+    sweep(main[at], side[at], main[1 - at], side[1 - at], True)
+    done = main[1 - at]
 
     square = jnp.zeros((8, 128), F32)
     for t in range(rows // 8):
@@ -355,24 +361,24 @@
         for r in range(corr.shape[0]):
             corr_ref[base + r : base + r + 1] = corr[r]
 
-        def gather(g, carry, base=base, part=part):
+        def gather(g, carry, base=base, part=part, wide=min(8, l1.shape[0])):
             _, xc, l1, l2, l3, l4t, d3t, d2t, d1t = part
-            at = WIDE * g
-            some = pl.ds(at, WIDE)
-            weights = [sens_ref[pl.ds(base + at + r, 1), :] for r in range(WIDE)]
+            at = wide * g
+            some = pl.ds(at, wide)
+            weights = [sens_ref[pl.ds(base + at + r, 1), :] for r in range(wide)]
             out = flat[4]
             scaled = []
-            for r in range(WIDE):
+            for r in range(wide):
                 value = l4t[at + r]
                 out = out + value * weights[r]
                 scaled.append(wt[...] * (1.0 - value * value) * weights[r])
             flat[4] = out
             term(scaled, l3[some], acc4, 3)
             for delta, layer, acc, slot in ((d3t, l2, acc3, 2), (d2t, l1, acc2, 1), (d1t, xc, acc1, 0)):
-                term([delta[at + r] * weights[r] for r in range(WIDE)], layer[some], acc, slot)
+                term([delta[at + r] * weights[r] for r in range(wide)], layer[some], acc, slot)
             return carry
 
-        lax.fori_loop(0, l1.shape[0] // WIDE, gather, 0)
+        lax.fori_loop(0, l1.shape[0] // min(8, l1.shape[0]), gather, 0)
         base += l1.shape[0]
 
     for n, acc in enumerate((acc4, acc3, acc2)):
@@ -386,10 +392,10 @@
     own = acc1[0:128] + acc1[128:256]
     own = jnp.concatenate([own, jnp.zeros((128, 80), F32)], axis=1)
     own = own + pltpu.roll(own, 112, 1)
-    sums_ref[pl.ds(384, 128)] = jnp.where(lanes < 12, own, block)
-
-
-def final_call(up, inv, cpl, mis, down, prod, froml, fromr, wt, parts):
+    sums_ref[pl.ds(384, ROWS - 384)] = jnp.where(lanes < 12, own, block).T[0 : ROWS - 384]
+
+
+def final_call(up, inv, cpl, mis, down, prod, far, near, wt, parts):
     rows = mis.shape[1]
     flat = [value for part in parts for value in part]
     return pl.pallas_call(
@@ -400,7 +406,7 @@
             jax.ShapeDtypeStruct((6, rows, 128), F32),
             jax.ShapeDtypeStruct((rows, 128), F32),
             jax.ShapeDtypeStruct((rows, 128), F32),
-            jax.ShapeDtypeStruct((512, 128), F32),
+            jax.ShapeDtypeStruct((ROWS, 128), F32),
         ],
         scratch_shapes=[
             pltpu.VMEM((46, rows + 16, 128), F32),
@@ -414,21 +420,18 @@
             pltpu.VMEM((256, 48), F32),
             pltpu.VMEM((5, 128, 128), F32),
         ],
-        compiler_params=pltpu.CompilerParams(vmem_limit_bytes=LIMIT),
+        compiler_params=pltpu.CompilerParams(vmem_limit_bytes=2 * LIMIT),
         name="final",
-    )(up, inv, cpl, mis, down, prod, froml, fromr, wt, *flat)
+    )(up, inv, cpl, mis, down, prod, far, near, wt, *flat)
 
 
 def unpack_kernel(sums_ref, w4_ref, w3_ref, w2_ref, win_ref, b1_ref, b2_ref, b3_ref, b4_ref, out_ref):
-    block = sums_ref[pl.ds(384, 128)]
-    scale = 1.0 / jnp.sqrt(jnp.broadcast_to(block[0:1, 21:22], (1, 128)) + EPS)
+    scale = 1.0 / jnp.sqrt(sums_ref[405:406] + EPS)
     for n, ref in enumerate((w4_ref, w3_ref, w2_ref)):
         ref[...] = sums_ref[pl.ds(128 * n, 128)] * scale
-    block = block * scale
-    turned = block.T
-    win_ref[...] = turned[0:12]
+    win_ref[...] = sums_ref[384:396] * scale
     for n, ref in enumerate((b1_ref, b2_ref, b3_ref, b4_ref, out_ref)):
-        ref[...] = turned[16 + n : 17 + n]
+        ref[...] = sums_ref[400 + n : 401 + n] * scale
 
 
 def unpack_call(sums):
@@ -442,21 +445,26 @@
     )(sums)
 
 
-def sent(value, axes, wrap, by):
+def sent(value, axes, by):
     size = lax.axis_size(axes)
-    pairs = [(i, (i + by) % size) for i in range(size) if wrap or 0 <= i + by < size]
-    return lax.ppermute(value, axes, pairs)
+    return lax.ppermute(value, axes, [(i, i + by) for i in range(size) if 0 <= i + by < size])
+
+
+def swapped(value, start):
+    size = lax.axis_size(BLK)
+    pairs = [(i, (i + 1) % size) for i in range(start, size, 2)]
+    return lax.ppermute(value, BLK, pairs + [(j, i) for i, j in pairs])
 
 
 def summed(value):
     near, far = lax.axis_size(NEAR), lax.axis_size(FAR)
-    rows = value.shape[0] // near
-    part = lax.all_to_all(value.reshape(near, rows, 128), NEAR, 0, 0)
+    piece = (value.shape[0] // near, 1, 128)
+    part = lax.all_to_all(value.reshape((near,) + piece), NEAR, 0, 0)
     part = jnp.sum(part, axis=0)
-    part = lax.all_to_all(jnp.broadcast_to(part[None], (far, rows, 128)), FAR, 0, 0)
+    part = lax.all_to_all(jnp.broadcast_to(part[None], (far,) + piece), FAR, 0, 0)
     part = jnp.sum(part, axis=0)
-    whole = lax.all_to_all(jnp.broadcast_to(part[None], (near, rows, 128)), NEAR, 0, 0)
-    return whole.reshape(near * rows, 128)
+    whole = lax.all_to_all(jnp.broadcast_to(part[None], (near,) + piece), NEAR, 0, 0)
+    return whole.reshape(value.shape)
 
 
 def local(features, inverse_diag, couplings, mismatch, production, weight_in, bias_in, weight_two,
@@ -468,22 +476,22 @@
     count = rows // 4
 
     last, initial = edge_call(inverse, couplings, mismatch)
-    above = sent(last, SUB, False, 1)
-    below = sent(initial, SUB, False, -1)
+    above = sent(last, SUB, 1)
+    below = sent(initial, SUB, -1)
     features, vectors, *rest = opening_call(
         0, 2 * count, last, initial, features, win, weight_two, weight_three, weight_four, vectors)
     prepared, first = rest[:8], rest[8:]
 
-    right = right_call(above, inverse, couplings, mismatch, below, first[0])
-    from_low = sent(right, BLK, True, 1)
-    left, *second = third_call(2 * count, count, above, inverse, couplings, mismatch, below, features,
-                              prepared, vectors)
-    from_high = sent(left, BLK, True, -1)
-    third = middle_call(3 * count, count, from_low, features, prepared, vectors)
+    far = far_call(above, inverse, couplings, mismatch, below, first[0])
+    from_far = swapped(far, 1)
+    near, *second = third_call(2 * count, count, above, inverse, couplings, mismatch, below, features,
+                               prepared, vectors)
+    from_near = swapped(near, 0)
+    third = middle_call(3 * count, count, from_far, features, prepared, vectors)
 
     parts = (first, second, third)
     adjoint, sensitivity, correction, sums = final_call(
-        above, inverse, couplings, mismatch, below, production, from_low, from_high, prepared[7],
+        above, inverse, couplings, mismatch, below, production, from_far, from_near, prepared[7],
         parts)
     g4, g3, g2, gin, b1, b2, b3, b4, gout = unpack_call(summed(sums))
     flat = lambda value: value.reshape(128)
@@ -492,7 +500,7 @@
 
 
 def solution(mesh):
-    sizes = (16, 2, 2, 4, 2) if mesh.devices.size == 512 else (mesh.shape["blk"], 1, 1, mesh.shape["sub"], 1)
+    sizes = (16, 2, 2, 4, 2) if mesh.devices.size == 512 else (mesh.shape["blk"] // 2, 1, 2, mesh.shape["sub"], 1)
     fine = Mesh(mesh.devices.reshape(sizes), BLK + SUB)
     three = P(None, SUB, BLK)
     two = P(SUB, BLK)

time: 95.8 us -> 90.1 us (0.941)
  blocking collectives: 56.8 us -> 47.9 us
  starting transfers between devices: 14.4 us -> 22.3 us
  waiting for transfers between devices: 7.46 us -> 2.74 us
    all_to_all x3, blocking collectives: 56.8 us -> 47.9 us  [the longest x1 20.7 us: summed(): lax.all_to_all(jnp.broadcast_to(part[None], (far,) + piece), FAR, 0, 0)]
    ppermute x4, starting transfers between devices: 14.4 us -> 22.3 us  [the longest x2 17 us: swapped(): return lax.ppermute(value, BLK, pairs + [(j, i) for i, j in pairs])]
    ppermute x4, waiting for transfers between devices: 7.46 us -> 2.74 us  [the longest x2 2.73 us: sent(): lax.ppermute(value, axes, [(i, i + by) for i in range(size) if 0 <= i + b...]
  transfers between devices with their start and end apart: 4 -> 4, of which waited for: 2 -> 1; matrix products, arithmetic and copies ran while one was open for 0% -> 0% of each run, Pallas kernels for 7% -> 8%
where the time goes in v5:
time: 90.1 us; the launch traced here: 89.7 us
  blocking collectives  47.9 us (53%)
  starting transfers between devices  22.3 us (25%)
  Pallas kernels  15.6 us (17%)
  waiting for transfers between devices  2.74 us (3%)
    all_to_all x1, blocking collectives, summed(): lax.all_to_all(jnp.broadcast_to(part[None], (far,) + piece), FAR, 0, 0)  20.7 us
    ppermute x2, starting transfers between devices, swapped(): return lax.ppermute(value, BLK, pairs + [(j, i) for i, j in pairs])  17 us
    all_to_all x1, blocking collectives, summed(): lax.all_to_all(jnp.broadcast_to(part[None], (near,) + piece), NEAR, 0, 0)  14.3 us
    all_to_all x1, blocking collectives, summed(): part = lax.all_to_all(value.reshape((near,) + piece), NEAR, 0, 0)  12.9 us
    pallas_call x1, Pallas kernels, final_call(): pl.pallas_call(final_kernel, in_specs=[VMEM] * (9 + len(flat)), out_specs...  6.44 us
    ppermute x2, starting transfers between devices, sent(): lax.ppermute(value, axes, [(i, i + by) for i in range(size) if 0 <= i + b...  5.25 us
    pallas_call x1, Pallas kernels, opening_call(): pl.pallas_call(functools.partial(opening_kernel, base, count), in_specs=[...  4.16 us
    ppermute x2, waiting for transfers between devices, sent(): lax.ppermute(value, axes, [(i, i + by) for i in range(size) if 0 <= i + b...  2.73 us
  transfers between devices with their start and end apart: 4, of which 1 were waited for; matrix products, arithmetic and copies ran while one was open for 0% of the time, Pallas kernels for 8%

profile of v5, /device:TPU:1, one launch (start us, length us, event | category | flops | bytes accessed | tf_op | source)
XLA Modules:
  0.0 89.7 jit_solution(1483383290064633858)
XLA Ops:
  0.6 1.1 %edge_rows.1 = (f32[46,8,128]{2,1,0:T(8,128)S(1)}, f32[46,8,128]{2,1,0:T(8,128)S(1)}) custom-call(f32[36,32,128]{2,1,0:T(8,128)} %bitcast.15, f32[4,32,128]{2,1,0:T(8,128)} %cpl_ref.5, f32[6,32,128]{2,1,0:T(8,128)} %mis_ref.5), custom_call_target="tpu_custom_call" | custom-call | tf_op jit(solution)/shard_map/edge_rows/pallas_call | solution.py:129
  1.7 4.0 %collective-permute-start = (f32[46,8,128]{2,1,0:T(8,128)S(1)}, f32[46,8,128]{2,1,0:T(8,128)S(1)}, u32[]{:S(2)}, u32[]{:S(2)}) collective-permute-start(f32[46,8,128]{2,1,0:T(8,128)S(1)} %get-tuple-element.65.last_hbm), channel_id=1, source_target_pairs={{0,1},{1,2},{2,3},{3,4},{4,5},{5,6},{6,7},{8,9},{9,10},{10,11},{11... | collective-permute-start | bytes 565256 | tf_op jit(solution)/shard_map/ppermute | solution.py:450
  5.7 1.3 %collective-permute-start.1 = (f32[46,8,128]{2,1,0:T(8,128)S(1)}, f32[46,8,128]{2,1,0:T(8,128)S(1)}, u32[]{:S(2)}, u32[]{:S(2)}) collective-permute-start(f32[46,8,128]{2,1,0:T(8,128)S(1)} %get-tuple-element.66.first_hbm), channel_id=1, source_target_pairs={{1,0},{2,1},{3,2},{4,3},{5,4},{6,5},{7,6},{9,8},{10,9},{11,10},{12... | collective-permute-start | bytes 565256 | tf_op jit(solution)/shard_map/ppermute | solution.py:450
  7.0 0.0 copy-start
  7.0 0.0 copy-start.1
  7.0 0.0 copy-start.2
  7.0 4.2 %network_first.1 = (f32[12,32,128]{2,1,0:T(8,128)S(1)}, f32[8,128]{1,0:T(8,128)S(1)}, bf16[48,128]{1,0:T(8,128)(2,1)S(1)}, bf16[256,256]{1,0:T(8,128)(2,1)S(1)},...) custom-call(f32[46,8,128]{2,1,0:T(8,128)S(1)} %get-tuple-element.65., ...), custom_call_target="tpu_custom_call" | custom-call | flops 4800000000 | bytes 16000 | tf_op jit(solution)/shard_map/network_first/pallas_call | solution.py:166
  11.2 0.0 collective-permute-done.up_ref
  11.2 2.7 %collective-permute-done.1.down_ref = f32[46,8,128]{2,1,0:T(8,128)S(1)} collective-permute-done((f32[46,8,128]{2,1,0:T(8,128)S(1)}, f32[46,8,128]{2,1,0:T(8,128)S(1)}, u32[]{:S(2)}, u32[]{:S(2)}) %collective-permute-start.1) | collective-permute-done | bytes 188448 | tf_op jit(solution)/shard_map/ppermute | solution.py:450
  13.9 0.3 far_columns.1
  14.3 7.2 %collective-permute-start.2 = (f32[3,48,128]{2,1,0:T(8,128)S(1)}, f32[3,48,128]{2,1,0:T(8,128)S(1)}, u32[]{:S(2)}, u32[]{:S(2)}) collective-permute-start(f32[3,48,128]{2,1,0:T(8,128)S(1)} %far_columns.1), channel_id=1, source_target_pairs={{8,16},{24,32},{40,48},{56,64},{72,80},{88,96},{104,112},{120,128}... | collective-permute-start | bytes 221192 | tf_op jit(solution)/shard_map/ppermute | solution.py:456
  21.5 1.5 %network_near.1 = (f32[3,48,128]{2,1,0:T(8,128)S(1)}, f32[8,1,128]{2,1,0:T(1,128)S(1)}, bf16[8,128,48]{2,1,0:T(8,128)(2,1)S(1)}, bf16[8,128,256]{2,1,0:T(8,128)(...) custom-call(f32[46,8,128]{2,1,0:T(8,128)S(1)} %collective-permute-do, ...), custom_call_target="tpu_custom_call" | custom-call | flops 2400000000 | bytes 8000 | tf_op jit(solution)/shard_map/network_near/pallas_call | solution.py:249
  23.0 9.8 %collective-permute-start.3 = (f32[3,48,128]{2,1,0:T(8,128)S(1)}, f32[3,48,128]{2,1,0:T(8,128)S(1)}, u32[]{:S(2)}, u32[]{:S(2)}) collective-permute-start(f32[3,48,128]{2,1,0:T(8,128)S(1)} %get-tuple-element.78), channel_id=1, source_target_pairs={{0,8},{16,24},{32,40},{48,56},{64,72},{80,88},{96,104},{112,120},{... | collective-permute-start | bytes 221192 | tf_op jit(solution)/shard_map/ppermute | solution.py:456
  32.8 0.0 copy-start.3
  32.8 1.4 %network.1 = (f32[8,1,128]{2,1,0:T(1,128)S(1)}, bf16[8,128,48]{2,1,0:T(8,128)(2,1)S(1)}, bf16[8,128,256]{2,1,0:T(8,128)(2,1)S(1)}, bf16[8,128,256]{2,1,0:T(8,128...) custom-call(f32[3,48,128]{2,1,0:T(8,128)S(1)} %collective-permute-do, ...), custom_call_target="tpu_custom_call" | custom-call | flops 2400000000 | bytes 8000 | tf_op jit(solution)/shard_map/network/pallas_call | solution.py:185
  34.2 6.4 %final.1 = (f32[6,32,128]{2,1,0:T(8,128)}, f32[32,128]{1,0:T(8,128)}, f32[32,128]{1,0:T(8,128)}, f32[416,128]{1,0:T(8,128)S(1)}) custom-call(f32[46,8,128]{2,1,0:T(8,128)S(1)} %collective-permute-done.up_ref, f32[36,32,128]{2,1,0:T(8,128)S(1)} %bitcast.18, f32[4,32,128]{2,1,0:T(8,128)S(1)} %copy-done.2, f32[6,32,128]{2,1,0:T(8,128)S(1)} %copy-done.1, ...), custom_call_target="tpu_custom_call" | custom-call | tf_op jit(solution)/shard_map/final/pallas_call | solution.py:401
  40.7 12.9 %all_to_all.15 = f32[32,13,1,128]{3,2,1,0:T(1,128)S(1)} all-to-all(f32[32,13,1,128]{3,2,1,0:T(1,128)S(1)} %bitcast.20), channel_id=1, replica_groups=mesh['z'=16,'xh'=2,'c'=2,'y'=4,'xl'=2] {'xh','c','y','xl'}, dimensions={0} | all-to-all | bytes 425984 | tf_op jit(solution)/shard_map/all_to_all | solution.py:462
  53.6 0.1 reduce_sum.18
  53.7 0.1 broadcast_in_dim.4
  53.8 20.7 %all_to_all.16 = f32[16,13,1,128]{3,2,1,0:T(1,128)S(1)} all-to-all(f32[16,13,1,128]{3,2,1,0:T(1,128)S(1)} %broadcast_in_dim.4), channel_id=1, replica_groups=mesh['z'=16,'xh'=2,'c'=2,'y'=4,'xl'=2] {'z'}, dimensions={0} | all-to-all | bytes 212992 | tf_op jit(solution)/shard_map/all_to_all | solution.py:464
  74.5 0.1 reduce_sum.19
  74.6 0.1 broadcast_in_dim.5
  74.7 14.3 %all_to_all.17 = f32[32,13,1,128]{3,2,1,0:T(1,128)S(1)} all-to-all(f32[32,13,1,128]{3,2,1,0:T(1,128)S(1)} %broadcast_in_dim.5), channel_id=1, replica_groups=mesh['z'=16,'xh'=2,'c'=2,'y'=4,'xl'=2] {'xh','c','y','xl'}, dimensions={0} | all-to-all | bytes 425984 | tf_op jit(solution)/shard_map/all_to_all | solution.py:466
  89.0 0.7 unpack.1
  (6 shorter events, 0.0 us)
Async XLA Ops:
  1.7 9.5 %collective-permute-start = (f32[46,8,128]{2,1,0:T(8,128)S(1)}, f32[46,8,128]{2,1,0:T(8,128)S(1)}, u32[]{:S(2)}, u32[]{:S(2)}) collective-permute-start(f32[46,8,128]{2,1,0:T(8,128)S(1)} %get-tuple-element.65.last_hbm), channel_id=1, source_target_pairs={{0,1},{1,2},{2,3},{3,4},{4,5},{5,6},{6,7},{8,9},{9,10},{10,11},{11... | collective-permute-start | bytes 565256 | tf_op jit(solution)/shard_map/ppermute | solution.py:450
  5.7 8.2 %collective-permute-start.1 = (f32[46,8,128]{2,1,0:T(8,128)S(1)}, f32[46,8,128]{2,1,0:T(8,128)S(1)}, u32[]{:S(2)}, u32[]{:S(2)}) collective-permute-start(f32[46,8,128]{2,1,0:T(8,128)S(1)} %get-tuple-element.66.first_hbm), channel_id=1, source_target_pairs={{1,0},{2,1},{3,2},{4,3},{5,4},{6,5},{7,6},{9,8},{10,9},{11,10},{12... | collective-permute-start | bytes 565256 | tf_op jit(solution)/shard_map/ppermute | solution.py:450
  7.0 6.9 %copy-start = (f32[6,6,32,128]{3,2,1,0:T(8,128)S(1)}, f32[6,6,32,128]{3,2,1,0:T(8,128)}, u32[]{:S(2)}) copy-start(f32[6,6,32,128]{3,2,1,0:T(8,128)} %param.15) | copy-start | bytes 1769476
  7.0 6.9 %copy-start.1 = (f32[6,32,128]{2,1,0:T(8,128)S(1)}, f32[6,32,128]{2,1,0:T(8,128)}, u32[]{:S(2)}) copy-start(f32[6,32,128]{2,1,0:T(8,128)} %mis_ref.5) | copy-start | bytes 294916
  7.0 6.9 %copy-start.2 = (f32[4,32,128]{2,1,0:T(8,128)S(1)}, f32[4,32,128]{2,1,0:T(8,128)}, u32[]{:S(2)}) copy-start(f32[4,32,128]{2,1,0:T(8,128)} %cpl_ref.5) | copy-start | bytes 196612
  14.3 18.5 %collective-permute-start.2 = (f32[3,48,128]{2,1,0:T(8,128)S(1)}, f32[3,48,128]{2,1,0:T(8,128)S(1)}, u32[]{:S(2)}, u32[]{:S(2)}) collective-permute-start(f32[3,48,128]{2,1,0:T(8,128)S(1)} %far_columns.1), channel_id=1, source_target_pairs={{8,16},{24,32},{40,48},{56,64},{72,80},{88,96},{104,112},{120,128}... | collective-permute-start | bytes 221192 | tf_op jit(solution)/shard_map/ppermute | solution.py:456
  23.0 11.2 %collective-permute-start.3 = (f32[3,48,128]{2,1,0:T(8,128)S(1)}, f32[3,48,128]{2,1,0:T(8,128)S(1)}, u32[]{:S(2)}, u32[]{:S(2)}) collective-permute-start(f32[3,48,128]{2,1,0:T(8,128)S(1)} %get-tuple-element.78), channel_id=1, source_target_pairs={{0,8},{16,24},{32,40},{48,56},{64,72},{80,88},{96,104},{112,120},{... | collective-permute-start | bytes 221192 | tf_op jit(solution)/shard_map/ppermute | solution.py:456
  32.8 1.4 %copy-start.3 = (f32[6,32,128]{2,1,0:T(8,128)S(1)}, f32[6,32,128]{2,1,0:T(8,128)}, u32[]{:S(2)}) copy-start(f32[6,32,128]{2,1,0:T(8,128)} %prod_ref.1) | copy-start | bytes 294916

commit v6 on v5

--- a/solution.py
+++ b/solution.py
@@ -15,7 +15,7 @@
 F32 = jnp.float32
 BF16 = jnp.bfloat16
 GROUP = 8
-PARTS = 3
+PARTS = 2
 MIB = 1 << 20
 ROWS = 416
 LIMIT = 8 * MIB
@@ -223,41 +223,39 @@
     return cpl_ref[a - 36, at] if a < 40 else mis_ref[a - 40, at]
 
 
-def far_kernel(up_ref, inv_ref, cpl_ref, mis_ref, down_ref, token, out_ref):
-    packed(up_ref, inv_ref, cpl_ref, mis_ref, down_ref, out_ref, 8 * lax.axis_index("c"))
-
-
-def far_call(up, inv, cpl, mis, down, token):
+def columns_kernel(far, up_ref, inv_ref, cpl_ref, mis_ref, down_ref, token, out_ref):
+    core = lax.axis_index("c")
+    packed(up_ref, inv_ref, cpl_ref, mis_ref, down_ref, out_ref, 8 * core if far else 8 - 8 * core)
+
+
+def columns_call(far, up, inv, cpl, mis, down, token):
     rows = mis.shape[1]
     return pl.pallas_call(
-        far_kernel,
+        functools.partial(columns_kernel, far),
         in_specs=[VMEM] * 5 + [ANY],
         out_specs=VMEM,
         out_shape=jax.ShapeDtypeStruct((3, rows + 16, 128), F32),
         compiler_params=pltpu.CompilerParams(vmem_limit_bytes=LIMIT),
-        name="far_columns",
+        name="far_columns" if far else "near_columns",
     )(up, inv, cpl, mis, down, token)
 
 
-def third_kernel(base, count, up_ref, inv_ref, cpl_ref, mis_ref, down_ref, x_ref, *rest):
-    network_rows(x_ref, base, count, rest[:8], rest[8], rest[10:])
-    packed(up_ref, inv_ref, cpl_ref, mis_ref, down_ref, rest[9], 8 - 8 * lax.axis_index("c"))
-
-
-def third_call(base, count, up, inv, cpl, mis, down, x, prepared, vectors):
-    rows = mis.shape[1]
-    return pl.pallas_call(
-        functools.partial(third_kernel, base, count),
-        in_specs=[VMEM] * 15,
-        out_specs=[VMEM] * 10,
-        out_shape=[jax.ShapeDtypeStruct((3, rows + 16, 128), F32)] + network_shapes(count),
+def mark_kernel(token, mark):
+    mark[...] = jnp.zeros_like(mark)
+
+
+def mark_call(token):
+    return pl.pallas_call(
+        mark_kernel,
+        in_specs=[ANY],
+        out_specs=VMEM,
+        out_shape=jax.ShapeDtypeStruct((8, 128), F32),
         compiler_params=pltpu.CompilerParams(vmem_limit_bytes=LIMIT),
-        cost_estimate=cost(count),
-        name="network_near",
-    )(up, inv, cpl, mis, down, x, *prepared, vectors)
-
-
-def final_kernel(up_ref, inv_ref, cpl_ref, mis_ref, down_ref, prod_ref, far_ref, near_ref, wt, *rest):
+        name="mark",
+    )(token)
+
+
+def final_kernel(token, up_ref, inv_ref, cpl_ref, mis_ref, down_ref, prod_ref, far_ref, near_ref, wt, *rest):
     parts = [rest[9 * p : 9 * p + 9] for p in range(PARTS)]
     adj_ref, sens_ref, corr_ref, sums_ref, ext, *rest = rest[9 * PARTS :]
     main, side, (acc4, acc3, acc2, acc1, flat) = rest[0:2], rest[2:4], rest[4:]
@@ -395,12 +393,12 @@
     sums_ref[pl.ds(384, ROWS - 384)] = jnp.where(lanes < 12, own, block).T[0 : ROWS - 384]
 
 
-def final_call(up, inv, cpl, mis, down, prod, far, near, wt, parts):
+def final_call(token, up, inv, cpl, mis, down, prod, far, near, wt, parts):
     rows = mis.shape[1]
     flat = [value for part in parts for value in part]
     return pl.pallas_call(
         final_kernel,
-        in_specs=[VMEM] * (9 + len(flat)),
+        in_specs=[VMEM] * (10 + len(flat)),
         out_specs=[VMEM] * 4,
         out_shape=[
             jax.ShapeDtypeStruct((6, rows, 128), F32),
@@ -422,7 +420,7 @@
         ],
         compiler_params=pltpu.CompilerParams(vmem_limit_bytes=2 * LIMIT),
         name="final",
-    )(up, inv, cpl, mis, down, prod, far, near, wt, *flat)
+    )(token, up, inv, cpl, mis, down, prod, far, near, wt, *flat)
 
 
 def unpack_kernel(sums_ref, w4_ref, w3_ref, w2_ref, win_ref, b1_ref, b2_ref, b3_ref, b4_ref, out_ref):
@@ -473,26 +471,23 @@
     inverse = inverse_diag.reshape(nvars * nvars, rows, cols)
     win = weight_in.T
     vectors = [v.reshape(1, 128) for v in (bias_in, bias_two, bias_three, bias_four, weight_out)]
-    count = rows // 4
+    count = 8 * (rows * 3 // 32)
 
     last, initial = edge_call(inverse, couplings, mismatch)
     above = sent(last, SUB, 1)
     below = sent(initial, SUB, -1)
     features, vectors, *rest = opening_call(
-        0, 2 * count, last, initial, features, win, weight_two, weight_three, weight_four, vectors)
+        0, count, last, initial, features, win, weight_two, weight_three, weight_four, vectors)
     prepared, first = rest[:8], rest[8:]
 
-    far = far_call(above, inverse, couplings, mismatch, below, first[0])
+    far = columns_call(True, above, inverse, couplings, mismatch, below, first[0])
     from_far = swapped(far, 1)
-    near, *second = third_call(2 * count, count, above, inverse, couplings, mismatch, below, features,
-                               prepared, vectors)
+    near = columns_call(False, above, inverse, couplings, mismatch, below, far)
     from_near = swapped(near, 0)
-    third = middle_call(3 * count, count, from_far, features, prepared, vectors)
-
-    parts = (first, second, third)
+    second = middle_call(count, rows - count, near, features, prepared, vectors)
     adjoint, sensitivity, correction, sums = final_call(
-        above, inverse, couplings, mismatch, below, production, from_far, from_near, prepared[7],
-        parts)
+        mark_call(from_far), above, inverse, couplings, mismatch, below, production, from_far, from_near,
+        prepared[7], (first, second))
     g4, g3, g2, gin, b1, b2, b3, b4, gout = unpack_call(summed(sums))
     flat = lambda value: value.reshape(128)
     return (adjoint, sensitivity, correction, gin.T, flat(b1), g2, flat(b2),

time: 90.1 us -> 89.2 us (0.990)
  waiting for transfers between devices: 2.74 us -> 1.36 us
    pallas_call x1, Pallas kernels: 4.16 us -> 5.54 us  [opening_call(): pl.pallas_call(functools.partial(opening_kernel, base, count), in_specs=[...]
    ppermute x2, waiting for transfers between devices: 2.73 us -> 1.35 us  [sent(): lax.ppermute(value, axes, [(i, i + by) for i in range(size) if 0 <= i + b...]
    pallas_call x3 -> x4, Pallas kernels: 8.24 us -> 7.63 us  [the longest x1 6.96 us: final_call(): pl.pallas_call(final_kernel, in_specs=[VMEM] * (10 + len(flat)), out_spec...]
where the time goes in v6:
time: 89.2 us; the launch traced here: 88.8 us
  blocking collectives  47.6 us (53%)
  starting transfers between devices  22.3 us (25%)
  Pallas kernels  16.4 us (18%)
  waiting for transfers between devices  1.36 us (2%)
    all_to_all x1, blocking collectives, summed(): lax.all_to_all(jnp.broadcast_to(part[None], (far,) + piece), FAR, 0, 0)  20.4 us
    ppermute x2, starting transfers between devices, swapped(): return lax.ppermute(value, BLK, pairs + [(j, i) for i, j in pairs])  17 us
    all_to_all x1, blocking collectives, summed(): lax.all_to_all(jnp.broadcast_to(part[None], (near,) + piece), NEAR, 0, 0)  14.3 us
    all_to_all x1, blocking collectives, summed(): part = lax.all_to_all(value.reshape((near,) + piece), NEAR, 0, 0)  12.9 us
    pallas_call x1, Pallas kernels, final_call(): pl.pallas_call(final_kernel, in_specs=[VMEM] * (10 + len(flat)), out_spec...  6.96 us
    pallas_call x1, Pallas kernels, opening_call(): pl.pallas_call(functools.partial(opening_kernel, base, count), in_specs=[...  5.54 us
    ppermute x2, starting transfers between devices, sent(): lax.ppermute(value, axes, [(i, i + by) for i in range(size) if 0 <= i + b...  5.25 us
  transfers between devices with their start and end apart: 4, of which 1 were waited for; matrix products, arithmetic and copies ran while one was open for 0% of the time, Pallas kernels for 8%

profile of v6, /device:TPU:1, one launch (start us, length us, event | category | flops | bytes accessed | tf_op | source)
XLA Modules:
  0.0 88.8 jit_solution(5906274294986011426)
XLA Ops:
  0.6 1.1 %edge_rows.1 = (f32[46,8,128]{2,1,0:T(8,128)S(1)}, f32[46,8,128]{2,1,0:T(8,128)S(1)}) custom-call(f32[36,32,128]{2,1,0:T(8,128)} %bitcast.15, f32[4,32,128]{2,1,0:T(8,128)} %cpl_ref.5, f32[6,32,128]{2,1,0:T(8,128)} %mis_ref.5), custom_call_target="tpu_custom_call" | custom-call | tf_op jit(solution)/shard_map/edge_rows/pallas_call | solution.py:129
  1.7 4.0 %collective-permute-start = (f32[46,8,128]{2,1,0:T(8,128)S(1)}, f32[46,8,128]{2,1,0:T(8,128)S(1)}, u32[]{:S(2)}, u32[]{:S(2)}) collective-permute-start(f32[46,8,128]{2,1,0:T(8,128)S(1)} %get-tuple-element.55.last_hbm), channel_id=1, source_target_pairs={{0,1},{1,2},{2,3},{3,4},{4,5},{5,6},{6,7},{8,9},{9,10},{10,11},{11... | collective-permute-start | bytes 565256 | tf_op jit(solution)/shard_map/ppermute | solution.py:448
  5.7 1.3 %collective-permute-start.1 = (f32[46,8,128]{2,1,0:T(8,128)S(1)}, f32[46,8,128]{2,1,0:T(8,128)S(1)}, u32[]{:S(2)}, u32[]{:S(2)}) collective-permute-start(f32[46,8,128]{2,1,0:T(8,128)S(1)} %get-tuple-element.56.first_hbm), channel_id=1, source_target_pairs={{1,0},{2,1},{3,2},{4,3},{5,4},{6,5},{7,6},{9,8},{10,9},{11,10},{12... | collective-permute-start | bytes 565256 | tf_op jit(solution)/shard_map/ppermute | solution.py:448
  7.0 0.0 copy-start
  7.0 0.0 copy-start.1
  7.0 0.0 copy-start.2
  7.0 5.5 %network_first.1 = (f32[12,32,128]{2,1,0:T(8,128)S(1)}, f32[8,128]{1,0:T(8,128)S(1)}, bf16[48,128]{1,0:T(8,128)(2,1)S(1)}, bf16[256,256]{1,0:T(8,128)(2,1)S(1)},...) custom-call(f32[46,8,128]{2,1,0:T(8,128)S(1)} %get-tuple-element.55., ...), custom_call_target="tpu_custom_call" | custom-call | flops 7200000000 | bytes 24000 | tf_op jit(solution)/shard_map/network_first/pallas_call | solution.py:166
  12.6 0.0 collective-permute-done.up_ref
  12.6 1.3 %collective-permute-done.1.down_ref = f32[46,8,128]{2,1,0:T(8,128)S(1)} collective-permute-done((f32[46,8,128]{2,1,0:T(8,128)S(1)}, f32[46,8,128]{2,1,0:T(8,128)S(1)}, u32[]{:S(2)}, u32[]{:S(2)}) %collective-permute-start.1) | collective-permute-done | bytes 188448 | tf_op jit(solution)/shard_map/ppermute | solution.py:448
  13.9 0.3 far_columns.1.token
  14.3 7.2 %collective-permute-start.2 = (f32[3,48,128]{2,1,0:T(8,128)S(1)}, f32[3,48,128]{2,1,0:T(8,128)S(1)}, u32[]{:S(2)}, u32[]{:S(2)}) collective-permute-start(f32[3,48,128]{2,1,0:T(8,128)S(1)} %far_columns.1.token), channel_id=1, source_target_pairs={{8,16},{24,32},{40,48},{56,64},{72,80},{88,96},{104,112},{120,128}... | collective-permute-start | bytes 221192 | tf_op jit(solution)/shard_map/ppermute | solution.py:454
  21.5 0.3 near_columns.1.token
  21.9 9.8 %collective-permute-start.3 = (f32[3,48,128]{2,1,0:T(8,128)S(1)}, f32[3,48,128]{2,1,0:T(8,128)S(1)}, u32[]{:S(2)}, u32[]{:S(2)}) collective-permute-start(f32[3,48,128]{2,1,0:T(8,128)S(1)} %near_columns.1.token), channel_id=1, source_target_pairs={{0,8},{16,24},{32,40},{48,56},{64,72},{80,88},{96,104},{112,120},{... | collective-permute-start | bytes 221192 | tf_op jit(solution)/shard_map/ppermute | solution.py:454
  31.7 0.0 copy-start.3
  31.7 1.4 %network.1 = (f32[8,1,128]{2,1,0:T(1,128)S(1)}, bf16[8,128,48]{2,1,0:T(8,128)(2,1)S(1)}, bf16[8,128,256]{2,1,0:T(8,128)(2,1)S(1)}, bf16[8,128,256]{2,1,0:T(8,128...) custom-call(f32[3,48,128]{2,1,0:T(8,128)S(1)} %near_columns.1.token,, ...), custom_call_target="tpu_custom_call" | custom-call | flops 2400000000 | bytes 8000 | tf_op jit(solution)/shard_map/network/pallas_call | solution.py:185
  33.1 7.0 %final.1 = (f32[6,32,128]{2,1,0:T(8,128)}, f32[32,128]{1,0:T(8,128)}, f32[32,128]{1,0:T(8,128)}, f32[416,128]{1,0:T(8,128)S(1)}) custom-call(f32[8,128]{1,0:T(8,128)S(1)} %mark.1.token, f32[46,8,128]{2,1,0:T(8,128)S(1)} %collective-permute-done.up_ref, f32[36,32,128]{2,1,0:T(8,128)S(1)} %bitcast.18, f32[4,32,128]{2,1,0:T(8,128)S(1)} %copy-done.2, ...), custom_call_target="tpu_custom_call" | custom-call | tf_op jit(solution)/shard_map/final/pallas_call | solution.py:399
  40.1 12.9 %all_to_all.15 = f32[32,13,1,128]{3,2,1,0:T(1,128)S(1)} all-to-all(f32[32,13,1,128]{3,2,1,0:T(1,128)S(1)} %bitcast.20), channel_id=1, replica_groups=mesh['z'=16,'xh'=2,'c'=2,'y'=4,'xl'=2] {'xh','c','y','xl'}, dimensions={0} | all-to-all | bytes 425984 | tf_op jit(solution)/shard_map/all_to_all | solution.py:460
  53.0 0.1 reduce_sum.18
  53.2 0.1 broadcast_in_dim.4
  53.2 20.4 %all_to_all.16 = f32[16,13,1,128]{3,2,1,0:T(1,128)S(1)} all-to-all(f32[16,13,1,128]{3,2,1,0:T(1,128)S(1)} %broadcast_in_dim.4), channel_id=1, replica_groups=mesh['z'=16,'xh'=2,'c'=2,'y'=4,'xl'=2] {'z'}, dimensions={0} | all-to-all | bytes 212992 | tf_op jit(solution)/shard_map/all_to_all | solution.py:462
  73.6 0.1 reduce_sum.19
  73.7 0.1 broadcast_in_dim.5
  73.8 14.3 %all_to_all.17 = f32[32,13,1,128]{3,2,1,0:T(1,128)S(1)} all-to-all(f32[32,13,1,128]{3,2,1,0:T(1,128)S(1)} %broadcast_in_dim.5), channel_id=1, replica_groups=mesh['z'=16,'xh'=2,'c'=2,'y'=4,'xl'=2] {'xh','c','y','xl'}, dimensions={0} | all-to-all | bytes 425984 | tf_op jit(solution)/shard_map/all_to_all | solution.py:464
  88.1 0.7 unpack.1
  (7 shorter events, 0.0 us)
Async XLA Ops:
  1.7 10.8 %collective-permute-start = (f32[46,8,128]{2,1,0:T(8,128)S(1)}, f32[46,8,128]{2,1,0:T(8,128)S(1)}, u32[]{:S(2)}, u32[]{:S(2)}) collective-permute-start(f32[46,8,128]{2,1,0:T(8,128)S(1)} %get-tuple-element.55.last_hbm), channel_id=1, source_target_pairs={{0,1},{1,2},{2,3},{3,4},{4,5},{5,6},{6,7},{8,9},{9,10},{10,11},{11... | collective-permute-start | bytes 565256 | tf_op jit(solution)/shard_map/ppermute | solution.py:448
  5.7 8.2 %collective-permute-start.1 = (f32[46,8,128]{2,1,0:T(8,128)S(1)}, f32[46,8,128]{2,1,0:T(8,128)S(1)}, u32[]{:S(2)}, u32[]{:S(2)}) collective-permute-start(f32[46,8,128]{2,1,0:T(8,128)S(1)} %get-tuple-element.56.first_hbm), channel_id=1, source_target_pairs={{1,0},{2,1},{3,2},{4,3},{5,4},{6,5},{7,6},{9,8},{10,9},{11,10},{12... | collective-permute-start | bytes 565256 | tf_op jit(solution)/shard_map/ppermute | solution.py:448
  7.0 6.9 %copy-start = (f32[6,6,32,128]{3,2,1,0:T(8,128)S(1)}, f32[6,6,32,128]{3,2,1,0:T(8,128)}, u32[]{:S(2)}) copy-start(f32[6,6,32,128]{3,2,1,0:T(8,128)} %param.15) | copy-start | bytes 1769476
  7.0 6.9 %copy-start.1 = (f32[6,32,128]{2,1,0:T(8,128)S(1)}, f32[6,32,128]{2,1,0:T(8,128)}, u32[]{:S(2)}) copy-start(f32[6,32,128]{2,1,0:T(8,128)} %mis_ref.5) | copy-start | bytes 294916
  7.0 6.9 %copy-start.2 = (f32[4,32,128]{2,1,0:T(8,128)S(1)}, f32[4,32,128]{2,1,0:T(8,128)}, u32[]{:S(2)}) copy-start(f32[4,32,128]{2,1,0:T(8,128)} %cpl_ref.5) | copy-start | bytes 196612
  14.3 18.8 %collective-permute-start.2 = (f32[3,48,128]{2,1,0:T(8,128)S(1)}, f32[3,48,128]{2,1,0:T(8,128)S(1)}, u32[]{:S(2)}, u32[]{:S(2)}) collective-permute-start(f32[3,48,128]{2,1,0:T(8,128)S(1)} %far_columns.1.token), channel_id=1, source_target_pairs={{8,16},{24,32},{40,48},{56,64},{72,80},{88,96},{104,112},{120,128}... | collective-permute-start | bytes 221192 | tf_op jit(solution)/shard_map/ppermute | solution.py:454
  21.9 11.2 %collective-permute-start.3 = (f32[3,48,128]{2,1,0:T(8,128)S(1)}, f32[3,48,128]{2,1,0:T(8,128)S(1)}, u32[]{:S(2)}, u32[]{:S(2)}) collective-permute-start(f32[3,48,128]{2,1,0:T(8,128)S(1)} %near_columns.1.token), channel_id=1, source_target_pairs={{0,8},{16,24},{32,40},{48,56},{64,72},{80,88},{96,104},{112,120},{... | collective-permute-start | bytes 221192 | tf_op jit(solution)/shard_map/ppermute | solution.py:454
  31.7 1.4 %copy-start.3 = (f32[6,32,128]{2,1,0:T(8,128)S(1)}, f32[6,32,128]{2,1,0:T(8,128)}, u32[]{:S(2)}) copy-start(f32[6,32,128]{2,1,0:T(8,128)} %prod_ref.1) | copy-start | bytes 294916
